TPU v7x, 128 devices: a whole 4x4x4 slice. The times are simulated.
128 devices in a mesh: dp: 8 (over x, core), fsdp: 4 (over y), tensor: 4 (over z).
Axes of the slice: x: 4, y: 4, z: 4, core: 2. Of those that a mesh axis runs over, the one named last changes fastest.
Arguments:
- tokens: bfloat16 [5120, 8192], P('dp', 'fsdp'), may hold values from -6 to 6
- cotangent: bfloat16 [5120, 28672], P('dp', 'tensor'), may hold values from -6 to 6
- left_factor: bfloat16 [8192, 512], P('fsdp'), may hold values from -0.0625 to 0.0625
- right_factor: bfloat16 [512, 4, 7168], P(None, 'tensor', 'fsdp'), may hold values from -0.25 to 0.25
- block_values: bfloat16 [512, 128, 128], P(('fsdp', 'tensor')), may hold values from -0.5 to 0.5
- block_rows: int32 [512], P(('fsdp', 'tensor')), may hold values from 0 to 15, as said below
- block_cols: int32 [512], P(('fsdp', 'tensor')), may hold values from 0 to 55
- block_counts: int32 [16], replicated, may hold values from 1 to 32, as said below
Outputs:
- mixed: bfloat16 [5120, 4, 7168], P('dp', 'tensor', 'fsdp')
- grad_left: bfloat16 [8192, 512], P('fsdp')
- grad_right: bfloat16 [512, 4, 7168], P(None, 'tensor', 'fsdp')
- grad_blocks: bfloat16 [512, 128, 128], P(('fsdp', 'tensor'))
Inputs may be any that keep to these rules, and one draw needn't show every extreme that they name: Within one owner's 32 slots, the pairs (block_rows, block_cols) are all different. `block_counts`: some owner has exactly 32 live slots.
All inputs are finite; a program needn't handle non-finite values.
Results may differ from a plain program's by a relative error of at most 0.005.
Values may be sent and summed in bfloat16 or wider, within the bound.
No kernel may reach another device: no remote copies, remote signals or barrier semaphores. Data moves between devices by JAX's collectives and lax.ppermute only.
A program may use at most 192 MiB of HBM per device.

v0:
```python
import jax
import jax.numpy as jnp
from jax import lax
from jax.sharding import PartitionSpec as P


def task_plan(offset, group, depth, live_count):
    peers = jnp.arange(group, dtype=jnp.int32)[:, None]
    turns = jnp.arange(depth, dtype=jnp.int32)[None, :]
    task = jnp.mod(peers - offset, group) + turns * group
    valid = task < live_count
    return (jnp.where(valid, task, 0), valid)


def task_panels(row_panels, col_panels, task, valid):
    group, depth = task.shape
    flat = task.reshape(-1)
    send_rows = jnp.moveaxis(jnp.take(row_panels, flat, axis=1), 1, 0)
    send_cols = jnp.moveaxis(jnp.take(col_panels, flat, axis=1), 1, 0)
    keep = valid.reshape(-1)[:, None, None]
    send_rows = jnp.where(keep, send_rows, jnp.zeros_like(send_rows))
    send_cols = jnp.where(keep, send_cols, jnp.zeros_like(send_cols))
    shape = (group, depth) + send_rows.shape[1:]
    return (send_rows.reshape(shape), send_cols.reshape(shape))


def panel_products(pair):
    return jnp.einsum("pstb,pstc->psbc", pair[0], pair[1], preferred_element_type=jnp.float32)


def collect_returns(returned, offset, group, live):
    maxb = live.shape[0]
    task = jnp.arange(maxb, dtype=jnp.int32)
    peer = jnp.mod(offset + task, group)
    turn = task // group
    grads = returned[peer, turn]
    return jnp.where(live[:, None, None], grads, jnp.zeros_like(grads))


def per_device(
    tokens, cotangent, left_factor, right_factor, block_values, block_rows, block_cols, block_counts
):
    tok_rows = tokens.shape[0]
    features = tokens.shape[1]
    n_fsdp = lax.axis_size("fsdp")
    n_tensor = lax.axis_size("tensor")
    n_data = lax.axis_size("dp")
    f_index = lax.axis_index("fsdp")
    t_index = lax.axis_index("tensor")
    d_index = lax.axis_index("dp")
    maxb = block_values.shape[0]
    side = block_values.shape[1]
    row_blocks = features // side
    col_blocks = cotangent.shape[1] // side
    q_blocks = col_blocks // n_fsdp
    slice_counts = block_counts.reshape(n_fsdp, n_tensor)[:, t_index]
    live_count = slice_counts[f_index]
    live = jnp.arange(maxb, dtype=jnp.int32) < live_count
    partial_rank = jnp.dot(tokens, left_factor, preferred_element_type=jnp.float32)
    rank = lax.psum(partial_rank, "fsdp").astype(jnp.bfloat16)
    right_local = right_factor.reshape(right_factor.shape[0], -1)
    quarter = right_local.shape[1]
    low = jnp.dot(rank, right_local, preferred_element_type=jnp.float32)
    my_cot = lax.dynamic_slice_in_dim(cotangent, f_index * quarter, quarter, 1)
    partial_back = jnp.einsum("tq,rq->tr", my_cot, right_local, preferred_element_type=jnp.float32)
    back = lax.psum(partial_back, ("fsdp", "tensor")).astype(jnp.bfloat16)
    grad_left = jnp.einsum("tf,tr->fr", tokens, back, preferred_element_type=jnp.float32)
    grad_right = jnp.einsum("tr,tq->rq", rank, my_cot, preferred_element_type=jnp.float32)
    rows3 = tokens.reshape(tok_rows, row_blocks, side)
    cols3 = cotangent.reshape(tok_rows, col_blocks, side)
    row_panels = jnp.take(rows3, block_rows, axis=1)
    col_panels = jnp.take(cols3, block_cols, axis=1)
    all_rows = lax.all_gather(tokens, "fsdp", axis=1, tiled=True)
    all_rows3 = all_rows.reshape(tok_rows, row_blocks * n_fsdp, side)
    start_acc = jnp.zeros((q_blocks, tok_rows, side), jnp.float32)
    values = lax.all_gather(block_values, "fsdp", axis=0, tiled=True)
    rws = lax.all_gather(block_rows, "fsdp", axis=0, tiled=True)
    cls = lax.all_gather(block_cols, "fsdp", axis=0, tiled=True)
    count = values.shape[0]
    gidx = jnp.arange(count, dtype=jnp.int32)
    owner_f = gidx // maxb
    owned = block_counts[owner_f * n_tensor + t_index]
    usable = (gidx % maxb < owned) & (cls // q_blocks == f_index)
    panels = jnp.take(all_rows3, owner_f * row_blocks + rws, axis=1)
    prods = jnp.einsum("tmb,mbc->mtc", panels, values, preferred_element_type=jnp.float32)
    prods = jnp.where(usable[:, None, None], prods, jnp.zeros_like(prods))
    target = jnp.where(usable, cls - f_index * q_blocks, 0)
    share = start_acc.at[target].add(prods)
    sparse_out = jnp.transpose(share, (1, 0, 2)).reshape(tok_rows, quarter)
    mixed = (low + sparse_out).astype(jnp.bfloat16).reshape(tok_rows, 1, quarter)
    group = n_data * n_fsdp
    depth = -(-maxb // group)
    before = jnp.cumsum(slice_counts) - slice_counts
    offset = d_index * jnp.sum(slice_counts) + before[f_index]
    task, valid = task_plan(offset, group, depth, live_count)
    send_rows, send_cols = task_panels(row_panels, col_panels, task, valid)
    returned = lax.all_to_all(
        panel_products(
            (
                lax.all_to_all(send_rows, ("dp", "fsdp"), split_axis=0, concat_axis=0, tiled=True),
                lax.all_to_all(send_cols, ("dp", "fsdp"), split_axis=0, concat_axis=0, tiled=True),
            )
        ),
        ("dp", "fsdp"),
        split_axis=0,
        concat_axis=0,
        tiled=True,
    )
    grad_blocks = collect_returns(returned, offset, group, live)
    summed_left, summed_right, summed_blocks = lax.psum((grad_left, grad_right, grad_blocks), "dp")
    out_left = summed_left.astype(jnp.bfloat16)
    out_right = summed_right.astype(jnp.bfloat16).reshape(right_factor.shape)
    out_blocks = summed_blocks.astype(jnp.bfloat16)
    return (mixed, out_left, out_right, out_blocks)


def solution(mesh):
    return jax.shard_map(
        per_device,
        mesh=mesh,
        in_specs=(
            P("dp", "fsdp"),
            P("dp", "tensor"),
            P("fsdp", None),
            P(None, "tensor", "fsdp"),
            P(("fsdp", "tensor"), None, None),
            P(("fsdp", "tensor")),
            P(("fsdp", "tensor")),
            P(),
        ),
        out_specs=(
            P("dp", "tensor", "fsdp"),
            P("fsdp", None),
            P(None, "tensor", "fsdp"),
            P(("fsdp", "tensor"), None, None),
        ),
        check_vma=False,
    )
```

profile of v0, /device:TPU:1, one launch (start us, length us, event | category | flops | bytes accessed | tf_op | source)
XLA Modules:
  0.0 716.9 jit_solution(8835562057175631562)
XLA Ops:
  17.6 13.2 %copy.36 = bf16[640,7168]{0,1:T(8,128)(2,1)} copy(bf16[640,7168]{1,0:T(8,128)(2,1)} %param.11) | data formatting | bytes 18350080 | tf_op args[1]
  30.7 12.9 %copy.37 = bf16[640,56,128]{2,0,1:T(8,128)(2,1)} copy(bf16[640,56,128]{0,2,1:T(8,128)(2,1)} %bitcast.156) | data formatting | bytes 18350080 | tf_op jit(solution)/shard_map/reshape | solution.py:70
  43.6 5.3 gather_fusion.1
  51.6 5.5 select_bitcast_fusion.1
  57.0 6.0 gather_fusion.4
  63.0 7.1 gather_fusion.2
  75.4 6.2 gather_fusion.5
  81.6 9.4 %fusion.11 = (bf16[32,1,640,128]{3,2,1,0:T(8,128)(2,1)}, bf16[32,1,640,128]{3,2,1,0:T(8,128)(2,1)}) fusion(bf16[32,640,128]{2,1,0:T(8,128)(2,1)} %gather_fusion.4, pred[32]{0:T(512)(128)(4,1)S(1)} %get-tuple-element.26, pred[32]{0:T(512)(128)(4,1)S(1)} %get-tuple-element.54, bf16[32,640,128]{2,1,0:T(8,128)(2,1)} %gather_fusion.5), kind=kLoop, calls=%fused_computation.19 | loop fusion | flops 10485760 | bytes 20971584 | tf_op jit(solution)/shard_map/reshape | solution.py:24
  91.0 81.0 %all_to_all.15 = bf16[32,1,640,128]{3,2,1,0:T(8,128)(2,1)} all-to-all(bf16[32,1,640,128]{3,2,1,0:T(8,128)(2,1)} %get-tuple-element.35), channel_id=1, replica_groups=mesh['dp'=8,'fsdp'=4,'tensor'=4] {'dp','fsdp'}, dimensions={0} | all-to-all | bytes 10485760 | tf_op jit(solution)/shard_map/all_to_all | solution.py:101
  172.0 6.9 all-to-all-start
  188.7 104.8 %all-reduce.7 = bf16[640,512]{1,0:T(8,128)(2,1)S(1)} all-reduce(f32[640,512]{1,0:T(8,128)S(1)} %copy-done.2), channel_id=1, replica_groups=mesh['dp'=8,'fsdp'=4,'tensor'=4] {'fsdp'}, use_global_device_ids=true, to_apply=%region_0.0 | all-reduce | flops 327680 | bytes 1966080 | tf_op jit(solution)/shard_map/psum | solution.py:60
  293.5 7.0 fusion.19
  300.6 8.3 %all-to-all-start.2 = ((f32[32,1,128,128]{3,2,1,0:T(8,128)}), f32[32,1,128,128]{3,2,1,0:T(8,128)S(1)}, u32[]{:S(2)}, u32[]{:S(2)}) async-start(f32[32,1,128,128]{3,2,1,0:T(8,128)} %fusion.19), calls=%async_computation.2 | async-start | bytes 4194304 | tf_op jit(solution)/shard_map/all_to_all | solution.py:97
  308.8 90.5 %all-reduce.8 = bf16[640,512]{1,0:T(8,128)(2,1)S(1)} all-reduce(f32[640,512]{1,0:T(8,128)} %fusion.15), channel_id=1, replica_groups=mesh['dp'=8,'fsdp'=4,'tensor'=4] {'fsdp','tensor'}, use_global_device_ids=true, to_apply=%region_2.3 | all-reduce | flops 327680 | bytes 1966080 | tf_op jit(solution)/shard_map/psum | solution.py:66
  401.0 5.6 convolution_bitcast_fusion
  417.7 10.2 %compare_select_fusion.6 = (s32[128]{0:T(128)S(1)}, pred[128]{0:T(512)(128)(4,1)S(1)}) fusion(s32[128]{0:T(128)S(1)} %get-tuple-element.21, s32[]{:T(128)S(6)} %mul.27, s32[]{:T(128)S(6)} %axis_index.35, s32[]{:T(128)} %bitcast.25, s32[]{:T(128)} %bitcast.24, s32[]{:T(128)} %bitcast.23, s32[]{:T(128)} %bitcast.22, s32[]{:T(128)} %bitcast.21, s32[]{:T(128)} %bitcast.20, ...), kind=kLoop, calls=%fused_computation.47 | loop fusion | flops 8320 | bytes 1228 | tf_op jit(solution)/shard_map/select_n | solution.py:88
  431.7 120.8 %all-reduce.9 = (bf16[2048,512]{0,1:T(8,128)(2,1)}, bf16[512,1792]{1,0:T(8,128)(2,1)}, bf16[32,128,128]{2,1,0:T(8,128)(2,1)}) all-reduce(f32[2048,512]{0,1:T(8,128)} %convolution_bitcast_fusion, f32[512,1792]{1,0:T(8,128)} %fusion.13, f32[32,128,128]{2,1,0:T(8,128)S(1)} %broadcast_select_fusion.1), channel_id=1, replica_groups=mesh['dp'=8,'fsdp'=4,'tensor'=4] {'dp'}, use_global_device_ids=true, to_apply=%region_3.4 | all-reduce | flops 2490368 | bytes 14942208 | tf_op jit(solution)/shard_map/psum | solution.py:110
  556.4 14.5 %copy.29 = bf16[640,64,128]{2,0,1:T(8,128)(2,1)} copy(bf16[640,64,128]{0,2,1:T(8,128)(2,1)} %bitcast.159) | data formatting | bytes 20971520 | tf_op jit(solution)/shard_map/reshape | solution.py:74
  570.9 13.7 %gather_fusion = bf16[128,640,128]{2,1,0:T(8,128)(2,1)} fusion(bf16[640,64,128]{2,0,1:T(8,128)(2,1)} %copy.29, s32[1024]{0:T(1024)S(1)} %pad_clamp_fusion.3), kind=kCustom, calls=%fused_computation.2 | custom fusion | bytes 41943552 | tf_op jit(solution)/shard_map/jit(_take)/gather | solution.py:84
  584.7 25.4 %broadcast_select_fusion = f32[128,640,128]{2,1,0:T(8,128)} fusion(pred[128]{0:T(512)(128)(4,1)S(1)} %get-tuple-element.33, bf16[128,128,128]{2,1,0:T(8,128)(2,1)} %all-gather.5.cloned.1.call-done, bf16[128,640,128]{2,1,0:T(8,128)(2,1)} %gather_fusion, pred[128]{0:T(512)(128)(4,1)S(1)} %get-tuple-element.30), kind=kOutput, calls=%fused_computation.10 | convolution fusion | flops 2705326080 | bytes 67109120 | tf_op jit(solution)/shard_map/tmb,mbc->mtc/dot_general | solution.py:85
  612.6 80.4 %scatter_fusion = f32[14,640,128]{2,1,0:T(8,128)} fusion(f32[14,640,128]{2,1,0:T(8,128)} %broadcast_in_dim.92, s32[128]{0:T(128)S(1)} %get-tuple-element.32, f32[128,640,128]{2,1,0:T(8,128)} %broadcast_select_fusion), kind=kCustom, calls=%fused_computation.6 | custom fusion | flops 10485760 | bytes 125829632 | tf_op jit(solution)/shard_map/scatter-add | solution.py:88
  692.9 5.7 copy.30
  698.6 5.9 copy.31
  704.5 5.6 fusion.12
  (55 shorter events, 49.1 us)
Async XLA Ops:
  7.2 172.5 %copy-start = (bf16[2048,512]{1,0:T(8,128)(2,1)S(1)}, bf16[2048,512]{1,0:T(8,128)(2,1)}, u32[]{:S(2)}) copy-start(bf16[2048,512]{1,0:T(8,128)(2,1)} %param.12) | copy-start | bytes 6291460
  7.2 549.2 %all-gather.3.cloned.1.call-start = ((), (), s32[]{:S(2)}) async-start(), calls=%async_computation.3 | async-start | bytes 13107200 | tf_op jit(solution)/shard_map/all_gather | solution.py:73
  11.8 4.4 copy-start.3
  30.7 12.9 %copy-start.4 = (s32[32]{0:T(128)S(1)}, s32[32]{0:T(128)}, u32[]{:S(2)}) copy-start(s32[32]{0:T(128)} %param.16) | copy-start | bytes 388
  30.7 12.9 %copy-start.5 = (s32[32]{0:T(128)S(1)}, s32[32]{0:T(128)}, u32[]{:S(2)}) copy-start(s32[32]{0:T(128)} %param.15) | copy-start | bytes 388
  172.0 121.5 %all-to-all-start = ((bf16[32,1,640,128]{3,2,1,0:T(8,128)(2,1)}), bf16[32,1,640,128]{3,2,1,0:T(8,128)(2,1)}, u32[]{:S(2)}, u32[]{:S(2)}) async-start(bf16[32,1,640,128]{3,2,1,0:T(8,128)(2,1)} %get-tuple-element.34), calls=%async_computation | async-start | bytes 10485760 | tf_op jit(solution)/shard_map/all_to_all | solution.py:100
  178.9 405.8 %all-gather.5.cloned.1.call-start = ((), (), s32[]{:S(2)}) async-start(), calls=%async_computation.4 | async-start | bytes 5242880 | tf_op jit(solution)/shard_map/all_gather | solution.py:76
  184.0 4.7 copy-start.2
  300.6 98.8 %copy-start.6 = (u32[128]{0:T(128)S(1)}, u32[128]{0:T(128)}, u32[]{:S(2)}) copy-start(u32[128]{0:T(128)} %constant.202) | copy-start | bytes 1540
  300.6 127.3 %all-to-all-start.2 = ((f32[32,1,128,128]{3,2,1,0:T(8,128)}), f32[32,1,128,128]{3,2,1,0:T(8,128)S(1)}, u32[]{:S(2)}, u32[]{:S(2)}) async-start(f32[32,1,128,128]{3,2,1,0:T(8,128)} %fusion.19), calls=%async_computation.2 | async-start | bytes 4194304 | tf_op jit(solution)/shard_map/all_to_all | solution.py:97
  698.6 11.5 %copy-start.1 = (bf16[2048,512]{1,0:T(8,128)(2,1)S(1)}, bf16[2048,512]{1,0:T(8,128)(2,1)}, u32[]{:S(2)}) copy-start(bf16[2048,512]{1,0:T(8,128)(2,1)} %param.12) | copy-start | bytes 6291460
Sparse Core Ops, SparseCore 0:
  11.9 159.4 all-gather.2
  181.4 112.3 all-gather.4
where the time goes:
time: 720 us; the launch traced here: 717 us
  blocking collectives  402 us (56%)
  other arithmetic  115 us (16%)
  local copies, waits for them, and re-layouts  111 us (15%)
  matrix products  57.7 us (8%)
  between operations  16.2 us (2%)
  starting transfers between devices  15.2 us (2%)
    psum x1, blocking collectives, per_device(): lax.psum((grad_left, grad_right, grad_blocks), 'dp')  121 us
    psum x1, blocking collectives, per_device(): rank = lax.psum(partial_rank, 'fsdp').astype(jnp.bfloat16)  105 us
    psum x1, blocking collectives, per_device(): back = lax.psum(partial_back, ('fsdp', 'tensor')).astype(jnp.bfloat16)  90.5 us
    all_to_all x1, blocking collectives, per_device(): lax.all_to_all(send_cols, ('dp', 'fsdp'), split_axis=0, concat_axis=0, ti...  81 us
    scatter-add x1, other arithmetic, per_device(): share = start_acc.at[target].add(prods)  80.4 us
    dot_general x1, matrix products, per_device(): jnp.einsum('tmb,mbc->mtc', panels, values, preferred_element_type=jnp.flo...  25.4 us
    unnamed x20, local copies, waits for them, and re-layouts  22.7 us
    reshape x1, local copies, waits for them, and re-layouts, per_device(): all_rows3 = all_rows.reshape(tok_rows, row_blocks * n_fsdp, side)  14.5 us
  transfers between devices with their start and end apart: 4, of which 0 were waited for; matrix products, arithmetic and copies ran while one was open for 21% of the time, Pallas kernels for 0%

commit v1 on v0

v1 whole, which is shorter than its diff:
```python
import jax
import jax.numpy as jnp
from jax import lax
from jax.experimental import pallas as pl
from jax.experimental.pallas import tpu as pltpu
from jax.sharding import PartitionSpec as P

F32 = jnp.float32
BF16 = jnp.bfloat16
SIDE = 128


def lanes(block):
    return pl.ds(pl.multiple_of(block * SIDE, SIDE), SIDE)


def block_grads_kernel(live_ref, rows_ref, cols_ref, tok_ref, cot_ref, out_ref):
    out_ref[...] = jnp.zeros_like(out_ref)

    def body(s, carry):
        panel = tok_ref[:, lanes(rows_ref[s])]
        cpanel = cot_ref[:, lanes(cols_ref[s])]
        grad = lax.dot_general(
            panel, cpanel, (((0,), (0,)), ((), ())), preferred_element_type=F32
        )
        out_ref[pl.ds(s, 1)] = grad.astype(BF16)[None]
        return carry

    lax.fori_loop(0, live_ref[0], body, 0)


def block_grads(live, rows, cols, tokens, cotangent, vmem_mib=40):
    maxb = rows.shape[0]
    smem = pl.BlockSpec(memory_space=pltpu.SMEM)
    vmem = pl.BlockSpec(memory_space=pltpu.VMEM)
    tok_rows = tokens.shape[0]
    return pl.pallas_call(
        block_grads_kernel,
        out_shape=jax.ShapeDtypeStruct((maxb, SIDE, SIDE), BF16),
        in_specs=[smem, smem, smem, vmem, vmem],
        out_specs=vmem,
        cost_estimate=pl.CostEstimate(
            flops=2 * maxb * tok_rows * SIDE * SIDE,
            bytes_accessed=2 * tokens.size + 2 * cotangent.size + 2 * maxb * SIDE * SIDE,
            transcendentals=0,
        ),
        compiler_params=pltpu.CompilerParams(vmem_limit_bytes=vmem_mib << 20),
    )(live, rows, cols, tokens, cotangent)


DEPTH = 6


def mixed_kernel(
    n_owners, maxb, q_blocks, chunk,
    info_ref, rows_ref, cols_ref, rank_ref, right_ref, tok_ref, val_ref, out_ref,
    acc, list_ref, panels, vals, sems,
):
    me = info_ref[n_owners]

    def scan(i, n):
        owner = i // maxb
        col = cols_ref[i]
        use = (i - owner * maxb < info_ref[owner]) & (col // q_blocks == me)
        list_ref[n] = i
        return n + use.astype(jnp.int32)

    total = lax.fori_loop(0, n_owners * maxb, scan, 0)
    per = chunk // SIDE
    owner_chunks = tok_ref.shape[0] // n_owners

    def copies(k):
        i = list_ref[k]
        slot = lax.rem(k, DEPTH)
        row = rows_ref[i]
        src = tok_ref.at[(i // maxb) * owner_chunks + row // per, :, lanes(lax.rem(row, per))]
        return (
            pltpu.make_async_copy(src, panels.at[slot], sems.at[slot, 0]),
            pltpu.make_async_copy(val_ref.at[i], vals.at[slot], sems.at[slot, 1]),
        )

    def start(k):
        @pl.when(k < total)
        def _():
            for c in copies(k):
                c.start()

    for k in range(DEPTH - 1):
        start(jnp.int32(k))
    acc[...] = jnp.dot(rank_ref[...], right_ref[...], preferred_element_type=F32)

    def body(k, carry):
        start(k + DEPTH - 1)
        for c in copies(k):
            c.wait()
        slot = lax.rem(k, DEPTH)
        col = cols_ref[list_ref[k]] - me * q_blocks
        acc[:, lanes(col)] += jnp.dot(panels[slot], vals[slot], preferred_element_type=F32)
        return carry

    lax.fori_loop(0, total, body, 0)
    out_ref[...] = acc[...].astype(BF16)


def mixed_product(info, rows, cols, rank, right, tok, vals, maxb, q_blocks):
    n_owners = rows.shape[0] // maxb
    tok_rows, quarter = rank.shape[0], right.shape[1]
    chunk = tok.shape[2]
    smem = pl.BlockSpec(memory_space=pltpu.SMEM)
    vmem = pl.BlockSpec(memory_space=pltpu.VMEM)
    hbm = pl.BlockSpec(memory_space=pl.ANY)

    def kernel(*refs):
        mixed_kernel(n_owners, maxb, q_blocks, chunk, *refs)

    return pl.pallas_call(
        kernel,
        out_shape=jax.ShapeDtypeStruct((tok_rows, quarter), BF16),
        in_specs=[smem, smem, smem, vmem, vmem, hbm, hbm],
        out_specs=vmem,
        scratch_shapes=[
            pltpu.VMEM((tok_rows, quarter), F32),
            pltpu.SMEM((n_owners * maxb + 1,), jnp.int32),
            pltpu.VMEM((DEPTH, tok_rows, SIDE), BF16),
            pltpu.VMEM((DEPTH, SIDE, SIDE), BF16),
            pltpu.SemaphoreType.DMA((DEPTH, 2)),
        ],
        cost_estimate=pl.CostEstimate(
            flops=2 * tok_rows * quarter * rank.shape[1],
            bytes_accessed=2 * tok.size,
            transcendentals=0,
        ),
        compiler_params=pltpu.CompilerParams(vmem_limit_bytes=40 << 20),
    )(info, rows, cols, rank, right, tok, vals)


def shift(x, axis, n, k):
    return lax.ppermute(x, axis, [(i, (i + k) % n) for i in range(n)])


def chip_shift(x, n_data, k):
    chips = n_data // 2
    perm = [(2 * a + c, 2 * ((a + k) % chips) + c) for a in range(chips) for c in range(2)]
    return lax.ppermute(x, "dp", perm)


def scatter_dp(x, n_data, d_index):
    chips = n_data // 2
    chip, core = d_index // 2, d_index % 2
    parts = x.reshape((chips, 2, x.shape[0] // n_data) + x.shape[1:])
    theirs = lax.dynamic_index_in_dim(parts, 1 - core, 1, keepdims=False).astype(BF16)
    mine = lax.dynamic_index_in_dim(parts, core, 1, keepdims=False).astype(F32)
    got = lax.ppermute(theirs, "dp", [(i, i ^ 1) for i in range(n_data)])
    both = mine + got.astype(F32)
    total = lax.dynamic_index_in_dim(both, chip, 0, keepdims=False)
    low = both.astype(BF16)
    for k in range(1, chips):
        piece = lax.dynamic_index_in_dim(low, (chip + k) % chips, 0, keepdims=False)
        total = total + chip_shift(piece, n_data, k).astype(F32)
    return total.astype(BF16)


def per_device(
    tokens, cotangent, left_factor, right_factor, block_values, block_rows, block_cols, block_counts
):
    n_fsdp = lax.axis_size("fsdp")
    n_tensor = lax.axis_size("tensor")
    n_data = lax.axis_size("dp")
    f_index = lax.axis_index("fsdp")
    t_index = lax.axis_index("tensor")
    d_index = lax.axis_index("dp")
    maxb = block_values.shape[0]
    tok_rows, features = tokens.shape
    right = right_factor.reshape(right_factor.shape[0], -1)
    rank_size, quarter = right.shape
    q_blocks = quarter // SIDE
    r_part = rank_size // n_tensor
    counts = block_counts.reshape(n_fsdp, n_tensor)[:, t_index]
    live = counts[f_index]

    chunk = features // n_tensor
    my_tok = lax.dynamic_slice_in_dim(tokens, t_index * chunk, chunk, 1)
    all_tok = lax.all_gather(my_tok, ("fsdp", "tensor"), axis=0)
    per = maxb // n_data
    my_vals = lax.dynamic_slice_in_dim(block_values, d_index * per, per, 0)
    all_vals = lax.all_gather(my_vals, ("fsdp", "dp"), axis=0, tiled=True)
    places = lax.all_gather(jnp.stack([block_rows, block_cols]), "fsdp", axis=0)
    all_rows = places[:, 0].reshape(-1)
    all_cols = places[:, 1].reshape(-1)

    left_part = lax.dynamic_slice_in_dim(left_factor, t_index * r_part, r_part, 1)
    rank_part = jnp.dot(tokens, left_part, preferred_element_type=F32)
    rank_low = rank_part.astype(BF16)
    for k in range(1, n_fsdp):
        rank_part = rank_part + shift(rank_low, "fsdp", n_fsdp, k).astype(F32)
    rank_t = rank_part.astype(BF16)
    rank = lax.all_gather(rank_t, "tensor", axis=1, tiled=True)

    my_cot = lax.dynamic_slice_in_dim(cotangent, f_index * quarter, quarter, 1)
    back_all = jnp.einsum("tq,rq->tr", my_cot, right, preferred_element_type=F32)
    back_sum = lax.dynamic_slice_in_dim(back_all, t_index * r_part, r_part, 1)
    back_low = back_all.astype(BF16)
    for k in range(1, n_tensor):
        piece = lax.dynamic_slice_in_dim(back_low, ((t_index + k) % n_tensor) * r_part, r_part, 1)
        back_sum = back_sum + shift(piece, "tensor", n_tensor, k).astype(F32)
    back_low = back_sum.astype(BF16)
    for k in range(1, n_fsdp):
        back_sum = back_sum + shift(back_low, "fsdp", n_fsdp, k).astype(F32)
    back = back_sum.astype(BF16)

    grads = block_grads(live.reshape(1), block_rows, block_cols, tokens, cotangent)
    block_part = scatter_dp(grads, n_data, d_index)
    out_blocks = lax.all_gather(block_part, "dp", axis=0, tiled=True)

    grad_right = jnp.einsum("tr,tq->rq", rank, my_cot, preferred_element_type=F32)
    right_part = scatter_dp(grad_right, n_data, d_index)
    out_right = lax.all_gather(right_part, "dp", axis=0, tiled=True).reshape(right_factor.shape)

    grad_left = jnp.einsum("tf,tr->fr", tokens, back, preferred_element_type=F32)
    left_part = scatter_dp(grad_left, n_data, d_index)
    left_all = lax.all_gather(left_part, ("dp", "tensor"), axis=0)
    left_all = left_all.reshape(n_data, n_tensor, features // n_data, r_part)
    out_left = jnp.transpose(left_all, (0, 2, 1, 3)).reshape(features, rank_size)

    info = jnp.concatenate([counts, f_index.reshape(1)]).astype(jnp.int32)
    mixed = mixed_product(
        info, all_rows, all_cols, rank, right, all_tok, all_vals, maxb, q_blocks
    ).reshape(tok_rows, 1, quarter)
    return (mixed, out_left, out_right, out_blocks)


def solution(mesh):
    return jax.shard_map(
        per_device,
        mesh=mesh,
        in_specs=(
            P("dp", "fsdp"),
            P("dp", "tensor"),
            P("fsdp", None),
            P(None, "tensor", "fsdp"),
            P(("fsdp", "tensor"), None, None),
            P(("fsdp", "tensor")),
            P(("fsdp", "tensor")),
            P(),
        ),
        out_specs=(
            P("dp", "tensor", "fsdp"),
            P("fsdp", None),
            P(None, "tensor", "fsdp"),
            P(("fsdp", "tensor"), None, None),
        ),
        check_vma=False,
    )
```

time: 720 us -> 328 us (0.46)
  blocking collectives: 402 us -> 23.3 us
  waiting for transfers between devices: 0.72 us -> 204 us
  other arithmetic: 115 us -> 4.69 us
  local copies, waits for them, and re-layouts: 111 us -> 31.8 us
  matrix products: 57.7 us -> 10.8 us
  Pallas kernels: 0 us -> 14.9 us
    psum x3 -> x0, blocking collectives: 316 us -> none  [the longest x1 121 us: per_device(): lax.psum((grad_left, grad_right, grad_blocks), 'dp')]
    all_gather x2 -> x5, waiting for transfers between devices: 0.01 us -> 156 us  [the longest x1 82.2 us: per_device(): all_tok = lax.all_gather(my_tok, ('fsdp', 'tensor'), axis=0)]
    all_to_all x1 -> x0, blocking collectives: 81 us -> none  [per_device(): lax.all_to_all(send_cols, ('dp', 'fsdp'), split_axis=0, concat_axis=0, ti...]
    scatter-add x1 -> x0, other arithmetic: 80.4 us -> none  [per_device(): share = start_acc.at[target].add(prods)]
    ppermute x0 -> x21, waiting for transfers between devices: none -> 48.4 us  [the longest x9 29.7 us: chip_shift(): return lax.ppermute(x, 'dp', perm)]
    dot_general x7 -> x4, matrix products: 57.7 us -> 10.8 us  [the longest x1 3.27 us: per_device(): jnp.einsum('tr,tq->rq', rank, my_cot, preferred_element_type=F32)]
    gather x7 -> x0, local copies, waits for them, and re-layouts: 41 us -> none  [the longest x1 13.7 us: per_device(): panels = jnp.take(all_rows3, owner_f * row_blocks + rws, axis=1)]
    reshape x5 -> x2, local copies, waits for them, and re-layouts: 37.8 us -> 3.16 us  [the longest x1 3.08 us: scatter_dp(): parts = x.reshape((chips, 2, x.shape[0] // n_data) + x.shape[1:])]
  transfers between devices with their start and end apart: 4 -> 26, of which waited for: 0 -> 17; matrix products, arithmetic and copies ran while one was open for 21% -> 10% of each run, Pallas kernels for 0% -> 2%
where the time goes in v1:
time: 328 us; the launch traced here: 326 us
  waiting for transfers between devices  204 us (62%)
  local copies, waits for them, and re-layouts  31.8 us (10%)
  blocking collectives  23.3 us (7%)
  starting transfers between devices  22.1 us (7%)
  Pallas kernels  14.9 us (5%)
  between operations  14.1 us (4%)
  matrix products  10.8 us (3%)
  other arithmetic  4.69 us (1%)
    all_gather x1, waiting for transfers between devices, per_device(): all_tok = lax.all_gather(my_tok, ('fsdp', 'tensor'), axis=0)  82.2 us
    all_gather x1, waiting for transfers between devices, per_device(): all_vals = lax.all_gather(my_vals, ('fsdp', 'dp'), axis=0, tiled=True)  43 us
    all_gather x1, waiting for transfers between devices, per_device(): left_all = lax.all_gather(left_part, ('dp', 'tensor'), axis=0)  30.8 us
    ppermute x9, waiting for transfers between devices, chip_shift(): return lax.ppermute(x, 'dp', perm)  29.7 us
    ppermute x9, waiting for transfers between devices, shift(): return lax.ppermute(x, axis, [(i, (i + k) % n) for i in range(n)])  18.6 us
    all_gather x1, blocking collectives, per_device(): rank = lax.all_gather(rank_t, 'tensor', axis=1, tiled=True)  17.7 us
    unnamed x31, local copies, waits for them, and re-layouts  17.3 us
    ppermute x9, starting transfers between devices, shift(): return lax.ppermute(x, axis, [(i, (i + k) % n) for i in range(n)])  12 us
  transfers between devices with their start and end apart: 26, of which 17 were waited for; matrix products, arithmetic and copies ran while one was open for 10% of the time, Pallas kernels for 2%

profile of v1, /device:TPU:1, one launch (start us, length us, event | category | flops | bytes accessed | tf_op | source)
XLA Modules:
  0.0 326.2 jit_solution(1342570443665974477)
XLA Ops:
  8.8 2.6 fusion.24
  11.4 3.6 %collective-permute-start.2 = (bf16[640,128]{1,0:T(8,128)(2,1)S(1)}, bf16[640,128]{1,0:T(8,128)(2,1)S(1)}, u32[]{:S(2)}, u32[]{:S(2)}) collective-permute-start(bf16[640,128]{1,0:T(8,128)(2,1)S(1)} %get-tuple-element.32), channel_id=1, source_target_pairs={{0,12},{4,0},{8,4},{12,8},{1,13},{5,1},{9,5},{13,9},{2,14},{6,2},{... | collective-permute-start | bytes 491528 | tf_op jit(solution)/shard_map/ppermute | solution.py:138
  18.5 3.6 %copy-done.4 = bf16[640,7168]{1,0:T(8,128)(2,1)S(1)} copy-done((bf16[640,7168]{1,0:T(8,128)(2,1)S(1)}, bf16[640,7168]{1,0:T(8,128)(2,1)}, u32[]{:S(2)}) %copy-start.4) | copy-done | bytes 9175064
  22.1 6.1 %shard_map.112 = bf16[32,128,128]{2,1,0:T(8,128)(2,1)S(1)} custom-call(s32[1]{0:T(128)} %bitcast.25.live_ref, s32[32]{0:T(128)S(1)} %copy-done.8, s32[32]{0:T(128)S(1)} %copy-done.7, bf16[640,2048]{1,0:T(8,128)(2,1)S(1)} %copy-done.2, bf16[640,7168]{1,0:T(8,128)(2,1)S(1)} %copy-done.4), custom_call_target="tpu_custom_call" | custom-call | flops 671088640 | bytes 12845056 | tf_op jit(solution)/shard_map/pallas_call | solution.py:37
  30.0 17.7 %all_gather.32.refs_3_ = bf16[640,512]{1,0:T(8,128)(2,1)S(1)} all-gather(bf16[640,128]{1,0:T(8,128)(2,1)S(1)} %add_convert_fusion.1), channel_id=1, replica_groups=mesh['dp'=8,'fsdp'=4,'tensor'=4] {'tensor'}, dimensions={1}, use_global_device_ids=true | all-gather | bytes 819200 | tf_op jit(solution)/shard_map/all_gather | solution.py:197
  47.7 3.3 %fusion = f32[512,1792]{1,0:T(8,128)S(1)} fusion(bf16[640,512]{1,0:T(8,128)(2,1)S(1)} %all_gather.32.refs_3_, bf16[640,7168]{1,0:T(8,128)(2,1)} %cot_ref.1, s32[]{:T(128)S(6)} %select_n.128), kind=kOutput, calls=%fused_computation.2 | convolution fusion | flops 1174405120 | bytes 6619140 | tf_op jit(solution)/shard_map/tr,tq->rq/dot_general | solution.py:215
  53.4 2.5 collective-permute-start.20
  58.8 2.8 collective-permute-done.19
  61.5 4.0 %collective-permute-done.18 = bf16[4,128,128]{2,1,0:T(8,128)(2,1)S(1)} collective-permute-done((bf16[4,128,128]{2,1,0:T(8,128)(2,1)S(1)}, bf16[4,128,128]{2,1,0:T(8,128)(2,1)S(1)}, u32[]{:S(2)}, u32[]{:S(2)}) %collective-permute-start.18) | collective-permute-done | bytes 131104 | tf_op jit(solution)/shard_map/ppermute | solution.py:144
  70.0 5.1 %collective-permute-done.16 = bf16[64,1792]{1,0:T(8,128)(2,1)S(1)} collective-permute-done((bf16[64,1792]{1,0:T(8,128)(2,1)S(1)}, bf16[64,1792]{1,0:T(8,128)(2,1)S(1)}, u32[]{:S(2)}, u32[]{:S(2)}) %collective-permute-start.16) | collective-permute-done | bytes 229408 | tf_op jit(solution)/shard_map/ppermute | solution.py:144
  76.2 9.6 %collective-permute-done.14 = bf16[64,1792]{1,0:T(8,128)(2,1)S(1)} collective-permute-done((bf16[64,1792]{1,0:T(8,128)(2,1)S(1)}, bf16[64,1792]{1,0:T(8,128)(2,1)S(1)}, u32[]{:S(2)}, u32[]{:S(2)}) %collective-permute-start.14) | collective-permute-done | bytes 229408 | tf_op jit(solution)/shard_map/ppermute | solution.py:144
  86.7 3.2 fusion.25
  92.6 2.7 collective-permute-done.5
  96.8 4.0 %collective-permute-done.3 = bf16[640,128]{1,0:T(8,128)(2,1)S(1)} collective-permute-done((bf16[640,128]{1,0:T(8,128)(2,1)S(1)}, bf16[640,128]{1,0:T(8,128)(2,1)S(1)}, u32[]{:S(2)}, u32[]{:S(2)}) %collective-permute-start.3) | collective-permute-done | bytes 163872 | tf_op jit(solution)/shard_map/ppermute | solution.py:138
  100.8 4.1 %collective-permute-start.8 = (bf16[640,128]{1,0:T(8,128)(2,1)S(1)}, bf16[640,128]{1,0:T(8,128)(2,1)S(1)}, u32[]{:S(2)}, u32[]{:S(2)}) collective-permute-start(bf16[640,128]{1,0:T(8,128)(2,1)S(1)} %fusion.18), channel_id=1, source_target_pairs={{0,12},{4,0},{8,4},{12,8},{1,13},{5,1},{9,5},{13,9},{2,14},{6,2},{... | collective-permute-start | bytes 491528 | tf_op jit(solution)/shard_map/ppermute | solution.py:138
  105.6 5.5 %collective-permute-done.8 = bf16[640,128]{1,0:T(8,128)(2,1)S(1)} collective-permute-done((bf16[640,128]{1,0:T(8,128)(2,1)S(1)}, bf16[640,128]{1,0:T(8,128)(2,1)S(1)}, u32[]{:S(2)}, u32[]{:S(2)}) %collective-permute-start.8) | collective-permute-done | bytes 163872 | tf_op jit(solution)/shard_map/ppermute | solution.py:138
  111.2 4.9 %collective-permute-done.6 = bf16[640,128]{1,0:T(8,128)(2,1)S(1)} collective-permute-done((bf16[640,128]{1,0:T(8,128)(2,1)S(1)}, bf16[640,128]{1,0:T(8,128)(2,1)S(1)}, u32[]{:S(2)}, u32[]{:S(2)}) %collective-permute-start.6) | collective-permute-done | bytes 163872 | tf_op jit(solution)/shard_map/ppermute | solution.py:138
  117.8 3.1 reshape.47
  139.0 5.6 %all-gather.3 = s32[4,2,32]{2,1,0:T(2,128)S(1)} all-gather(s32[1,2,32]{2,1,0:T(2,128)S(1)} %add_bitcast_fusion), channel_id=2, replica_groups=mesh['dp'=8,'fsdp'=4,'tensor'=4] {'fsdp'}, dimensions={0}, use_global_device_ids=true | all-gather | bytes 1280 | tf_op jit(solution)/shard_map/all_gather | solution.py:187
  144.9 30.8 %all-gather.18.cloned.1.call-done = bf16[8192,128]{1,0:T(8,128)(2,1)} async-done(((bf16[256,128]{1,0:T(8,128)(2,1)}), bf16[8192,128]{1,0:T(8,128)(2,1)}) %all-gather.18.cloned.1.call-update) | async-done | bytes 2097168 | tf_op jit(solution)/shard_map/all_gather | solution.py:221
  175.7 3.2 copy.27
  180.6 43.0 %all-gather.10.cloned.1.call-done.refs_6_ = bf16[128,128,128]{2,1,0:T(8,128)(2,1)} async-done(((bf16[4,128,128]{2,1,0:T(8,128)(2,1)}), bf16[128,128,128]{2,1,0:T(8,128)(2,1)}) %all-gather.10.cloned.1.call-update) | async-done | bytes 4194320 | tf_op jit(solution)/shard_map/all_gather | solution.py:186
  223.6 82.2 %all-gather.16.cloned.1.call-done = bf16[10240,512]{1,0:T(8,128)(2,1)} async-done(((bf16[640,512]{1,0:T(8,128)(2,1)}), bf16[10240,512]{1,0:T(8,128)(2,1)}) %all-gather.16.cloned.1.call-update) | async-done | bytes 10485776 | tf_op jit(solution)/shard_map/all_gather | solution.py:183
  307.9 8.8 %shard_map.111 = bf16[640,1792]{1,0:T(8,128)(2,1)} custom-call(s32[5]{0:T(128)S(1)} %pad_add_fusion.refs_0_, s32[128]{0:T(128)S(1)} %reshape_squeeze.6.refs_1_, s32[128]{0:T(128)S(1)} %reshape_squeeze.7.refs_2_, bf16[640,512]{1,0:T(8,128)(2,1)S(1)} %all_gather.32.refs_3_, bf16[512,1792]{1,0:T(8,128)(2,1)S(1)} %bitcast.94, bf16[16,640,512]{2,1,0:T(8,128)(2,1)} %bitcast.97, ...), custom_call_target="tpu_custom_call" | custom-call | flops 1174405120 | bytes 10485760 | tf_op jit(solution)/shard_map/pallas_call | solution.py:116
  (100 shorter events, 49.9 us)
Async XLA Ops:
  7.2 137.7 %all-gather.14.cloned.1.call-start = ((), (), s32[]{:S(2)}) async-start(), calls=%async_computation.2 | async-start | bytes 1179648 | tf_op jit(solution)/shard_map/all_gather | solution.py:213
  11.4 18.5 %collective-permute-start.2 = (bf16[640,128]{1,0:T(8,128)(2,1)S(1)}, bf16[640,128]{1,0:T(8,128)(2,1)S(1)}, u32[]{:S(2)}, u32[]{:S(2)}) collective-permute-start(bf16[640,128]{1,0:T(8,128)(2,1)S(1)} %get-tuple-element.32), channel_id=1, source_target_pairs={{0,12},{4,0},{8,4},{12,8},{1,13},{5,1},{9,5},{13,9},{2,14},{6,2},{... | collective-permute-start | bytes 491528 | tf_op jit(solution)/shard_map/ppermute | solution.py:138
  15.0 14.9 %collective-permute-start.1 = (bf16[640,128]{1,0:T(8,128)(2,1)S(1)}, bf16[640,128]{1,0:T(8,128)(2,1)S(1)}, u32[]{:S(2)}, u32[]{:S(2)}) collective-permute-start(bf16[640,128]{1,0:T(8,128)(2,1)S(1)} %get-tuple-element.32), channel_id=1, source_target_pairs={{0,8},{4,12},{8,0},{12,4},{1,9},{5,13},{9,1},{13,5},{2,10},{6,14},... | collective-permute-start | bytes 491528 | tf_op jit(solution)/shard_map/ppermute | solution.py:138
  15.4 14.5 %collective-permute-start = (bf16[640,128]{1,0:T(8,128)(2,1)S(1)}, bf16[640,128]{1,0:T(8,128)(2,1)S(1)}, u32[]{:S(2)}, u32[]{:S(2)}) collective-permute-start(bf16[640,128]{1,0:T(8,128)(2,1)S(1)} %get-tuple-element.32), channel_id=1, source_target_pairs={{0,4},{4,8},{8,12},{12,0},{1,5},{5,9},{9,13},{13,1},{2,6},{6,10},{... | collective-permute-start | bytes 491528 | tf_op jit(solution)/shard_map/ppermute | solution.py:138
  28.3 24.8 %collective-permute-start.17 = (bf16[4,4,128,128]{3,2,1,0:T(8,128)(2,1)S(1)}, bf16[4,4,128,128]{3,2,1,0:T(8,128)(2,1)S(1)}, u32[]{:S(2)}, u32[]{:S(2)}) collective-permute-start(bf16[4,4,128,128]{3,2,1,0:T(8,128)(2,1)S(1)} %dynamic-slice_bitcast_fusion), channel_id=1, source_target_pairs={{0,16},{16,0},{32,48},{48,32},{64,80},{80,64},{96,112},{112,96},{1... | collective-permute-start | bytes 1572872 | tf_op jit(solution)/shard_map/ppermute | solution.py:153
  52.2 14.2 %collective-permute-start.13 = (bf16[4,64,1792]{2,1,0:T(8,128)(2,1)}, bf16[4,64,1792]{2,1,0:T(8,128)(2,1)}, u32[]{:S(2)}, u32[]{:S(2)}) collective-permute-start(bf16[4,64,1792]{2,1,0:T(8,128)(2,1)} %fusion.4), channel_id=1, source_target_pairs={{0,16},{16,0},{32,48},{48,32},{64,80},{80,64},{96,112},{112,96},{1... | collective-permute-start | bytes 2752520 | tf_op jit(solution)/shard_map/ppermute | solution.py:153
  53.4 5.4 %collective-permute-start.20 = (bf16[4,128,128]{2,1,0:T(8,128)(2,1)S(1)}, bf16[4,128,128]{2,1,0:T(8,128)(2,1)S(1)}, u32[]{:S(2)}, u32[]{:S(2)}) collective-permute-start(bf16[4,128,128]{2,1,0:T(8,128)(2,1)S(1)} %get-tuple-element.27), channel_id=1, source_target_pairs={{0,96},{16,112},{32,0},{48,16},{64,32},{80,48},{96,64},{112,80},{1... | collective-permute-start | bytes 393224 | tf_op jit(solution)/shard_map/ppermute | solution.py:144
  55.9 5.6 %collective-permute-start.19 = (bf16[4,128,128]{2,1,0:T(8,128)(2,1)S(1)}, bf16[4,128,128]{2,1,0:T(8,128)(2,1)S(1)}, u32[]{:S(2)}, u32[]{:S(2)}) collective-permute-start(bf16[4,128,128]{2,1,0:T(8,128)(2,1)S(1)} %get-tuple-element.28), channel_id=1, source_target_pairs={{0,64},{16,80},{32,96},{48,112},{64,0},{80,16},{96,32},{112,48},{1... | collective-permute-start | bytes 393224 | tf_op jit(solution)/shard_map/ppermute | solution.py:144
  56.4 9.1 %collective-permute-start.18 = (bf16[4,128,128]{2,1,0:T(8,128)(2,1)S(1)}, bf16[4,128,128]{2,1,0:T(8,128)(2,1)S(1)}, u32[]{:S(2)}, u32[]{:S(2)}) collective-permute-start(bf16[4,128,128]{2,1,0:T(8,128)(2,1)S(1)} %get-tuple-element.26), channel_id=1, source_target_pairs={{0,32},{16,48},{32,64},{48,80},{64,96},{80,112},{96,0},{112,16},{1... | collective-permute-start | bytes 393224 | tf_op jit(solution)/shard_map/ppermute | solution.py:144
  66.3 78.6 %all-gather.12.cloned.1.call-start = ((), (), s32[]{:S(2)}) async-start(), calls=%async_computation.1 | async-start | bytes 2064384 | tf_op jit(solution)/shard_map/all_gather | solution.py:217
  68.4 6.6 %collective-permute-start.16 = (bf16[64,1792]{1,0:T(8,128)(2,1)S(1)}, bf16[64,1792]{1,0:T(8,128)(2,1)S(1)}, u32[]{:S(2)}, u32[]{:S(2)}) collective-permute-start(bf16[64,1792]{1,0:T(8,128)(2,1)S(1)} %get-tuple-element.21), channel_id=1, source_target_pairs={{0,96},{16,112},{32,0},{48,16},{64,32},{80,48},{96,64},{112,80},{1... | collective-permute-start | bytes 688136 | tf_op jit(solution)/shard_map/ppermute | solution.py:144
  68.5 7.6 %collective-permute-start.15 = (bf16[64,1792]{1,0:T(8,128)(2,1)S(1)}, bf16[64,1792]{1,0:T(8,128)(2,1)S(1)}, u32[]{:S(2)}, u32[]{:S(2)}) collective-permute-start(bf16[64,1792]{1,0:T(8,128)(2,1)S(1)} %get-tuple-element.22), channel_id=1, source_target_pairs={{0,64},{16,80},{32,96},{48,112},{64,0},{80,16},{96,32},{112,48},{1... | collective-permute-start | bytes 688136 | tf_op jit(solution)/shard_map/ppermute | solution.py:144
  68.7 17.1 %collective-permute-start.14 = (bf16[64,1792]{1,0:T(8,128)(2,1)S(1)}, bf16[64,1792]{1,0:T(8,128)(2,1)S(1)}, u32[]{:S(2)}, u32[]{:S(2)}) collective-permute-start(bf16[64,1792]{1,0:T(8,128)(2,1)S(1)} %get-tuple-element.20), channel_id=1, source_target_pairs={{0,32},{16,48},{32,64},{48,80},{64,96},{80,112},{96,0},{112,16},{1... | collective-permute-start | bytes 688136 | tf_op jit(solution)/shard_map/ppermute | solution.py:144
  86.6 89.1 %all-gather.18.cloned.1.call-start = ((), (), s32[]{:S(2)}) async-start(), calls=%async_computation.4 | async-start | bytes 2162688 | tf_op jit(solution)/shard_map/all_gather | solution.py:221
  90.0 5.3 %collective-permute-start.5 = (bf16[640,128]{1,0:T(8,128)(2,1)S(1)}, bf16[640,128]{1,0:T(8,128)(2,1)S(1)}, u32[]{:S(2)}, u32[]{:S(2)}) collective-permute-start(bf16[640,128]{1,0:T(8,128)(2,1)S(1)} %get-tuple-element.24), channel_id=1, source_target_pairs={{0,3},{1,0},{2,1},{3,2},{4,7},{5,4},{6,5},{7,6},{8,11},{9,8},{10,9... | collective-permute-start | bytes 491528 | tf_op jit(solution)/shard_map/ppermute | solution.py:138
  90.1 6.7 %collective-permute-start.4 = (bf16[640,128]{1,0:T(8,128)(2,1)S(1)}, bf16[640,128]{1,0:T(8,128)(2,1)S(1)}, u32[]{:S(2)}, u32[]{:S(2)}) collective-permute-start(bf16[640,128]{1,0:T(8,128)(2,1)S(1)} %get-tuple-element.25), channel_id=1, source_target_pairs={{0,2},{1,3},{2,0},{3,1},{4,6},{5,7},{6,4},{7,5},{8,10},{9,11},{10,... | collective-permute-start | bytes 491528 | tf_op jit(solution)/shard_map/ppermute | solution.py:138
  92.6 8.2 %collective-permute-start.3 = (bf16[640,128]{1,0:T(8,128)(2,1)S(1)}, bf16[640,128]{1,0:T(8,128)(2,1)S(1)}, u32[]{:S(2)}, u32[]{:S(2)}) collective-permute-start(bf16[640,128]{1,0:T(8,128)(2,1)S(1)} %get-tuple-element.23), channel_id=1, source_target_pairs={{0,1},{1,2},{2,3},{3,0},{4,5},{5,6},{6,7},{7,4},{8,9},{9,10},{10,1... | collective-permute-start | bytes 491528 | tf_op jit(solution)/shard_map/ppermute | solution.py:138
  100.8 10.3 %collective-permute-start.8 = (bf16[640,128]{1,0:T(8,128)(2,1)S(1)}, bf16[640,128]{1,0:T(8,128)(2,1)S(1)}, u32[]{:S(2)}, u32[]{:S(2)}) collective-permute-start(bf16[640,128]{1,0:T(8,128)(2,1)S(1)} %fusion.18), channel_id=1, source_target_pairs={{0,12},{4,0},{8,4},{12,8},{1,13},{5,1},{9,5},{13,9},{2,14},{6,2},{... | collective-permute-start | bytes 491528 | tf_op jit(solution)/shard_map/ppermute | solution.py:138
  105.0 6.2 %collective-permute-start.7 = (bf16[640,128]{1,0:T(8,128)(2,1)S(1)}, bf16[640,128]{1,0:T(8,128)(2,1)S(1)}, u32[]{:S(2)}, u32[]{:S(2)}) collective-permute-start(bf16[640,128]{1,0:T(8,128)(2,1)S(1)} %fusion.18), channel_id=1, source_target_pairs={{0,8},{4,12},{8,0},{12,4},{1,9},{5,13},{9,1},{13,5},{2,10},{6,14},... | collective-permute-start | bytes 491528 | tf_op jit(solution)/shard_map/ppermute | solution.py:138
  105.3 10.8 %collective-permute-start.6 = (bf16[640,128]{1,0:T(8,128)(2,1)S(1)}, bf16[640,128]{1,0:T(8,128)(2,1)S(1)}, u32[]{:S(2)}, u32[]{:S(2)}) collective-permute-start(bf16[640,128]{1,0:T(8,128)(2,1)S(1)} %fusion.18), channel_id=1, source_target_pairs={{0,4},{4,8},{8,12},{12,0},{1,5},{5,9},{9,13},{13,1},{2,6},{6,10},{... | collective-permute-start | bytes 491528 | tf_op jit(solution)/shard_map/ppermute | solution.py:138
  127.5 5.3 %collective-permute-start.11 = (bf16[256,128]{1,0:T(8,128)(2,1)S(1)}, bf16[256,128]{1,0:T(8,128)(2,1)S(1)}, u32[]{:S(2)}, u32[]{:S(2)}) collective-permute-start(bf16[256,128]{1,0:T(8,128)(2,1)S(1)} %get-tuple-element.31), channel_id=1, source_target_pairs={{0,64},{16,80},{32,96},{48,112},{64,0},{80,16},{96,32},{112,48},{1... | collective-permute-start | bytes 196616 | tf_op jit(solution)/shard_map/ppermute | solution.py:144
  127.6 6.8 %collective-permute-start.10 = (bf16[256,128]{1,0:T(8,128)(2,1)S(1)}, bf16[256,128]{1,0:T(8,128)(2,1)S(1)}, u32[]{:S(2)}, u32[]{:S(2)}) collective-permute-start(bf16[256,128]{1,0:T(8,128)(2,1)S(1)} %get-tuple-element.29), channel_id=1, source_target_pairs={{0,32},{16,48},{32,64},{48,80},{64,96},{80,112},{96,0},{112,16},{1... | collective-permute-start | bytes 196616 | tf_op jit(solution)/shard_map/ppermute | solution.py:144
  135.1 88.4 %all-gather.10.cloned.1.call-start = ((), (), s32[]{:S(2)}) async-start(), calls=%async_computation | async-start | bytes 4325376 | tf_op jit(solution)/shard_map/all_gather | solution.py:186
  136.8 169.0 %all-gather.16.cloned.1.call-start = ((), (), s32[]{:S(2)}) async-start(), calls=%async_computation.3 | async-start | bytes 11141120 | tf_op jit(solution)/shard_map/all_gather | solution.py:183
  (15 other events, 104.1 us)
Sparse Core Ops, SparseCore 0:
  66.4 24.0 all-gather.13
  92.7 24.0 all-gather.11
  135.3 40.3 all-gather.17
  178.3 45.1 all-gather.9
  226.2 79.5 all-gather.15

commit v2 on v0

v2 whole, which is shorter than its diff:
```python
import jax
import jax.numpy as jnp
from jax import lax
from jax.experimental import pallas as pl
from jax.experimental.pallas import tpu as pltpu
from jax.sharding import PartitionSpec as P

F32 = jnp.float32
BF16 = jnp.bfloat16
SIDE = 128
SMEM = pl.BlockSpec(memory_space=pltpu.SMEM)
VMEM = pl.BlockSpec(memory_space=pltpu.VMEM)
HBM = pl.BlockSpec(memory_space=pl.ANY)


def lanes(block):
    return pl.ds(pl.multiple_of(block * SIDE, SIDE), SIDE)


def params(mib):
    return pltpu.CompilerParams(vmem_limit_bytes=mib << 20)


def shape(dims, dtype):
    return jax.ShapeDtypeStruct(dims, dtype)


def cost(flops, nbytes):
    return pl.CostEstimate(flops=int(flops), bytes_accessed=int(nbytes), transcendentals=0)


def far_kernel(
    n_f, q_blocks, info, rows, cols, tok, vals, left, top, bottom, part, part_low, acc
):
    quarter = lax.rem(info[1] + n_f // 2, n_f)
    acc[...] = jnp.zeros_like(acc)

    def body(s, carry):
        col = cols[s]

        @pl.when(col // q_blocks == quarter)
        def _():
            acc[:, lanes(col - quarter * q_blocks)] += jnp.dot(
                tok[:, lanes(rows[s])], vals[s], preferred_element_type=F32
            )

        return carry

    lax.fori_loop(0, info[0], body, 0)
    half = top.shape[0]
    top[...] = acc[:half].astype(BF16)
    bottom[...] = acc[half:].astype(BF16)
    rank = jnp.dot(tok[...], left[:, lanes(info[2])], preferred_element_type=F32)
    part[...] = rank
    part_low[...] = rank.astype(BF16)


def near_kernel(
    n_f, q_blocks, info, rows, cols, tok, vals, p1t, p1b, p3t, p3b, p0, acc
):
    acc[...] = jnp.zeros_like(acc)
    p0[...] = jnp.zeros_like(p0)

    def body(s, carry):
        col = cols[s]
        q = col // q_blocks
        k = lax.rem(q - info[1] + n_f, n_f)
        here = lanes(col - q * q_blocks)

        @pl.when(k != n_f // 2)
        def _():
            prod = jnp.dot(tok[:, lanes(rows[s])], vals[s], preferred_element_type=F32)

            @pl.when(k == 0)
            def _():
                p0[:, here] += prod

            @pl.when(k != 0)
            def _():
                acc[k // 2, :, here] += prod

        return carry

    lax.fori_loop(0, info[0], body, 0)
    half = p1t.shape[0]
    p1t[...] = acc[0, :half]
    p1b[...] = acc[0, half:].astype(BF16)
    p3t[...] = acc[1, :half].astype(BF16)
    p3b[...] = acc[1, half:]


def back_kernel(n_t, info, cot, right, own, s1, s2, s3, cotq, full, sem):
    quarter = cotq.shape[1]
    src = cot.at[:, pl.ds(pl.multiple_of(info[1] * quarter, SIDE), quarter)]
    copy = pltpu.make_async_copy(src, cotq, sem)
    copy.start()
    copy.wait()
    full[...] = lax.dot_general(
        cotq[...], right[...], (((1,), (1,)), ((), ())), preferred_element_type=F32
    )
    own[...] = full[:, lanes(info[2])]
    for k, out in ((1, s1), (2, s2), (3, s3)):
        out[...] = full[:, lanes(lax.rem(info[2] + k, n_t))].astype(BF16)


def blocks_kernel(chips, info, rows, cols, tok, cot, mine, theirs):
    mine[...] = jnp.zeros_like(mine)
    theirs[...] = jnp.zeros_like(theirs)
    per = mine.shape[1]

    def body(s, carry):
        grad = lax.dot_general(
            tok[:, lanes(rows[s])],
            cot[:, lanes(cols[s])],
            (((0,), (0,)), ((), ())),
            preferred_element_type=F32,
        )
        owner = s // per
        j = lax.rem(owner // 2 - info[3] + chips, chips)
        at = lax.rem(s, per)
        keep = lax.rem(owner, 2) == info[4]

        @pl.when(keep)
        def _():
            mine[j, at] = grad

        @pl.when(jnp.logical_not(keep))
        def _():
            theirs[j, at] = grad.astype(BF16)

        return carry

    lax.fori_loop(0, info[0], body, 0)


def factors_kernel(
    n_t, chips, info, tok, cot, g0, g1, g2, g3, back,
    m0, m1, m2, m3, theirs, cotq, left, right, sem,
):
    quarter = cotq.shape[1]
    src = cot.at[:, pl.ds(pl.multiple_of(info[1] * quarter, SIDE), quarter)]
    copy = pltpu.make_async_copy(src, cotq, sem)
    copy.start()
    left[...] = lax.dot_general(
        back[...], tok[...], (((0,), (0,)), ((), ())), preferred_element_type=F32
    ).T
    copy.wait()
    for k, g in enumerate((g0, g1, g2, g3)):
        row = pl.multiple_of(lax.rem(info[2] - k + n_t, n_t) * SIDE, SIDE)
        right[pl.ds(row, SIDE), :] = lax.dot_general(
            g[...], cotq[...], (((0,), (0,)), ((), ())), preferred_element_type=F32
        )
    n_l = left.shape[0] // (2 * chips)
    n_r = right.shape[0] // (2 * chips)
    for j, mine in enumerate((m0, m1, m2, m3)):
        chip = lax.rem(info[3] + j, chips)
        for core, out in ((info[4], mine), (1 - info[4], theirs.at[j])):
            at = chip * 2 + core
            out[:n_l] = left[pl.ds(pl.multiple_of(at * n_l, n_l), n_l), :].astype(out.dtype)
            for p in range(quarter // SIDE):
                out[n_l + p * n_r : n_l + (p + 1) * n_r] = right[
                    pl.ds(pl.multiple_of(at * n_r, n_r), n_r), p * SIDE : (p + 1) * SIDE
                ].astype(out.dtype)


def finish_kernel(n_t, info, g0, g1, g2, g3, right, p0, at, ab, bt, bb, out):
    i = pl.program_id(0)
    acc = p0[...]
    for k, g in enumerate((g0, g1, g2, g3)):
        row = pl.multiple_of(lax.rem(info[2] - k + n_t, n_t) * SIDE, SIDE)
        acc += jnp.dot(g[...], right[pl.ds(row, SIDE), :], preferred_element_type=F32)

    @pl.when(i < pl.num_programs(0) // 2)
    def _():
        out[...] = (acc + at[...].astype(F32) + bt[...].astype(F32)).astype(BF16)

    @pl.when(i >= pl.num_programs(0) // 2)
    def _():
        out[...] = (acc + ab[...].astype(F32) + bb[...].astype(F32)).astype(BF16)


def spread_kernel(n_t, chips, n_l, n_r, *refs):
    info, ours, partner, left, right, blocks, sem = refs
    quarter = right.shape[1]
    panels = quarter // SIDE
    copies = []
    for who, src in ((info[4], ours), (1 - info[4], partner)):
        for j in range(chips):
            at = lax.rem(info[3] - j + chips, chips) * 2 + who
            for k in range(n_t):
                col = lax.rem(info[2] - k + n_t, n_t)
                dst = left.at[pl.ds(pl.multiple_of(at * n_l, n_l), n_l), lanes(col)]
                copies.append((src.at[j, pl.ds(k * n_l, n_l)], dst))
            base = n_t * n_l
            for p in range(panels):
                dst = right.at[
                    pl.ds(pl.multiple_of(at * n_r, n_r), n_r), pl.ds(p * SIDE, SIDE)
                ]
                copies.append((src.at[j, pl.ds(base + p * n_r, n_r)], dst))
            base += panels * n_r
            per = blocks.shape[0] // (2 * chips * SIDE) * SIDE
            dst = blocks.at[pl.ds(pl.multiple_of(at * per, per), per)]
            copies.append((src.at[j, pl.ds(base, per)], dst))
    for src, dst in copies:
        dst[...] = src[...]


def shift(x, axis, n, k):
    return lax.ppermute(x, axis, [(i, (i + k) % n) for i in range(n)])


def chip_shift(x, n_data, k):
    chips = n_data // 2
    perm = [(2 * a + c, 2 * ((a + k) % chips) + c) for a in range(chips) for c in range(2)]
    return lax.ppermute(x, "dp", perm)


def core_swap(x, n_data):
    return lax.ppermute(x, "dp", [(i, i ^ 1) for i in range(n_data)])


def scatter_chips(mine, got, n_data):
    chips = n_data // 2
    total = mine[0] + got[0].astype(F32)
    for k in range(1, chips):
        piece = (mine[k] + got[k].astype(F32)).astype(BF16)
        total = total + chip_shift(piece, n_data, k).astype(F32)
    return total.astype(BF16)


def per_device(
    tokens, cotangent, left_factor, right_factor, block_values, block_rows, block_cols, block_counts
):
    n_fsdp = lax.axis_size("fsdp")
    n_tensor = lax.axis_size("tensor")
    n_data = lax.axis_size("dp")
    f_index = lax.axis_index("fsdp")
    t_index = lax.axis_index("tensor")
    d_index = lax.axis_index("dp")
    chips = n_data // 2
    maxb = block_values.shape[0]
    tok_rows, features = tokens.shape
    right = right_factor.reshape(right_factor.shape[0], -1)
    rank_size, quarter = right.shape
    q_blocks = quarter // SIDE
    r_part = rank_size // n_tensor
    half = tok_rows // 2
    live = block_counts[f_index * n_tensor + t_index]
    info = jnp.stack([live, f_index, t_index, d_index // 2, d_index % 2]).astype(jnp.int32)
    block_flops = 2 * tok_rows * SIDE * SIDE * maxb

    half_low = shape((half, quarter), BF16)
    half_wide = shape((half, quarter), F32)
    part = shape((tok_rows, r_part), F32)
    part_low = shape((tok_rows, r_part), BF16)
    p2t, p2b, rank_part, rank_low = pl.pallas_call(
        lambda *refs: far_kernel(n_fsdp, q_blocks, *refs),
        out_shape=(half_low, half_low, part, part_low),
        in_specs=[SMEM, SMEM, SMEM, VMEM, VMEM, VMEM],
        out_specs=(VMEM,) * 4,
        scratch_shapes=[pltpu.VMEM((tok_rows, quarter), F32)],
        cost_estimate=cost(block_flops / 2, 8 << 20),
        compiler_params=params(32),
    )(info, block_rows, block_cols, tokens, block_values, left_factor)
    in_t = shift(p2t, "fsdp", n_fsdp, 1)
    in_b = shift(p2b, "fsdp", n_fsdp, -1)
    for k in range(1, n_fsdp):
        rank_part = rank_part + shift(rank_low, "fsdp", n_fsdp, k).astype(F32)
    rank_t = rank_part.astype(BF16)
    ranks = [rank_t] + [shift(rank_t, "tensor", n_tensor, k) for k in range(1, n_tensor)]

    back_sum, b1, b2, b3 = pl.pallas_call(
        lambda *refs: back_kernel(n_tensor, *refs),
        out_shape=(part, part_low, part_low, part_low),
        in_specs=[SMEM, HBM, VMEM],
        out_specs=(VMEM,) * 4,
        scratch_shapes=[
            pltpu.VMEM((tok_rows, quarter), BF16),
            pltpu.VMEM((tok_rows, rank_size), F32),
            pltpu.SemaphoreType.DMA,
        ],
        cost_estimate=cost(2 * tok_rows * quarter * rank_size, 6 << 20),
        compiler_params=params(24),
    )(info, cotangent, right)
    for k, b in ((1, b1), (2, b2), (3, b3)):
        back_sum = back_sum + shift(b, "tensor", n_tensor, k).astype(F32)
    back_low = back_sum.astype(BF16)
    for k in range(1, n_fsdp):
        back_sum = back_sum + shift(back_low, "fsdp", n_fsdp, k).astype(F32)
    back = back_sum.astype(BF16)

    p1t, p1b, p3t, p3b, p0 = pl.pallas_call(
        lambda *refs: near_kernel(n_fsdp, q_blocks, *refs),
        out_shape=(half_wide, half_low, half_low, half_wide, shape((tok_rows, quarter), F32)),
        in_specs=[SMEM, SMEM, SMEM, VMEM, VMEM],
        out_specs=(VMEM,) * 5,
        scratch_shapes=[pltpu.VMEM((2, tok_rows, quarter), F32)],
        cost_estimate=cost(block_flops, 15 << 20),
        compiler_params=params(40),
    )(info, block_rows, block_cols, tokens, block_values)
    ab = shift(p1b, "fsdp", n_fsdp, 1)
    bt = shift(p3t, "fsdp", n_fsdp, -1)
    at = shift((p1t + in_t.astype(F32)).astype(BF16), "fsdp", n_fsdp, 1)
    bb = shift((p3b + in_b.astype(F32)).astype(BF16), "fsdp", n_fsdp, -1)

    per = maxb // n_data
    blocks_mine, blocks_theirs = pl.pallas_call(
        lambda *refs: blocks_kernel(chips, *refs),
        out_shape=(
            shape((chips, per, SIDE, SIDE), F32),
            shape((chips, per, SIDE, SIDE), BF16),
        ),
        in_specs=[SMEM, SMEM, SMEM, VMEM, VMEM],
        out_specs=(VMEM,) * 2,
        cost_estimate=cost(block_flops, 15 << 20),
        compiler_params=params(40),
    )(info, block_rows, block_cols, tokens, cotangent)
    blocks_got = core_swap(blocks_theirs, n_data)
    block_part = scatter_chips(blocks_mine, blocks_got, n_data).reshape(per * SIDE, SIDE)

    n_l = features // n_data
    n_r = rank_size // n_data
    rows_lr = n_l + q_blocks * n_r
    wide = shape((rows_lr, SIDE), F32)
    m0, m1, m2, m3, theirs = pl.pallas_call(
        lambda *refs: factors_kernel(n_tensor, chips, *refs),
        out_shape=(wide,) * 4 + (shape((chips, rows_lr, SIDE), BF16),),
        in_specs=[SMEM, VMEM, HBM] + [VMEM] * 5,
        out_specs=(VMEM,) * 5,
        scratch_shapes=[
            pltpu.VMEM((tok_rows, quarter), BF16),
            pltpu.VMEM((features, r_part), F32),
            pltpu.VMEM((rank_size, quarter), F32),
            pltpu.SemaphoreType.DMA,
        ],
        cost_estimate=cost(2 * tok_rows * (quarter * rank_size + features * r_part), 10 << 20),
        compiler_params=params(40),
    )(info, tokens, cotangent, *ranks, back)
    got = core_swap(theirs, n_data)
    chunk = scatter_chips((m0, m1, m2, m3), got, n_data)
    left_own = chunk[:n_l]
    lefts = [left_own] + [shift(left_own, "tensor", n_tensor, k) for k in range(1, n_tensor)]
    message = jnp.concatenate(lefts + [chunk[n_l:], block_part], axis=0)
    ours = jnp.stack([message] + [chip_shift(message, n_data, k) for k in range(1, chips)])
    partner = core_swap(ours, n_data)
    out_left, out_right, out_blocks = pl.pallas_call(
        lambda *refs: spread_kernel(n_tensor, chips, n_l, n_r, *refs),
        out_shape=(
            shape((features, rank_size), BF16),
            shape((rank_size, quarter), BF16),
            shape((maxb * SIDE, SIDE), BF16),
        ),
        in_specs=[SMEM, VMEM, VMEM],
        out_specs=(VMEM,) * 3,
        scratch_shapes=[pltpu.SemaphoreType.DMA],
        cost_estimate=cost(0, 10 << 20),
        compiler_params=params(32),
    )(info, ours, partner)

    steps = 4
    block = tok_rows // steps
    whole = lambda dims: pl.BlockSpec(dims, lambda i: (0, 0))
    by_row = lambda width: pl.BlockSpec((block, width), lambda i: (i, 0))
    first = pl.BlockSpec((block, quarter), lambda i: (jnp.minimum(i, steps // 2 - 1), 0))
    last = pl.BlockSpec((block, quarter), lambda i: (jnp.maximum(i - steps // 2, 0), 0))
    mixed = pl.pallas_call(
        lambda *refs: finish_kernel(n_tensor, *refs),
        out_shape=shape((tok_rows, quarter), BF16),
        grid=(steps,),
        in_specs=[SMEM] + [by_row(r_part)] * 4
        + [whole((rank_size, quarter)), by_row(quarter), first, last, first, last],
        out_specs=by_row(quarter),
        cost_estimate=cost(2 * tok_rows * quarter * rank_size, 14 << 20),
        compiler_params=params(32),
    )(info, *ranks, right, p0, at, ab, bt, bb)
    return (
        mixed.reshape(tok_rows, 1, quarter),
        out_left,
        out_right.reshape(right_factor.shape),
        out_blocks.reshape(maxb, SIDE, SIDE),
    )


def solution(mesh):
    return jax.shard_map(
        per_device,
        mesh=mesh,
        in_specs=(
            P("dp", "fsdp"),
            P("dp", "tensor"),
            P("fsdp", None),
            P(None, "tensor", "fsdp"),
            P(("fsdp", "tensor"), None, None),
            P(("fsdp", "tensor")),
            P(("fsdp", "tensor")),
            P(),
        ),
        out_specs=(
            P("dp", "tensor", "fsdp"),
            P("fsdp", None),
            P(None, "tensor", "fsdp"),
            P(("fsdp", "tensor"), None, None),
        ),
        check_vma=False,
    )
```

time: 720 us -> 196 us (0.27)
  the two profiles are of different devices: /device:TPU:1 before, /device:TPU:32 now
where the time goes in v2:
time: 196 us; the launch traced here: 194 us
  waiting for transfers between devices  96.8 us (49%)
  starting transfers between devices  56.2 us (29%)
  Pallas kernels  27.1 us (14%)
  local copies, waits for them, and re-layouts  11.6 us (6%)
    ppermute x21, waiting for transfers between devices, shift(): return lax.ppermute(x, axis, [(i, (i + k) % n) for i in range(n)])  65.2 us
    ppermute x21, starting transfers between devices, shift(): return lax.ppermute(x, axis, [(i, (i + k) % n) for i in range(n)])  40.4 us
    ppermute x9, waiting for transfers between devices, chip_shift(): return lax.ppermute(x, 'dp', perm)  31.7 us
    ppermute x9, starting transfers between devices, chip_shift(): return lax.ppermute(x, 'dp', perm)  15.1 us
    unnamed x32, local copies, waits for them, and re-layouts  9.62 us
    pallas_call x1, Pallas kernels, per_device(): pl.pallas_call(lambda *refs: near_kernel(n_fsdp, q_blocks, *refs), out_sh...  5.44 us
    pallas_call x1, Pallas kernels, per_device(): pl.pallas_call(lambda *refs: finish_kernel(n_tensor, *refs), out_shape=sh...  5.28 us
    pallas_call x1, Pallas kernels, per_device(): pl.pallas_call(lambda *refs: factors_kernel(n_tensor, chips, *refs), out_...  4.53 us
  transfers between devices with their start and end apart: 33, of which 19 were waited for; matrix products, arithmetic and copies ran while one was open for 1% of the time, Pallas kernels for 9%

profile of v2, /device:TPU:32, one launch (start us, length us, event | category | flops | bytes accessed | tf_op | source)
XLA Modules:
  0.0 194.5 jit_solution(10649544427345090938)
XLA Ops:
  2.6 3.6 %copy-done = bf16[640,7168]{1,0:T(8,128)(2,1)S(1)} copy-done((bf16[640,7168]{1,0:T(8,128)(2,1)S(1)}, bf16[640,7168]{1,0:T(8,128)(2,1)}, u32[]{:S(2)}) %copy-start) | copy-done | bytes 9175064
  7.8 2.4 %shard_map.114 = (f32[640,128]{1,0:T(8,128)S(1)}, bf16[640,128]{1,0:T(8,128)(2,1)S(1)}, bf16[640,128]{1,0:T(8,128)(2,1)S(1)}, bf16[640,128]{1,0:T(8,128)(2,1)S(1)}) custom-call(s32[5]{0:T(128)S(1)} %stack.34.refs_0_, bf16[640,7168]{1,0:T(8,128)(2,1)S(1)} %copy-done, bf16[512,1792]{1,0:T(8,128)(2,1)S(1)} %bitcast.49), custom_call_target="tpu_custom_call" | custom-call | flops 1174405120 | bytes 6291456 | tf_op jit(solution)/shard_map/pallas_call | solution.py:272
  10.3 3.4 %collective-permute-start.13 = (bf16[640,128]{1,0:T(8,128)(2,1)S(1)}, bf16[640,128]{1,0:T(8,128)(2,1)S(1)}, u32[]{:S(2)}, u32[]{:S(2)}) collective-permute-start(bf16[640,128]{1,0:T(8,128)(2,1)S(1)} %get-tuple-element.38), channel_id=1, source_target_pairs={{0,2},{1,3},{2,0},{3,1},{4,6},{5,7},{6,4},{7,5},{8,10},{9,11},{10,... | collective-permute-start | bytes 491528 | tf_op jit(solution)/shard_map/ppermute | solution.py:209
  18.7 3.2 %shard_map.111 = (bf16[320,1792]{1,0:T(8,128)(2,1)}, bf16[320,1792]{1,0:T(8,128)(2,1)S(1)}, f32[640,128]{1,0:T(8,128)S(1)}, bf16[640,128]{1,0:T(8,128)(2,1)S(1)}) custom-call(s32[5]{0:T(128)S(1)} %stack.34.refs_0_, s32[32]{0:T(128)S(1)} %copy-done.9, s32[32]{0:T(128)S(1)} %copy-done.10, bf16[640,2048]{1,0:T(8,128)(2,1)S(1)} %copy-done.1, ...), custom_call_target="tpu_custom_call" | custom-call | flops 335544320 | bytes 8388608 | tf_op jit(solution)/shard_map/pallas_call | solution.py:256
  21.9 3.4 %collective-permute-start.2 = (bf16[640,128]{1,0:T(8,128)(2,1)S(1)}, bf16[640,128]{1,0:T(8,128)(2,1)S(1)}, u32[]{:S(2)}, u32[]{:S(2)}) collective-permute-start(bf16[640,128]{1,0:T(8,128)(2,1)S(1)} %get-tuple-element.28), channel_id=1, source_target_pairs={{0,12},{4,0},{8,4},{12,8},{1,13},{5,1},{9,5},{13,9},{2,14},{6,2},{... | collective-permute-start | bytes 491528 | tf_op jit(solution)/shard_map/ppermute | solution.py:209
  33.9 5.0 %collective-permute-done = bf16[640,128]{1,0:T(8,128)(2,1)S(1)} collective-permute-done((bf16[640,128]{1,0:T(8,128)(2,1)S(1)}, bf16[640,128]{1,0:T(8,128)(2,1)S(1)}, u32[]{:S(2)}, u32[]{:S(2)}) %collective-permute-start) | collective-permute-done | bytes 163872 | tf_op jit(solution)/shard_map/ppermute | solution.py:209
  47.6 4.5 %shard_map.115 = (f32[1152,128]{1,0:T(8,128)S(1)}, f32[1152,128]{1,0:T(8,128)S(1)}, f32[1152,128]{1,0:T(8,128)S(1)}, f32[1152,128]{1,0:T(8,128)S(1)}, bf16[4,1152,128]{2,1,0:T(8,128)(2,1)S(1)}) custom-call(s32[5]{0:T(128)S(1)} %stack.34.refs_0_, bf16[640,2048]{1,0:T(8,128)(2,1)S(1)} %copy-done.1, bf16[640,7168]{1,0:T(8,128)(2,1)} %refs_4_.5, ...), custom_call_target="tpu_custom_call" | custom-call | flops 1509949440 | bytes 10485760 | tf_op jit(solution)/shard_map/pallas_call | solution.py:325
  52.3 2.7 %shard_map.116 = (f32[4,4,128,128]{3,2,1,0:T(8,128)S(1)}, bf16[4,4,128,128]{3,2,1,0:T(8,128)(2,1)S(1)}) custom-call(s32[5]{0:T(128)S(1)} %stack.34.refs_0_, s32[32]{0:T(128)S(1)} %copy-done.9, s32[32]{0:T(128)S(1)} %copy-done.10, bf16[640,2048]{1,0:T(8,128)(2,1)S(1)} %copy-done.1, bf16[640,7168]{1,0:T(8,128)(2,1)S(1)} %bitcast.48), custom_call_target="tpu_custom_call" | custom-call | flops 671088640 | bytes 15728640 | tf_op jit(solution)/shard_map/pallas_call | solution.py:307
  55.7 2.8 %collective-permute-start.21 = (bf16[1152,128]{1,0:T(8,128)(2,1)S(1)}, bf16[1152,128]{1,0:T(8,128)(2,1)S(1)}, u32[]{:S(2)}, u32[]{:S(2)}) collective-permute-start(bf16[1152,128]{1,0:T(8,128)(2,1)S(1)} %get-tuple-element.54), channel_id=1, source_target_pairs={{0,96},{16,112},{32,0},{48,16},{64,32},{80,48},{96,64},{112,80},{1... | collective-permute-start | bytes 884744 | tf_op jit(solution)/shard_map/ppermute | solution.py:215
  60.2 5.9 %collective-permute-start.6 = (bf16[320,1792]{1,0:T(8,128)(2,1)}, bf16[320,1792]{1,0:T(8,128)(2,1)S(1)}, u32[]{:S(2)}, u32[]{:S(2)}) collective-permute-start(bf16[320,1792]{1,0:T(8,128)(2,1)} %get-tuple-element.31), channel_id=1, source_target_pairs={{0,4},{4,8},{8,12},{12,0},{1,5},{5,9},{9,13},{13,1},{2,6},{6,10},{... | collective-permute-start | bytes 3440648 | tf_op jit(solution)/shard_map/ppermute | solution.py:209
  66.2 2.6 %collective-permute-start.28 = (bf16[4,128,128]{2,1,0:T(8,128)(2,1)S(1)}, bf16[4,128,128]{2,1,0:T(8,128)(2,1)S(1)}, u32[]{:S(2)}, u32[]{:S(2)}) collective-permute-start(bf16[4,128,128]{2,1,0:T(8,128)(2,1)S(1)} %get-tuple-element.51), channel_id=1, source_target_pairs={{0,96},{16,112},{32,0},{48,16},{64,32},{80,48},{96,64},{112,80},{1... | collective-permute-start | bytes 393224 | tf_op jit(solution)/shard_map/ppermute | solution.py:215
  68.8 3.3 %collective-permute-done.21 = bf16[1152,128]{1,0:T(8,128)(2,1)S(1)} collective-permute-done((bf16[1152,128]{1,0:T(8,128)(2,1)S(1)}, bf16[1152,128]{1,0:T(8,128)(2,1)S(1)}, u32[]{:S(2)}, u32[]{:S(2)}) %collective-permute-start.21) | collective-permute-done | bytes 294944 | tf_op jit(solution)/shard_map/ppermute | solution.py:215
  72.1 4.7 %collective-permute-start.26 = (bf16[4,128,128]{2,1,0:T(8,128)(2,1)S(1)}, bf16[4,128,128]{2,1,0:T(8,128)(2,1)S(1)}, u32[]{:S(2)}, u32[]{:S(2)}) collective-permute-start(bf16[4,128,128]{2,1,0:T(8,128)(2,1)S(1)} %get-tuple-element.50), channel_id=1, source_target_pairs={{0,32},{16,48},{32,64},{48,80},{64,96},{80,112},{96,0},{112,16},{1... | collective-permute-start | bytes 393224 | tf_op jit(solution)/shard_map/ppermute | solution.py:215
  80.7 3.7 %collective-permute-start.23 = (bf16[256,128]{1,0:T(8,128)(2,1)S(1)}, bf16[256,128]{1,0:T(8,128)(2,1)S(1)}, u32[]{:S(2)}, u32[]{:S(2)}) collective-permute-start(bf16[256,128]{1,0:T(8,128)(2,1)S(1)} %get-tuple-element.56), channel_id=1, source_target_pairs={{0,2},{1,3},{2,0},{3,1},{4,6},{5,7},{6,4},{7,5},{8,10},{9,11},{10,... | collective-permute-start | bytes 196616 | tf_op jit(solution)/shard_map/ppermute | solution.py:209
  93.3 12.5 %collective-permute-done.31 = bf16[2432,128]{1,0:T(8,128)(2,1)S(1)} collective-permute-done((bf16[2432,128]{1,0:T(8,128)(2,1)S(1)}, bf16[2432,128]{1,0:T(8,128)(2,1)S(1)}, u32[]{:S(2)}, u32[]{:S(2)}) %collective-permute-start.31) | collective-permute-done | bytes 622624 | tf_op jit(solution)/shard_map/ppermute | solution.py:215
  105.8 3.3 %collective-permute-done.30 = bf16[2432,128]{1,0:T(8,128)(2,1)S(1)} collective-permute-done((bf16[2432,128]{1,0:T(8,128)(2,1)S(1)}, bf16[2432,128]{1,0:T(8,128)(2,1)S(1)}, u32[]{:S(2)}, u32[]{:S(2)}) %collective-permute-start.30) | collective-permute-done | bytes 622624 | tf_op jit(solution)/shard_map/ppermute | solution.py:215
  109.1 9.3 %collective-permute-done.29 = bf16[2432,128]{1,0:T(8,128)(2,1)S(1)} collective-permute-done((bf16[2432,128]{1,0:T(8,128)(2,1)S(1)}, bf16[2432,128]{1,0:T(8,128)(2,1)S(1)}, u32[]{:S(2)}, u32[]{:S(2)}) %collective-permute-start.29) | collective-permute-done | bytes 622624 | tf_op jit(solution)/shard_map/ppermute | solution.py:215
  120.4 5.4 %shard_map.112 = (f32[320,1792]{1,0:T(8,128)S(1)}, bf16[320,1792]{1,0:T(8,128)(2,1)S(1)}, bf16[320,1792]{1,0:T(8,128)(2,1)S(1)}, f32[320,1792]{1,0:T(8,128)S(1)}, f32[640,1792]{1,0:T(8,128)}) custom-call(s32[5]{0:T(128)S(1)} %stack.34.refs_0_, s32[32]{0:T(128)S(1)} %copy-done.9, s32[32]{0:T(128)S(1)} %copy-done.10, bf16[640,2048]{1,0:T(8,128)(2,1)S(1)} %copy-done.2, ...), custom_call_target="tpu_custom_call" | custom-call | flops 671088640 | bytes 15728640 | tf_op jit(solution)/shard_map/pallas_call | solution.py:292
  125.9 8.1 %collective-permute-start.8 = (bf16[320,1792]{1,0:T(8,128)(2,1)S(1)}, bf16[320,1792]{1,0:T(8,128)(2,1)S(1)}, u32[]{:S(2)}, u32[]{:S(2)}) collective-permute-start(bf16[320,1792]{1,0:T(8,128)(2,1)S(1)} %get-tuple-element.32), channel_id=1, source_target_pairs={{0,4},{4,8},{8,12},{12,0},{1,5},{5,9},{9,13},{13,1},{2,6},{6,10},{... | collective-permute-start | bytes 3440648 | tf_op jit(solution)/shard_map/ppermute | solution.py:209
  137.8 21.8 %collective-permute-done.8.refs_8_ = bf16[320,1792]{1,0:T(8,128)(2,1)S(1)} collective-permute-done((bf16[320,1792]{1,0:T(8,128)(2,1)S(1)}, bf16[320,1792]{1,0:T(8,128)(2,1)S(1)}, u32[]{:S(2)}, u32[]{:S(2)}) %collective-permute-start.8) | collective-permute-done | bytes 1146912 | tf_op jit(solution)/shard_map/ppermute | solution.py:209
  159.6 2.5 %collective-permute-done.9.refs_9_ = bf16[320,1792]{1,0:T(8,128)(2,1)S(1)} collective-permute-done((bf16[320,1792]{1,0:T(8,128)(2,1)S(1)}, bf16[320,1792]{1,0:T(8,128)(2,1)S(1)}, u32[]{:S(2)}, u32[]{:S(2)}) %collective-permute-start.9) | collective-permute-done | bytes 1146912 | tf_op jit(solution)/shard_map/ppermute | solution.py:209
  162.1 21.1 %collective-permute-done.7.refs_7_ = bf16[320,1792]{1,0:T(8,128)(2,1)S(1)} collective-permute-done((bf16[320,1792]{1,0:T(8,128)(2,1)S(1)}, bf16[320,1792]{1,0:T(8,128)(2,1)S(1)}, u32[]{:S(2)}, u32[]{:S(2)}) %collective-permute-start.7) | collective-permute-done | bytes 1146912 | tf_op jit(solution)/shard_map/ppermute | solution.py:209
  185.5 5.3 %shard_map.113 = bf16[640,1792]{1,0:T(8,128)(2,1)} custom-call(s32[5]{0:T(128)S(1)} %stack.34.refs_0_, bf16[640,128]{1,0:T(8,128)(2,1)S(1)} %add_convert_fusion.3.refs_1_.refs_3_, bf16[640,128]{1,0:T(8,128)(2,1)S(1)} %collective-permute-done.3.refs_2_.refs_4_, bf16[640,128]{1,0:T(8,128)(2,1)S(1)} %collective-permute-done.4.refs_3_.refs_5_, ...), custom_call_target="tpu_custom_call" | custom-call | flops 1174405120 | bytes 14680064 | tf_op jit(solution)/shard_map/pallas_call | solution.py:366
  190.7 3.6 %shard_map.117 = (bf16[2048,512]{1,0:T(8,128)(2,1)}, bf16[512,1792]{1,0:T(8,128)(2,1)}, bf16[4096,128]{1,0:T(8,128)(2,1)}) custom-call(s32[5]{0:T(128)S(1)} %stack.34.refs_0_, bf16[4,2432,128]{2,1,0:T(8,128)(2,1)S(1)} %pad_maximum_fusion.refs_1_, bf16[4,2432,128]{2,1,0:T(8,128)(2,1)S(1)} %collective-permute-done.32.refs_2_), custom_call_target="tpu_custom_call" | custom-call | bytes 10485760 | tf_op jit(solution)/shard_map/pallas_call | solution.py:346
  (96 shorter events, 49.5 us)
Async XLA Ops:
  10.2 16.8 %collective-permute-start.14 = (bf16[640,128]{1,0:T(8,128)(2,1)S(1)}, bf16[640,128]{1,0:T(8,128)(2,1)S(1)}, u32[]{:S(2)}, u32[]{:S(2)}) collective-permute-start(bf16[640,128]{1,0:T(8,128)(2,1)S(1)} %get-tuple-element.39), channel_id=1, source_target_pairs={{0,3},{1,0},{2,1},{3,2},{4,7},{5,4},{6,5},{7,6},{8,11},{9,8},{10,9... | collective-permute-start | bytes 491528 | tf_op jit(solution)/shard_map/ppermute | solution.py:209
  10.3 17.8 %collective-permute-start.13 = (bf16[640,128]{1,0:T(8,128)(2,1)S(1)}, bf16[640,128]{1,0:T(8,128)(2,1)S(1)}, u32[]{:S(2)}, u32[]{:S(2)}) collective-permute-start(bf16[640,128]{1,0:T(8,128)(2,1)S(1)} %get-tuple-element.38), channel_id=1, source_target_pairs={{0,2},{1,3},{2,0},{3,1},{4,6},{5,7},{6,4},{7,5},{8,10},{9,11},{10,... | collective-permute-start | bytes 491528 | tf_op jit(solution)/shard_map/ppermute | solution.py:209
  13.6 14.4 %collective-permute-start.12 = (bf16[640,128]{1,0:T(8,128)(2,1)S(1)}, bf16[640,128]{1,0:T(8,128)(2,1)S(1)}, u32[]{:S(2)}, u32[]{:S(2)}) collective-permute-start(bf16[640,128]{1,0:T(8,128)(2,1)S(1)} %get-tuple-element.37), channel_id=1, source_target_pairs={{0,1},{1,2},{2,3},{3,0},{4,5},{5,6},{6,7},{7,4},{8,9},{9,10},{10,1... | collective-permute-start | bytes 491528 | tf_op jit(solution)/shard_map/ppermute | solution.py:209
  21.9 10.0 %collective-permute-start.2 = (bf16[640,128]{1,0:T(8,128)(2,1)S(1)}, bf16[640,128]{1,0:T(8,128)(2,1)S(1)}, u32[]{:S(2)}, u32[]{:S(2)}) collective-permute-start(bf16[640,128]{1,0:T(8,128)(2,1)S(1)} %get-tuple-element.28), channel_id=1, source_target_pairs={{0,12},{4,0},{8,4},{12,8},{1,13},{5,1},{9,5},{13,9},{2,14},{6,2},{... | collective-permute-start | bytes 491528 | tf_op jit(solution)/shard_map/ppermute | solution.py:209
  25.2 8.7 %collective-permute-start.1 = (bf16[640,128]{1,0:T(8,128)(2,1)S(1)}, bf16[640,128]{1,0:T(8,128)(2,1)S(1)}, u32[]{:S(2)}, u32[]{:S(2)}) collective-permute-start(bf16[640,128]{1,0:T(8,128)(2,1)S(1)} %get-tuple-element.28), channel_id=1, source_target_pairs={{0,8},{4,12},{8,0},{12,4},{1,9},{5,13},{9,1},{13,5},{2,10},{6,14},... | collective-permute-start | bytes 491528 | tf_op jit(solution)/shard_map/ppermute | solution.py:209
  27.0 11.9 %collective-permute-start = (bf16[640,128]{1,0:T(8,128)(2,1)S(1)}, bf16[640,128]{1,0:T(8,128)(2,1)S(1)}, u32[]{:S(2)}, u32[]{:S(2)}) collective-permute-start(bf16[640,128]{1,0:T(8,128)(2,1)S(1)} %get-tuple-element.28), channel_id=1, source_target_pairs={{0,4},{4,8},{8,12},{12,0},{1,5},{5,9},{9,13},{13,1},{2,6},{6,10},{... | collective-permute-start | bytes 491528 | tf_op jit(solution)/shard_map/ppermute | solution.py:209
  28.2 11.7 %collective-permute-start.17 = (bf16[640,128]{1,0:T(8,128)(2,1)S(1)}, bf16[640,128]{1,0:T(8,128)(2,1)S(1)}, u32[]{:S(2)}, u32[]{:S(2)}) collective-permute-start(bf16[640,128]{1,0:T(8,128)(2,1)S(1)} %fusion.13), channel_id=1, source_target_pairs={{0,12},{4,0},{8,4},{12,8},{1,13},{5,1},{9,5},{13,9},{2,14},{6,2},{... | collective-permute-start | bytes 491528 | tf_op jit(solution)/shard_map/ppermute | solution.py:209
  30.4 10.8 %collective-permute-start.16 = (bf16[640,128]{1,0:T(8,128)(2,1)S(1)}, bf16[640,128]{1,0:T(8,128)(2,1)S(1)}, u32[]{:S(2)}, u32[]{:S(2)}) collective-permute-start(bf16[640,128]{1,0:T(8,128)(2,1)S(1)} %fusion.13), channel_id=1, source_target_pairs={{0,8},{4,12},{8,0},{12,4},{1,9},{5,13},{9,1},{13,5},{2,10},{6,14},... | collective-permute-start | bytes 491528 | tf_op jit(solution)/shard_map/ppermute | solution.py:209
  31.9 10.2 %collective-permute-start.15 = (bf16[640,128]{1,0:T(8,128)(2,1)S(1)}, bf16[640,128]{1,0:T(8,128)(2,1)S(1)}, u32[]{:S(2)}, u32[]{:S(2)}) collective-permute-start(bf16[640,128]{1,0:T(8,128)(2,1)S(1)} %fusion.13), channel_id=1, source_target_pairs={{0,4},{4,8},{8,12},{12,0},{1,5},{5,9},{9,13},{13,1},{2,6},{6,10},{... | collective-permute-start | bytes 491528 | tf_op jit(solution)/shard_map/ppermute | solution.py:209
  55.0 11.1 %collective-permute-start.25 = (bf16[4,4,128,128]{3,2,1,0:T(8,128)(2,1)S(1)}, bf16[4,4,128,128]{3,2,1,0:T(8,128)(2,1)S(1)}, u32[]{:S(2)}, u32[]{:S(2)}) collective-permute-start(bf16[4,4,128,128]{3,2,1,0:T(8,128)(2,1)S(1)} %get-tuple-element.46), channel_id=1, source_target_pairs={{0,16},{16,0},{32,48},{48,32},{64,80},{80,64},{96,112},{112,96},{1... | collective-permute-start | bytes 1572872 | tf_op jit(solution)/shard_map/ppermute | solution.py:219
  55.7 16.4 %collective-permute-start.21 = (bf16[1152,128]{1,0:T(8,128)(2,1)S(1)}, bf16[1152,128]{1,0:T(8,128)(2,1)S(1)}, u32[]{:S(2)}, u32[]{:S(2)}) collective-permute-start(bf16[1152,128]{1,0:T(8,128)(2,1)S(1)} %get-tuple-element.54), channel_id=1, source_target_pairs={{0,96},{16,112},{32,0},{48,16},{64,32},{80,48},{96,64},{112,80},{1... | collective-permute-start | bytes 884744 | tf_op jit(solution)/shard_map/ppermute | solution.py:215
  58.5 13.6 %collective-permute-start.20 = (bf16[1152,128]{1,0:T(8,128)(2,1)S(1)}, bf16[1152,128]{1,0:T(8,128)(2,1)S(1)}, u32[]{:S(2)}, u32[]{:S(2)}) collective-permute-start(bf16[1152,128]{1,0:T(8,128)(2,1)S(1)} %get-tuple-element.55), channel_id=1, source_target_pairs={{0,64},{16,80},{32,96},{48,112},{64,0},{80,16},{96,32},{112,48},{1... | collective-permute-start | bytes 884744 | tf_op jit(solution)/shard_map/ppermute | solution.py:215
  59.3 17.5 %collective-permute-start.19 = (bf16[1152,128]{1,0:T(8,128)(2,1)S(1)}, bf16[1152,128]{1,0:T(8,128)(2,1)S(1)}, u32[]{:S(2)}, u32[]{:S(2)}) collective-permute-start(bf16[1152,128]{1,0:T(8,128)(2,1)S(1)} %get-tuple-element.53), channel_id=1, source_target_pairs={{0,32},{16,48},{32,64},{48,80},{64,96},{80,112},{96,0},{112,16},{1... | collective-permute-start | bytes 884744 | tf_op jit(solution)/shard_map/ppermute | solution.py:215
  60.2 73.7 %collective-permute-start.6 = (bf16[320,1792]{1,0:T(8,128)(2,1)}, bf16[320,1792]{1,0:T(8,128)(2,1)S(1)}, u32[]{:S(2)}, u32[]{:S(2)}) collective-permute-start(bf16[320,1792]{1,0:T(8,128)(2,1)} %get-tuple-element.31), channel_id=1, source_target_pairs={{0,4},{4,8},{8,12},{12,0},{1,5},{5,9},{9,13},{13,1},{2,6},{6,10},{... | collective-permute-start | bytes 3440648 | tf_op jit(solution)/shard_map/ppermute | solution.py:209
  66.2 11.1 %collective-permute-start.28 = (bf16[4,128,128]{2,1,0:T(8,128)(2,1)S(1)}, bf16[4,128,128]{2,1,0:T(8,128)(2,1)S(1)}, u32[]{:S(2)}, u32[]{:S(2)}) collective-permute-start(bf16[4,128,128]{2,1,0:T(8,128)(2,1)S(1)} %get-tuple-element.51), channel_id=1, source_target_pairs={{0,96},{16,112},{32,0},{48,16},{64,32},{80,48},{96,64},{112,80},{1... | collective-permute-start | bytes 393224 | tf_op jit(solution)/shard_map/ppermute | solution.py:215
  88.8 17.0 %collective-permute-start.31 = (bf16[2432,128]{1,0:T(8,128)(2,1)S(1)}, bf16[2432,128]{1,0:T(8,128)(2,1)S(1)}, u32[]{:S(2)}, u32[]{:S(2)}) collective-permute-start(bf16[2432,128]{1,0:T(8,128)(2,1)S(1)} %constant_dynamic-update-slice_fusion), channel_id=1, source_target_pairs={{0,96},{16,112},{32,0},{48,16},{64,32},{80,48},{96,64},{112,80},{1... | collective-permute-start | bytes 1867784 | tf_op jit(solution)/shard_map/ppermute | solution.py:215
  90.6 18.5 %collective-permute-start.30 = (bf16[2432,128]{1,0:T(8,128)(2,1)S(1)}, bf16[2432,128]{1,0:T(8,128)(2,1)S(1)}, u32[]{:S(2)}, u32[]{:S(2)}) collective-permute-start(bf16[2432,128]{1,0:T(8,128)(2,1)S(1)} %constant_dynamic-update-slice_fusion), channel_id=1, source_target_pairs={{0,64},{16,80},{32,96},{48,112},{64,0},{80,16},{96,32},{112,48},{1... | collective-permute-start | bytes 1867784 | tf_op jit(solution)/shard_map/ppermute | solution.py:215
  92.0 26.4 %collective-permute-start.29 = (bf16[2432,128]{1,0:T(8,128)(2,1)S(1)}, bf16[2432,128]{1,0:T(8,128)(2,1)S(1)}, u32[]{:S(2)}, u32[]{:S(2)}) collective-permute-start(bf16[2432,128]{1,0:T(8,128)(2,1)S(1)} %constant_dynamic-update-slice_fusion), channel_id=1, source_target_pairs={{0,32},{16,48},{32,64},{48,80},{64,96},{80,112},{96,0},{112,16},{1... | collective-permute-start | bytes 1867784 | tf_op jit(solution)/shard_map/ppermute | solution.py:215
  92.0 44.3 %collective-permute-start.10 = (bf16[320,1792]{1,0:T(8,128)(2,1)S(1)}, bf16[320,1792]{1,0:T(8,128)(2,1)S(1)}, u32[]{:S(2)}, u32[]{:S(2)}) collective-permute-start(bf16[320,1792]{1,0:T(8,128)(2,1)S(1)} %get-tuple-element.35), channel_id=1, source_target_pairs={{0,12},{4,0},{8,4},{12,8},{1,13},{5,1},{9,5},{13,9},{2,14},{6,2},{... | collective-permute-start | bytes 3440648 | tf_op jit(solution)/shard_map/ppermute | solution.py:209
  118.7 72.0 %collective-permute-start.32 = (bf16[4,2432,128]{2,1,0:T(8,128)(2,1)S(1)}, bf16[4,2432,128]{2,1,0:T(8,128)(2,1)S(1)}, u32[]{:S(2)}, u32[]{:S(2)}) collective-permute-start(bf16[4,2432,128]{2,1,0:T(8,128)(2,1)S(1)} %pad_maximum_fusion.refs_1_), channel_id=1, source_target_pairs={{0,16},{16,0},{32,48},{48,32},{64,80},{80,64},{96,112},{112,96},{1... | collective-permute-start | bytes 7471112 | tf_op jit(solution)/shard_map/ppermute | solution.py:219
  125.9 33.7 %collective-permute-start.8 = (bf16[320,1792]{1,0:T(8,128)(2,1)S(1)}, bf16[320,1792]{1,0:T(8,128)(2,1)S(1)}, u32[]{:S(2)}, u32[]{:S(2)}) collective-permute-start(bf16[320,1792]{1,0:T(8,128)(2,1)S(1)} %get-tuple-element.32), channel_id=1, source_target_pairs={{0,4},{4,8},{8,12},{12,0},{1,5},{5,9},{9,13},{13,1},{2,6},{6,10},{... | collective-permute-start | bytes 3440648 | tf_op jit(solution)/shard_map/ppermute | solution.py:209
  134.0 28.2 %collective-permute-start.9 = (bf16[320,1792]{1,0:T(8,128)(2,1)S(1)}, bf16[320,1792]{1,0:T(8,128)(2,1)S(1)}, u32[]{:S(2)}, u32[]{:S(2)}) collective-permute-start(bf16[320,1792]{1,0:T(8,128)(2,1)S(1)} %get-tuple-element.33), channel_id=1, source_target_pairs={{0,12},{4,0},{8,4},{12,8},{1,13},{5,1},{9,5},{13,9},{2,14},{6,2},{... | collective-permute-start | bytes 3440648 | tf_op jit(solution)/shard_map/ppermute | solution.py:209
  134.2 49.0 %collective-permute-start.7 = (bf16[320,1792]{1,0:T(8,128)(2,1)S(1)}, bf16[320,1792]{1,0:T(8,128)(2,1)S(1)}, u32[]{:S(2)}, u32[]{:S(2)}) collective-permute-start(bf16[320,1792]{1,0:T(8,128)(2,1)S(1)} %add_convert_fusion.1), channel_id=1, source_target_pairs={{0,4},{4,8},{8,12},{12,0},{1,5},{5,9},{9,13},{13,1},{2,6},{6,10},{... | collective-permute-start | bytes 3440648 | tf_op jit(solution)/shard_map/ppermute | solution.py:209
  136.6 48.9 %collective-permute-start.11 = (bf16[320,1792]{1,0:T(8,128)(2,1)S(1)}, bf16[320,1792]{1,0:T(8,128)(2,1)S(1)}, u32[]{:S(2)}, u32[]{:S(2)}) collective-permute-start(bf16[320,1792]{1,0:T(8,128)(2,1)S(1)} %add_convert_fusion), channel_id=1, source_target_pairs={{0,12},{4,0},{8,4},{12,8},{1,13},{5,1},{9,5},{13,9},{2,14},{6,2},{... | collective-permute-start | bytes 3440648 | tf_op jit(solution)/shard_map/ppermute | solution.py:209
  (23 other events, 292.7 us)

commit v3 on v0

v3 whole, which is shorter than its diff:
```python
import jax
import jax.numpy as jnp
from jax import lax
from jax.experimental import pallas as pl
from jax.experimental.pallas import tpu as pltpu
from jax.sharding import PartitionSpec as P

F32 = jnp.float32
BF16 = jnp.bfloat16
SIDE = 128
SMEM = pl.BlockSpec(memory_space=pltpu.SMEM)
VMEM = pl.BlockSpec(memory_space=pltpu.VMEM)
HBM = pl.BlockSpec(memory_space=pl.ANY)


def lanes(block):
    return pl.ds(pl.multiple_of(block * SIDE, SIDE), SIDE)


def sublanes(block, size):
    return pl.ds(pl.multiple_of(block * size, size), size)


def shape(dims, dtype):
    return jax.ShapeDtypeStruct(dims, dtype)


def call(kernel, outs, smem, vmem, scratch=(), after=None, flops=0, mib=40):
    tokens = () if after is None else (after,)
    n_in, n_out = len(smem) + len(vmem), len(outs)

    def body(*refs):
        ins, rest = refs[:n_in], refs[n_in + len(tokens) :]
        rest[n_out][0] = 0
        kernel(*ins, *rest[:n_out], *rest[n_out + 1 :])

    nbytes = sum(a.size * a.dtype.itemsize for a in (*vmem, *outs))
    return pl.pallas_call(
        body,
        out_shape=(*outs, shape((1,), jnp.int32)),
        in_specs=[SMEM] * len(smem) + [VMEM] * len(vmem) + [SMEM] * len(tokens),
        out_specs=(VMEM,) * n_out + (SMEM,),
        scratch_shapes=list(scratch),
        cost_estimate=pl.CostEstimate(
            flops=0, bytes_accessed=0, transcendentals=0
        ),
        compiler_params=pltpu.CompilerParams(vmem_limit_bytes=mib << 20),
    )(*smem, *vmem, *tokens)


class Place:
    def __init__(self, n_f, n_t, n_d):
        self.n_f, self.n_t, self.n_d, self.chips = n_f, n_t, n_d, n_d // 2

    f = property(lambda self: lax.axis_index("fsdp"))
    t = property(lambda self: lax.axis_index("tensor"))
    chip = property(lambda self: lax.axis_index("dp") // 2)
    core = property(lambda self: lax.rem(lax.axis_index("dp"), 2))

    def live(self, counts):
        return counts[self.f * self.n_t + self.t]


def far_kernel(place, q_blocks, counts, rows, cols, tok, left, vals, top, bottom, part, low, acc):
    rank = jnp.dot(tok[...], left[:, lanes(place.t)], preferred_element_type=F32)
    part[...] = rank
    for k in range(place.n_f):
        low[k] = rank.astype(BF16)
    quarter = lax.rem(place.f + place.n_f // 2, place.n_f)
    acc[...] = jnp.zeros_like(acc)

    def body(s, carry):
        col = cols[s]

        @pl.when(col // q_blocks == quarter)
        def _():
            acc[:, lanes(col - quarter * q_blocks)] += jnp.dot(
                tok[:, lanes(rows[s])], vals[s], preferred_element_type=F32
            )

        return carry

    lax.fori_loop(0, place.live(counts), body, 0)
    half = top.shape[0]
    top[...] = acc[:half].astype(BF16)
    bottom[...] = acc[half:].astype(BF16)


def near_kernel(place, q_blocks, counts, rows, cols, tok, vals, p1t, p1b, p3t, p3b, p0, acc):
    acc[...] = jnp.zeros_like(acc)
    p0[...] = jnp.zeros_like(p0)
    n_f, f = place.n_f, place.f

    def body(s, carry):
        col = cols[s]
        q = col // q_blocks
        k = lax.rem(q - f + n_f, n_f)
        here = lanes(col - q * q_blocks)

        @pl.when(k != n_f // 2)
        def _():
            prod = jnp.dot(tok[:, lanes(rows[s])], vals[s], preferred_element_type=F32)

            @pl.when(k == 0)
            def _():
                p0[:, here] += prod

            @pl.when(k != 0)
            def _():
                acc[k // 2, :, here] += prod

        return carry

    lax.fori_loop(0, place.live(counts), body, 0)
    half = p1t.shape[0]
    p1t[...] = acc[0, :half]
    p1b[...] = acc[0, half:].astype(BF16)
    p3t[...] = acc[1, :half].astype(BF16)
    p3b[...] = acc[1, half:]


def back_kernel(place, cot, right, own, parts, full):
    quarter = right.shape[1]
    here = pl.ds(pl.multiple_of(place.f * quarter, SIDE), quarter)
    full[...] = lax.dot_general(
        cot[:, here], right[...], (((1,), (1,)), ((), ())), preferred_element_type=F32
    )
    own[...] = full[:, lanes(place.t)]
    for k in range(place.n_t):
        parts[k] = full[:, k * SIDE : (k + 1) * SIDE].astype(BF16)


def blocks_kernel(place, counts, rows, cols, tok, cot, mine, theirs):
    mine[...] = jnp.zeros_like(mine)
    theirs[...] = jnp.zeros_like(theirs)
    per = mine.shape[1] // SIDE
    core = place.core

    def body(s, carry):
        grad = lax.dot_general(
            tok[:, lanes(rows[s])],
            cot[:, lanes(cols[s])],
            (((0,), (0,)), ((), ())),
            preferred_element_type=F32,
        )
        owner = s // per
        j = owner // 2
        at = sublanes(lax.rem(s, per), SIDE)
        keep = lax.rem(owner, 2) == core

        @pl.when(keep)
        def _():
            mine[j, at] = grad

        @pl.when(jnp.logical_not(keep))
        def _():
            theirs[j, at] = grad.astype(BF16)

        return carry

    lax.fori_loop(0, place.live(counts), body, 0)


def factors_kernel(place, tok, cot, ranks, back_part, back_in, mine, theirs, left, right):
    quarter = right.shape[1]
    here = pl.ds(pl.multiple_of(place.f * quarter, SIDE), quarter)
    back = back_part[...]
    for k in range(1, place.n_f):
        back = back + back_in[lax.rem(place.f + k, place.n_f)].astype(F32)
    left[...] = lax.dot_general(
        back.astype(BF16), tok[...], (((0,), (0,)), ((), ())), preferred_element_type=F32
    ).T
    for k in range(place.n_t):
        right[k * SIDE : (k + 1) * SIDE, :] = lax.dot_general(
            ranks[k], cot[:, here], (((0,), (0,)), ((), ())), preferred_element_type=F32
        )
    n_l = left.shape[0] // place.n_d
    n_r = right.shape[0] // place.n_d
    for chip in range(place.chips):
        for core, out in ((place.core, mine), (1 - place.core, theirs)):
            at = chip * 2 + core
            out[chip, :n_l] = left[sublanes(at, n_l), :].astype(out.dtype)
            for p in range(quarter // SIDE):
                out[chip, n_l + p * n_r : n_l + (p + 1) * n_r] = right[
                    sublanes(at, n_r), p * SIDE : (p + 1) * SIDE
                ].astype(out.dtype)


def cores_kernel(place, mine, got, own, parts):
    for k in range(place.chips):
        parts[k] = (mine[k] + got[k].astype(F32)).astype(BF16)
    own[...] = mine[place.chip] + got[place.chip].astype(F32)


def total_kernel(place, axis, own, got, *outs):
    n = got.shape[0]
    me = getattr(place, axis)
    total = own[...]
    for k in range(1, n):
        total = total + got[lax.rem(me + k, n)].astype(F32)
    row = 0
    for out in outs:
        if len(out.shape) == 2:
            out[...] = total.astype(out.dtype)
            continue
        for k in range(out.shape[0]):
            out[k] = total[row : row + out.shape[1]].astype(out.dtype)
        row += out.shape[1]


def copies_kernel(parts, out):
    rows = parts.shape[1]
    for k in range(out.shape[0]):
        for p in range(parts.shape[0]):
            out[k, p * rows : (p + 1) * rows] = parts[p]


def add_kernel(a, x, b, y, a_out, b_out):
    a_out[...] = (a[...] + x[...].astype(F32)).astype(BF16)
    b_out[...] = (b[...] + y[...].astype(F32)).astype(BF16)


def low_kernel(place, ranks, right, p0, bottom, top, out):
    half = top.shape[0]
    acc = p0[...]
    for k in range(place.n_t):
        acc += jnp.dot(ranks[k], right[k * SIDE : (k + 1) * SIDE, :], preferred_element_type=F32)
    out[:half] = acc[:half] + top[...].astype(F32)
    out[half:] = acc[half:] + bottom[...].astype(F32)


def finish_kernel(pre, top, bottom, out):
    half = top.shape[0]
    out[:half] = (pre[:half] + top[...].astype(F32)).astype(BF16)
    out[half:] = (pre[half:] + bottom[...].astype(F32)).astype(BF16)


def spread_kernel(place, ours_l, theirs_l, ours_r, theirs_r, ours_b, theirs_b, left, right, blocks):
    n_l = left.shape[0] // place.n_d
    n_r = right.shape[0] // place.n_d
    n_b = blocks.shape[0] // place.n_d
    for core, src_l, src_r, src_b in (
        (place.core, ours_l, ours_r, ours_b),
        (1 - place.core, theirs_l, theirs_r, theirs_b),
    ):
        for chip in range(place.chips):
            at = chip * 2 + core
            for k in range(place.n_t):
                left[sublanes(at, n_l), k * SIDE : (k + 1) * SIDE] = src_l[
                    chip, k * n_l : (k + 1) * n_l
                ]
            for p in range(right.shape[1] // SIDE):
                right[sublanes(at, n_r), p * SIDE : (p + 1) * SIDE] = src_r[
                    chip, p * n_r : (p + 1) * n_r
                ]
            blocks[sublanes(at, n_b)] = src_b[chip]


def shift(x, axis, n, k):
    return lax.ppermute(x, axis, [(i, (i + k) % n) for i in range(n)])


def core_swap(x, n_data):
    return lax.ppermute(x, "dp", [(i, i ^ 1) for i in range(n_data)])


def exchange(x, axis):
    return lax.all_to_all(x, axis, 0, 0, tiled=True)


def chip_exchange(x, n_data):
    groups = [[c + 2 * a for a in range(n_data // 2)] for c in range(2)]
    return lax.all_to_all(x, "dp", 0, 0, axis_index_groups=groups, tiled=True)


def per_device(
    tokens, cotangent, left_factor, right_factor, block_values, block_rows, block_cols, block_counts
):
    n_f = lax.axis_size("fsdp")
    n_t = lax.axis_size("tensor")
    n_d = lax.axis_size("dp")
    place = Place(n_f, n_t, n_d)
    chips = n_d // 2
    maxb = block_values.shape[0]
    tok_rows, features = tokens.shape
    right = right_factor.reshape(right_factor.shape[0], -1)
    rank_size, quarter = right.shape
    q_blocks = quarter // SIDE
    r_part = rank_size // n_t
    half = tok_rows // 2
    lists = (block_counts, block_rows, block_cols)
    block_flops = 2 * tok_rows * SIDE * SIDE * maxb

    def bind(kernel, *args):
        return lambda *refs: kernel(place, *args, *refs)

    half_low = shape((half, quarter), BF16)
    half_wide = shape((half, quarter), F32)
    part = shape((tok_rows, r_part), F32)
    parts_f = shape((n_f, tok_rows, r_part), BF16)
    parts_t = shape((n_t, tok_rows, r_part), BF16)

    p2t, p2b, rank_part, rank_low, step = call(
        bind(far_kernel, q_blocks),
        (half_low, half_low, part, parts_f),
        lists,
        (tokens, left_factor, block_values),
        [pltpu.VMEM((tok_rows, quarter), F32)],
        flops=block_flops,
    )
    rank_in = exchange(rank_low, "fsdp")
    in_t = shift(p2t, "fsdp", n_f, 1)
    in_b = shift(p2b, "fsdp", n_f, -1)

    back_part, back_out, step = call(
        bind(back_kernel),
        (part, parts_t),
        (),
        (cotangent, right),
        [pltpu.VMEM((tok_rows, rank_size), F32)],
        after=step,
        flops=2 * tok_rows * quarter * rank_size,
    )
    back_in = exchange(back_out, "tensor")

    p1t, p1b, p3t, p3b, p0, step = call(
        bind(near_kernel, q_blocks),
        (half_wide, half_low, half_low, half_wide, shape((tok_rows, quarter), F32)),
        lists,
        (tokens, block_values),
        [pltpu.VMEM((2, tok_rows, quarter), F32)],
        after=step,
        flops=block_flops,
    )
    ab = shift(p1b, "fsdp", n_f, 1)
    bt = shift(p3t, "fsdp", n_f, -1)

    rank_out, step = call(
        bind(total_kernel, "f"), (parts_t,), (), (rank_part, rank_in), after=step
    )
    ranks = exchange(rank_out, "tensor")
    back_part, back_out, step = call(
        bind(total_kernel, "t"), (part, parts_f), (), (back_part, back_in), after=step
    )
    back_in = exchange(back_out, "fsdp")

    n_b = maxb // n_d * SIDE
    blocks_mine, blocks_theirs, step = call(
        bind(blocks_kernel),
        (shape((chips, n_b, SIDE), F32), shape((chips, n_b, SIDE), BF16)),
        lists,
        (tokens, cotangent),
        after=step,
        flops=block_flops,
    )
    blocks_got = core_swap(blocks_theirs, n_d)

    n_l = features // n_d
    n_r = rank_size // n_d
    n_lr = n_l + q_blocks * n_r
    mine, theirs, step = call(
        bind(factors_kernel),
        (shape((chips, n_lr, SIDE), F32), shape((chips, n_lr, SIDE), BF16)),
        (),
        (tokens, cotangent, ranks, back_part, back_in),
        [pltpu.VMEM((features, r_part), F32), pltpu.VMEM((rank_size, quarter), F32)],
        after=step,
        flops=2 * tok_rows * (quarter * rank_size + features * r_part),
    )
    got = core_swap(theirs, n_d)

    block_own, block_out, step = call(
        bind(cores_kernel),
        (shape((n_b, SIDE), F32), shape((chips, n_b, SIDE), BF16)),
        (),
        (blocks_mine, blocks_got),
        after=step,
    )
    block_in = chip_exchange(block_out, n_d)
    own, out, step = call(
        bind(cores_kernel),
        (shape((n_lr, SIDE), F32), shape((chips, n_lr, SIDE), BF16)),
        (),
        (mine, got),
        after=step,
    )
    lr_in = chip_exchange(out, n_d)
    at_out, bb_out, step = call(
        add_kernel, (half_low, half_low), (), (p1t, in_t, p3b, in_b), after=step
    )
    at = shift(at_out, "fsdp", n_f, 1)
    bb = shift(bb_out, "fsdp", n_f, -1)
    block_copies, step = call(
        bind(total_kernel, "chip"),
        (shape((chips, n_b, SIDE), BF16),),
        (),
        (block_own, block_in),
        after=step,
    )
    blocks_ours = chip_exchange(block_copies, n_d)
    left_copies, right_copies, step = call(
        bind(total_kernel, "chip"),
        (shape((n_t, n_l, SIDE), BF16), shape((chips, q_blocks * n_r, SIDE), BF16)),
        (),
        (own, lr_in),
        after=step,
    )
    right_ours = chip_exchange(right_copies, n_d)
    lefts = exchange(left_copies, "tensor")
    left_copies, step = call(
        copies_kernel, (shape((chips, n_t * n_l, SIDE), BF16),), (), (lefts,), after=step
    )
    left_ours = chip_exchange(left_copies, n_d)
    pre, step = call(
        bind(low_kernel),
        (shape((tok_rows, quarter), F32),),
        (),
        (ranks, right, p0, ab, bt),
        after=step,
        flops=2 * tok_rows * quarter * rank_size,
    )
    blocks_theirs = core_swap(blocks_ours, n_d)
    right_theirs = core_swap(right_ours, n_d)
    left_theirs = core_swap(left_ours, n_d)
    mixed, step = call(
        finish_kernel, (shape((tok_rows, quarter), BF16),), (), (pre, at, bb), after=step
    )
    out_left, out_right, out_blocks, _ = call(
        bind(spread_kernel),
        (
            shape((features, rank_size), BF16),
            shape((rank_size, quarter), BF16),
            shape((maxb * SIDE, SIDE), BF16),
        ),
        (),
        (left_ours, left_theirs, right_ours, right_theirs, blocks_ours, blocks_theirs),
    )
    return (
        mixed.reshape(tok_rows, 1, quarter),
        out_left,
        out_right.reshape(right_factor.shape),
        out_blocks.reshape(maxb, SIDE, SIDE),
    )


def solution(mesh):
    return jax.shard_map(
        per_device,
        mesh=mesh,
        in_specs=(
            P("dp", "fsdp"),
            P("dp", "tensor"),
            P("fsdp", None),
            P(None, "tensor", "fsdp"),
            P(("fsdp", "tensor"), None, None),
            P(("fsdp", "tensor")),
            P(("fsdp", "tensor")),
            P(),
        ),
        out_specs=(
            P("dp", "tensor", "fsdp"),
            P("fsdp", None),
            P(None, "tensor", "fsdp"),
            P(("fsdp", "tensor"), None, None),
        ),
        check_vma=False,
    )
```

time: 720 us -> 230 us (0.32)
  blocking collectives: 402 us -> 25.9 us
  other arithmetic: 115 us -> 0 us
  local copies, waits for them, and re-layouts: 111 us -> 42.5 us
  matrix products: 57.7 us -> 0 us
  starting transfers between devices: 15.2 us -> 69.9 us
  Pallas kernels: 0 us -> 53.3 us
  waiting for transfers between devices: 0.72 us -> 33.7 us
  between operations: 16.2 us -> 1.16 us
    psum x3 -> x0, blocking collectives: 316 us -> none  [the longest x1 121 us: per_device(): lax.psum((grad_left, grad_right, grad_blocks), 'dp')]
    scatter-add x1 -> x0, other arithmetic: 80.4 us -> none  [per_device(): share = start_acc.at[target].add(prods)]
    dot_general x7 -> x0, matrix products: 57.7 us -> none  [the longest x1 25.4 us: per_device(): jnp.einsum('tmb,mbc->mtc', panels, values, preferred_element_type=jnp.flo...]
    all_to_all x1 -> x2, blocking collectives: 81 us -> 25.9 us  [exchange(): return lax.all_to_all(x, axis, 0, 0, tiled=True)]
    pallas_call x0 -> x16, Pallas kernels: none -> 53.3 us  [call(): pl.pallas_call(body, out_shape=(*outs, shape((1,), jnp.int32)), in_specs=...]
    gather x7 -> x0, local copies, waits for them, and re-layouts: 41 us -> none  [the longest x1 13.7 us: per_device(): panels = jnp.take(all_rows3, owner_f * row_blocks + rws, axis=1)]
    reshape x5 -> x0, local copies, waits for them, and re-layouts: 37.8 us -> none  [the longest x1 14.5 us: per_device(): all_rows3 = all_rows.reshape(tok_rows, row_blocks * n_fsdp, side)]
    ppermute x0 -> x11, starting transfers between devices: none -> 30.8 us  [the longest x5 20.7 us: core_swap(): return lax.ppermute(x, 'dp', [(i, i ^ 1) for i in range(n_data)])]
  transfers between devices with their start and end apart: 4 -> 19, of which waited for: 0 -> 8; matrix products, arithmetic and copies ran while one was open for 21% -> 0% of each run, Pallas kernels for 0% -> 14%
where the time goes in v3:
time: 230 us; the launch traced here: 226 us
  starting transfers between devices  69.9 us (30%)
  Pallas kernels  53.3 us (23%)
  local copies, waits for them, and re-layouts  42.5 us (18%)
  waiting for transfers between devices  33.7 us (15%)
  blocking collectives  25.9 us (11%)
    pallas_call x16, Pallas kernels, call(): pl.pallas_call(body, out_shape=(*outs, shape((1,), jnp.int32)), in_specs=...  53.3 us
    unnamed x92, local copies, waits for them, and re-layouts  42.5 us
    all_to_all x2, blocking collectives, exchange(): return lax.all_to_all(x, axis, 0, 0, tiled=True)  25.9 us
    ppermute x5, starting transfers between devices, core_swap(): return lax.ppermute(x, 'dp', [(i, i ^ 1) for i in range(n_data)])  20.7 us
    all_to_all x5, starting transfers between devices, chip_exchange(): return lax.all_to_all(x, 'dp', 0, 0, axis_index_groups=groups, tiled=True)  20.6 us
    all_to_all x3, starting transfers between devices, exchange(): return lax.all_to_all(x, axis, 0, 0, tiled=True)  18.5 us
    ppermute x6, waiting for transfers between devices, shift(): return lax.ppermute(x, axis, [(i, (i + k) % n) for i in range(n)])  17.9 us
    all_to_all x5, waiting for transfers between devices, chip_exchange(): return lax.all_to_all(x, 'dp', 0, 0, axis_index_groups=groups, tiled=True)  11.6 us
  transfers between devices with their start and end apart: 19, of which 8 were waited for; matrix products, arithmetic and copies ran while one was open for 0% of the time, Pallas kernels for 14%

profile of v3, /device:TPU:1, one launch (start us, length us, event | category | flops | bytes accessed | tf_op | source)
XLA Modules:
  0.0 226.5 jit_solution(6711018510314320350)
XLA Ops:
  12.6 6.2 %all-to-all-start = ((bf16[4,640,128]{2,1,0:T(8,128)(2,1)}), bf16[4,640,128]{2,1,0:T(8,128)(2,1)}, u32[]{:S(2)}, u32[]{:S(2)}) async-start(bf16[4,640,128]{2,1,0:T(8,128)(2,1)} %get-tuple-element.52), calls=%async_computation | async-start | bytes 1310720 | tf_op jit(solution)/shard_map/all_to_all | solution.py:268
  18.7 3.6 %copy-done = bf16[640,7168]{1,0:T(8,128)(2,1)S(1)} copy-done((bf16[640,7168]{1,0:T(8,128)(2,1)S(1)}, bf16[640,7168]{1,0:T(8,128)(2,1)}, u32[]{:S(2)}) %copy-start) | copy-done | bytes 9175064
  28.8 5.4 %all-to-all-start.2 = ((bf16[4,640,128]{2,1,0:T(8,128)(2,1)}), bf16[4,640,128]{2,1,0:T(8,128)(2,1)}, u32[]{:S(2)}, u32[]{:S(2)}) async-start(bf16[4,640,128]{2,1,0:T(8,128)(2,1)} %get-tuple-element.61), calls=%async_computation.2 | async-start | bytes 1310720 | tf_op jit(solution)/shard_map/all_to_all | solution.py:268
  35.5 6.4 %shard_map.113 = (f32[320,1792]{1,0:T(8,128)S(1)}, bf16[320,1792]{1,0:T(8,128)(2,1)}, bf16[320,1792]{1,0:T(8,128)(2,1)}, f32[320,1792]{1,0:T(8,128)S(1)}, f32[640,1792]{1,0:T(8,128)}, /*index=5*/s32[1]{0:T(128)}) custom-call(s32[16]{0:T(128)S(1)} %copy-done.35, s32[32]{0:T(128)S(1)} %copy-done.37, s32[32]{0:T(128)S(1)} %copy-done.39, ...), custom_call_target="tpu_custom_call" | custom-call | tf_op jit(solution)/shard_map/pallas_call | solution.py:38
  51.1 13.0 %all_to_all.50.refs_4_ = bf16[4,640,128]{2,1,0:T(8,128)(2,1)} all-to-all(bf16[4,640,128]{2,1,0:T(8,128)(2,1)S(1)} %get-tuple-element.64), channel_id=1, replica_groups=mesh['dp'=8,'fsdp'=4,'tensor'=4] {'fsdp'}, dimensions={0} | all-to-all | bytes 1310720 | tf_op jit(solution)/shard_map/all_to_all | solution.py:268
  64.1 6.9 %all-to-all-start.1 = ((bf16[4,640,128]{2,1,0:T(8,128)(2,1)}), bf16[4,640,128]{2,1,0:T(8,128)(2,1)S(1)}, u32[]{:S(2)}, u32[]{:S(2)}) async-start(bf16[4,640,128]{2,1,0:T(8,128)(2,1)} %copy-done.21), calls=%async_computation.1 | async-start | bytes 1310720 | tf_op jit(solution)/shard_map/all_to_all | solution.py:268
  71.0 3.6 %copy-done.1 = bf16[640,7168]{1,0:T(8,128)(2,1)S(1)} copy-done((bf16[640,7168]{1,0:T(8,128)(2,1)S(1)}, bf16[640,7168]{1,0:T(8,128)(2,1)}, u32[]{:S(2)}) %copy-start.1) | copy-done | bytes 9175064
  74.6 3.3 %shard_map.116 = (f32[4,512,128]{2,1,0:T(8,128)S(1)}, bf16[4,512,128]{2,1,0:T(8,128)(2,1)S(1)}, s32[1]{0:T(128)}) custom-call(s32[16]{0:T(128)S(1)} %copy-done.35, s32[32]{0:T(128)S(1)} %copy-done.37, s32[32]{0:T(128)S(1)} %copy-done.39, bf16[640,2048]{1,0:T(8,128)(2,1)S(1)} %copy-done.3, bf16[640,7168]{1,0:T(8,128)(2,1)S(1)} %copy-done.1, ...), custom_call_target="tpu_custom_call" | custom-call | tf_op jit(solution)/shard_map/pallas_call | solution.py:38
  81.7 8.7 %shard_map.117 = (f32[4,1152,128]{2,1,0:T(8,128)S(1)}, bf16[4,1152,128]{2,1,0:T(8,128)(2,1)}, s32[1]{0:T(128)}) custom-call(bf16[640,2048]{1,0:T(8,128)(2,1)S(1)} %copy-done.3, bf16[640,7168]{1,0:T(8,128)(2,1)} %refs_1_.7, bf16[4,640,128]{2,1,0:T(8,128)(2,1)S(1)} %all-to-all-done.1.refs_2_.refs_0_, f32[640,128]{1,0:T(8,128)S(1)} %copy-done.31, ...), custom_call_target="tpu_custom_call" | custom-call | tf_op jit(solution)/shard_map/pallas_call | solution.py:38
  101.0 4.0 %all-to-all-start.5 = ((bf16[4,512,128]{2,1,0:T(8,128)(2,1)}), bf16[4,512,128]{2,1,0:T(8,128)(2,1)S(1)}, u32[]{:S(2)}, u32[]{:S(2)}) async-start(bf16[4,512,128]{2,1,0:T(8,128)(2,1)} %copy-done.25), calls=%async_computation.5 | async-start | bytes 1048576 | tf_op jit(solution)/shard_map/all_to_all | solution.py:273
  105.0 4.7 %collective-permute-start.4 = (bf16[320,1792]{1,0:T(8,128)(2,1)}, bf16[320,1792]{1,0:T(8,128)(2,1)}, u32[]{:S(2)}, u32[]{:S(2)}) collective-permute-start(bf16[320,1792]{1,0:T(8,128)(2,1)} %copy-done.41), channel_id=1, source_target_pairs={{0,4},{4,8},{8,12},{12,0},{1,5},{5,9},{9,13},{13,1},{2,6},{6,10},{... | collective-permute-start | bytes 3440648 | tf_op jit(solution)/shard_map/ppermute | solution.py:260
  114.2 4.0 %all-to-all-start.4 = ((bf16[4,1152,128]{2,1,0:T(8,128)(2,1)}), bf16[4,1152,128]{2,1,0:T(8,128)(2,1)S(1)}, u32[]{:S(2)}, u32[]{:S(2)}) async-start(bf16[4,1152,128]{2,1,0:T(8,128)(2,1)} %copy-done.17), calls=%async_computation.4 | async-start | bytes 2359296 | tf_op jit(solution)/shard_map/all_to_all | solution.py:273
  118.2 16.3 %collective-permute-done.4.refs_1_ = bf16[320,1792]{1,0:T(8,128)(2,1)} collective-permute-done((bf16[320,1792]{1,0:T(8,128)(2,1)}, bf16[320,1792]{1,0:T(8,128)(2,1)}, u32[]{:S(2)}, u32[]{:S(2)}) %collective-permute-start.4) | collective-permute-done | bytes 1146912 | tf_op jit(solution)/shard_map/ppermute | solution.py:260
  148.3 12.9 %all_to_all.51.refs_0_ = bf16[4,256,128]{2,1,0:T(8,128)(2,1)S(1)} all-to-all(bf16[4,256,128]{2,1,0:T(8,128)(2,1)S(1)} %get-tuple-element.84), channel_id=1, replica_groups=mesh['dp'=8,'fsdp'=4,'tensor'=4] {'tensor'}, dimensions={0} | all-to-all | bytes 524288 | tf_op jit(solution)/shard_map/all_to_all | solution.py:268
  163.0 3.9 %all-to-all-start.7 = ((bf16[4,1024,128]{2,1,0:T(8,128)(2,1)}), bf16[4,1024,128]{2,1,0:T(8,128)(2,1)S(1)}, u32[]{:S(2)}, u32[]{:S(2)}) async-start(bf16[4,1024,128]{2,1,0:T(8,128)(2,1)} %get-tuple-element.92), calls=%async_computation.7 | async-start | bytes 2097152 | tf_op jit(solution)/shard_map/all_to_all | solution.py:273
  169.6 8.9 %all-to-all-done.7.refs_0_ = bf16[4,1024,128]{2,1,0:T(8,128)(2,1)S(1)} async-done(((bf16[4,1024,128]{2,1,0:T(8,128)(2,1)}), bf16[4,1024,128]{2,1,0:T(8,128)(2,1)S(1)}, u32[]{:S(2)}, u32[]{:S(2)}) %all-to-all-start.7) | async-done | bytes 1048608 | tf_op jit(solution)/shard_map/all_to_all | solution.py:273
  178.4 4.5 %all-to-all-start.8 = ((bf16[4,896,128]{2,1,0:T(8,128)(2,1)}), bf16[4,896,128]{2,1,0:T(8,128)(2,1)}, u32[]{:S(2)}, u32[]{:S(2)}) async-start(bf16[4,896,128]{2,1,0:T(8,128)(2,1)} %copy-done.20), calls=%async_computation.8 | async-start | bytes 1835008 | tf_op jit(solution)/shard_map/all_to_all | solution.py:273
  185.7 5.1 %collective-permute-start.8 = (bf16[4,1024,128]{2,1,0:T(8,128)(2,1)S(1)}, bf16[4,1024,128]{2,1,0:T(8,128)(2,1)}, u32[]{:S(2)}, u32[]{:S(2)}) collective-permute-start(bf16[4,1024,128]{2,1,0:T(8,128)(2,1)S(1)} %all-to-all-done.7.refs_0_), channel_id=1, source_target_pairs={{0,16},{16,0},{32,48},{48,32},{64,80},{80,64},{96,112},{112,96},{1... | collective-permute-start | bytes 3145736 | tf_op jit(solution)/shard_map/ppermute | solution.py:264
  192.1 4.1 %all-to-all-start.9 = ((bf16[4,512,128]{2,1,0:T(8,128)(2,1)}), bf16[4,512,128]{2,1,0:T(8,128)(2,1)}, u32[]{:S(2)}, u32[]{:S(2)}) async-start(bf16[4,512,128]{2,1,0:T(8,128)(2,1)} %copy-done.24), calls=%async_computation.9 | async-start | bytes 1048576 | tf_op jit(solution)/shard_map/all_to_all | solution.py:273
  196.2 5.7 %collective-permute-start.9 = (bf16[4,896,128]{2,1,0:T(8,128)(2,1)}, bf16[4,896,128]{2,1,0:T(8,128)(2,1)}, u32[]{:S(2)}, u32[]{:S(2)}) collective-permute-start(bf16[4,896,128]{2,1,0:T(8,128)(2,1)} %all-to-all-done.8.refs_2_), channel_id=1, source_target_pairs={{0,16},{16,0},{32,48},{48,32},{64,80},{80,64},{96,112},{112,96},{1... | collective-permute-start | bytes 2752520 | tf_op jit(solution)/shard_map/ppermute | solution.py:264
  203.2 6.8 %collective-permute-start.10 = (bf16[4,512,128]{2,1,0:T(8,128)(2,1)}, bf16[4,512,128]{2,1,0:T(8,128)(2,1)S(1)}, u32[]{:S(2)}, u32[]{:S(2)}) collective-permute-start(bf16[4,512,128]{2,1,0:T(8,128)(2,1)} %all-to-all-done.9.refs_4_), channel_id=1, source_target_pairs={{0,16},{16,0},{32,48},{48,32},{64,80},{80,64},{96,112},{112,96},{1... | collective-permute-start | bytes 1572872 | tf_op jit(solution)/shard_map/ppermute | solution.py:264
  212.3 5.0 %shard_map.124 = (f32[640,1792]{1,0:T(8,128)S(1)}, s32[1]{0:T(128)}) custom-call(bf16[4,640,128]{2,1,0:T(8,128)(2,1)S(1)} %all-to-all-done.1.refs_2_.refs_0_, bf16[512,1792]{1,0:T(8,128)(2,1)S(1)} %bitcast.5, f32[640,1792]{1,0:T(8,128)S(1)} %copy-done.6, bf16[320,1792]{1,0:T(8,128)(2,1)} %collective-permute-done.refs_3_, ...), custom_call_target="tpu_custom_call" | custom-call | tf_op jit(solution)/shard_map/pallas_call | solution.py:38
  217.3 4.0 %shard_map.125 = (bf16[640,1792]{1,0:T(8,128)(2,1)}, s32[1]{0:T(128)}) custom-call(f32[640,1792]{1,0:T(8,128)S(1)} %get-tuple-element.87.refs_0_, bf16[320,1792]{1,0:T(8,128)(2,1)} %collective-permute-done.6.refs_1_, bf16[320,1792]{1,0:T(8,128)(2,1)} %collective-permute-done.7.refs_2_, s32[1]{0:T(128)} %get-tuple-element.90.refs_3_), custom_call_target="tpu_custom_call" | custom-call | tf_op jit(solution)/shard_map/pallas_call | solution.py:38
  221.4 4.9 %shard_map.126 = (bf16[2048,512]{1,0:T(8,128)(2,1)}, bf16[512,1792]{1,0:T(8,128)(2,1)}, bf16[4096,128]{1,0:T(8,128)(2,1)}, s32[1]{0:T(128)}) custom-call(bf16[4,1024,128]{2,1,0:T(8,128)(2,1)S(1)} %all-to-all-done.7.refs_0_, bf16[4,1024,128]{2,1,0:T(8,128)(2,1)} %collective-permute-done.8.refs_1_, bf16[4,896,128]{2,1,0:T(8,128)(2,1)} %all-to-all-done.8.refs_2_, ...), custom_call_target="tpu_custom_call" | custom-call | tf_op jit(solution)/shard_map/pallas_call | solution.py:38
  (124 shorter events, 73.5 us)
Async XLA Ops:
  12.6 16.2 %all-to-all-start = ((bf16[4,640,128]{2,1,0:T(8,128)(2,1)}), bf16[4,640,128]{2,1,0:T(8,128)(2,1)}, u32[]{:S(2)}, u32[]{:S(2)}) async-start(bf16[4,640,128]{2,1,0:T(8,128)(2,1)} %get-tuple-element.52), calls=%async_computation | async-start | bytes 1310720 | tf_op jit(solution)/shard_map/all_to_all | solution.py:268
  28.8 19.0 %all-to-all-start.2 = ((bf16[4,640,128]{2,1,0:T(8,128)(2,1)}), bf16[4,640,128]{2,1,0:T(8,128)(2,1)}, u32[]{:S(2)}, u32[]{:S(2)}) async-start(bf16[4,640,128]{2,1,0:T(8,128)(2,1)} %get-tuple-element.61), calls=%async_computation.2 | async-start | bytes 1310720 | tf_op jit(solution)/shard_map/all_to_all | solution.py:268
  51.1 13.1 %copy-start.30 = (f32[640,128]{1,0:T(8,128)}, f32[640,128]{1,0:T(8,128)S(1)}, u32[]{:S(2)}) copy-start(f32[640,128]{1,0:T(8,128)S(1)} %get-tuple-element.63.refs_3_) | copy-start | bytes 983044
  64.1 15.5 %all-to-all-start.1 = ((bf16[4,640,128]{2,1,0:T(8,128)(2,1)}), bf16[4,640,128]{2,1,0:T(8,128)(2,1)S(1)}, u32[]{:S(2)}, u32[]{:S(2)}) async-start(bf16[4,640,128]{2,1,0:T(8,128)(2,1)} %copy-done.21), calls=%async_computation.1 | async-start | bytes 1310720 | tf_op jit(solution)/shard_map/all_to_all | solution.py:268
  81.7 13.3 %copy-start.45 = (bf16[4,512,128]{2,1,0:T(8,128)(2,1)S(1)}, bf16[4,512,128]{2,1,0:T(8,128)(2,1)}, u32[]{:S(2)}) copy-start(bf16[4,512,128]{2,1,0:T(8,128)(2,1)} %copy-done.44) | copy-start | bytes 1572868
  81.7 16.3 %copy-start.19 = (f32[4,512,128]{2,1,0:T(8,128)S(1)}, f32[4,512,128]{2,1,0:T(8,128)}, u32[]{:S(2)}) copy-start(f32[4,512,128]{2,1,0:T(8,128)} %copy-done.18) | copy-start | bytes 3145732
  91.9 17.8 %collective-permute-start.2 = (bf16[4,1152,128]{2,1,0:T(8,128)(2,1)}, bf16[4,1152,128]{2,1,0:T(8,128)(2,1)}, u32[]{:S(2)}, u32[]{:S(2)}) collective-permute-start(bf16[4,1152,128]{2,1,0:T(8,128)(2,1)} %get-tuple-element.68), channel_id=1, source_target_pairs={{0,16},{16,0},{32,48},{48,32},{64,80},{80,64},{96,112},{112,96},{1... | collective-permute-start | bytes 3538952 | tf_op jit(solution)/shard_map/ppermute | solution.py:264
  95.0 3.1 %collective-permute-start.3 = (bf16[4,512,128]{2,1,0:T(8,128)(2,1)S(1)}, bf16[4,512,128]{2,1,0:T(8,128)(2,1)S(1)}, u32[]{:S(2)}, u32[]{:S(2)}) collective-permute-start(bf16[4,512,128]{2,1,0:T(8,128)(2,1)S(1)} %copy-done.45), channel_id=1, source_target_pairs={{0,16},{16,0},{32,48},{48,32},{64,80},{80,64},{96,112},{112,96},{1... | collective-permute-start | bytes 1572872 | tf_op jit(solution)/shard_map/ppermute | solution.py:264
  98.1 11.6 %copy-start.11 = (f32[4,1152,128]{2,1,0:T(8,128)S(1)}, f32[4,1152,128]{2,1,0:T(8,128)}, u32[]{:S(2)}) copy-start(f32[4,1152,128]{2,1,0:T(8,128)} %copy-done.10) | copy-start | bytes 7077892
  101.0 13.1 %all-to-all-start.5 = ((bf16[4,512,128]{2,1,0:T(8,128)(2,1)}), bf16[4,512,128]{2,1,0:T(8,128)(2,1)S(1)}, u32[]{:S(2)}, u32[]{:S(2)}) async-start(bf16[4,512,128]{2,1,0:T(8,128)(2,1)} %copy-done.25), calls=%async_computation.5 | async-start | bytes 1048576 | tf_op jit(solution)/shard_map/all_to_all | solution.py:273
  105.0 29.4 %collective-permute-start.4 = (bf16[320,1792]{1,0:T(8,128)(2,1)}, bf16[320,1792]{1,0:T(8,128)(2,1)}, u32[]{:S(2)}, u32[]{:S(2)}) collective-permute-start(bf16[320,1792]{1,0:T(8,128)(2,1)} %copy-done.41), channel_id=1, source_target_pairs={{0,4},{4,8},{8,12},{12,0},{1,5},{5,9},{9,13},{13,1},{2,6},{6,10},{... | collective-permute-start | bytes 3440648 | tf_op jit(solution)/shard_map/ppermute | solution.py:260
  109.7 26.4 %collective-permute-start.5 = (bf16[320,1792]{1,0:T(8,128)(2,1)}, bf16[320,1792]{1,0:T(8,128)(2,1)}, u32[]{:S(2)}, u32[]{:S(2)}) collective-permute-start(bf16[320,1792]{1,0:T(8,128)(2,1)} %copy-done.40), channel_id=1, source_target_pairs={{0,12},{4,0},{8,4},{12,8},{1,13},{5,1},{9,5},{13,9},{2,14},{6,2},{... | collective-permute-start | bytes 3440648 | tf_op jit(solution)/shard_map/ppermute | solution.py:260
  114.2 32.1 %all-to-all-start.4 = ((bf16[4,1152,128]{2,1,0:T(8,128)(2,1)}), bf16[4,1152,128]{2,1,0:T(8,128)(2,1)S(1)}, u32[]{:S(2)}, u32[]{:S(2)}) async-start(bf16[4,1152,128]{2,1,0:T(8,128)(2,1)} %copy-done.17), calls=%async_computation.4 | async-start | bytes 2359296 | tf_op jit(solution)/shard_map/all_to_all | solution.py:273
  163.0 15.5 %all-to-all-start.7 = ((bf16[4,1024,128]{2,1,0:T(8,128)(2,1)}), bf16[4,1024,128]{2,1,0:T(8,128)(2,1)S(1)}, u32[]{:S(2)}, u32[]{:S(2)}) async-start(bf16[4,1024,128]{2,1,0:T(8,128)(2,1)} %get-tuple-element.92), calls=%async_computation.7 | async-start | bytes 2097152 | tf_op jit(solution)/shard_map/all_to_all | solution.py:273
  166.9 29.4 %collective-permute-start = (bf16[320,1792]{1,0:T(8,128)(2,1)}, bf16[320,1792]{1,0:T(8,128)(2,1)}, u32[]{:S(2)}, u32[]{:S(2)}) collective-permute-start(bf16[320,1792]{1,0:T(8,128)(2,1)} %get-tuple-element.58), channel_id=1, source_target_pairs={{0,4},{4,8},{8,12},{12,0},{1,5},{5,9},{9,13},{13,1},{2,6},{6,10},{... | collective-permute-start | bytes 3440648 | tf_op jit(solution)/shard_map/ppermute | solution.py:260
  166.9 35.1 %collective-permute-start.1 = (bf16[320,1792]{1,0:T(8,128)(2,1)}, bf16[320,1792]{1,0:T(8,128)(2,1)}, u32[]{:S(2)}, u32[]{:S(2)}) collective-permute-start(bf16[320,1792]{1,0:T(8,128)(2,1)} %get-tuple-element.59), channel_id=1, source_target_pairs={{0,12},{4,0},{8,4},{12,8},{1,13},{5,1},{9,5},{13,9},{2,14},{6,2},{... | collective-permute-start | bytes 3440648 | tf_op jit(solution)/shard_map/ppermute | solution.py:260
  178.4 31.6 %copy-start.5 = (bf16[512,1,1792]{2,0,1:T(8,128)(2,1)S(1)}, bf16[512,1,1792]{2,0,1:T(8,128)(2,1)}, u32[]{:S(2)}) copy-start(bf16[512,1,1792]{2,0,1:T(8,128)(2,1)} %param.11) | copy-start | bytes 5505028
  178.4 13.7 %all-to-all-start.8 = ((bf16[4,896,128]{2,1,0:T(8,128)(2,1)}), bf16[4,896,128]{2,1,0:T(8,128)(2,1)}, u32[]{:S(2)}, u32[]{:S(2)}) async-start(bf16[4,896,128]{2,1,0:T(8,128)(2,1)} %copy-done.20), calls=%async_computation.8 | async-start | bytes 1835008 | tf_op jit(solution)/shard_map/all_to_all | solution.py:273
  183.0 34.3 %collective-permute-start.6 = (bf16[320,1792]{1,0:T(8,128)(2,1)}, bf16[320,1792]{1,0:T(8,128)(2,1)}, u32[]{:S(2)}, u32[]{:S(2)}) collective-permute-start(bf16[320,1792]{1,0:T(8,128)(2,1)} %copy-done.43), channel_id=1, source_target_pairs={{0,4},{4,8},{8,12},{12,0},{1,5},{5,9},{9,13},{13,1},{2,6},{6,10},{... | collective-permute-start | bytes 3440648 | tf_op jit(solution)/shard_map/ppermute | solution.py:260
  183.1 34.3 %collective-permute-start.7 = (bf16[320,1792]{1,0:T(8,128)(2,1)}, bf16[320,1792]{1,0:T(8,128)(2,1)}, u32[]{:S(2)}, u32[]{:S(2)}) collective-permute-start(bf16[320,1792]{1,0:T(8,128)(2,1)} %copy-done.42), channel_id=1, source_target_pairs={{0,12},{4,0},{8,4},{12,8},{1,13},{5,1},{9,5},{13,9},{2,14},{6,2},{... | collective-permute-start | bytes 3440648 | tf_op jit(solution)/shard_map/ppermute | solution.py:260
  185.7 35.7 %collective-permute-start.8 = (bf16[4,1024,128]{2,1,0:T(8,128)(2,1)S(1)}, bf16[4,1024,128]{2,1,0:T(8,128)(2,1)}, u32[]{:S(2)}, u32[]{:S(2)}) collective-permute-start(bf16[4,1024,128]{2,1,0:T(8,128)(2,1)S(1)} %all-to-all-done.7.refs_0_), channel_id=1, source_target_pairs={{0,16},{16,0},{32,48},{48,32},{64,80},{80,64},{96,112},{112,96},{1... | collective-permute-start | bytes 3145736 | tf_op jit(solution)/shard_map/ppermute | solution.py:264
  192.1 11.1 %all-to-all-start.9 = ((bf16[4,512,128]{2,1,0:T(8,128)(2,1)}), bf16[4,512,128]{2,1,0:T(8,128)(2,1)}, u32[]{:S(2)}, u32[]{:S(2)}) async-start(bf16[4,512,128]{2,1,0:T(8,128)(2,1)} %copy-done.24), calls=%async_computation.9 | async-start | bytes 1048576 | tf_op jit(solution)/shard_map/all_to_all | solution.py:273
  196.2 25.1 %collective-permute-start.9 = (bf16[4,896,128]{2,1,0:T(8,128)(2,1)}, bf16[4,896,128]{2,1,0:T(8,128)(2,1)}, u32[]{:S(2)}, u32[]{:S(2)}) collective-permute-start(bf16[4,896,128]{2,1,0:T(8,128)(2,1)} %all-to-all-done.8.refs_2_), channel_id=1, source_target_pairs={{0,16},{16,0},{32,48},{48,32},{64,80},{80,64},{96,112},{112,96},{1... | collective-permute-start | bytes 2752520 | tf_op jit(solution)/shard_map/ppermute | solution.py:264
  203.2 18.1 %collective-permute-start.10 = (bf16[4,512,128]{2,1,0:T(8,128)(2,1)}, bf16[4,512,128]{2,1,0:T(8,128)(2,1)S(1)}, u32[]{:S(2)}, u32[]{:S(2)}) collective-permute-start(bf16[4,512,128]{2,1,0:T(8,128)(2,1)} %all-to-all-done.9.refs_4_), channel_id=1, source_target_pairs={{0,16},{16,0},{32,48},{48,32},{64,80},{80,64},{96,112},{112,96},{1... | collective-permute-start | bytes 1572872 | tf_op jit(solution)/shard_map/ppermute | solution.py:264
  (41 other events, 88.8 us)

commit v4 on v3

v4 whole, which is shorter than its diff:
```python
import jax
import jax.numpy as jnp
from jax import lax
from jax.experimental import pallas as pl
from jax.experimental.pallas import tpu as pltpu
from jax.sharding import PartitionSpec as P

F32 = jnp.float32
BF16 = jnp.bfloat16
SIDE = 128
SMEM = pl.BlockSpec(memory_space=pltpu.SMEM)
VMEM = pl.BlockSpec(memory_space=pltpu.VMEM)
HBM = pl.BlockSpec(memory_space=pl.ANY)


def lanes(block):
    return pl.ds(pl.multiple_of(block * SIDE, SIDE), SIDE)


def sublanes(block, size):
    return pl.ds(pl.multiple_of(block * size, size), size)


def shape(dims, dtype):
    return jax.ShapeDtypeStruct(dims, dtype)


def call(kernel, outs, smem, vmem, scratch=(), flops=0, mib=8, hbm_outs=0):
    nbytes = sum(a.size * a.dtype.itemsize for a in (*vmem, *outs))
    return pl.pallas_call(
        kernel,
        out_shape=tuple(outs),
        in_specs=[SMEM] * len(smem) + [VMEM] * len(vmem),
        out_specs=(HBM,) * hbm_outs + (VMEM,) * (len(outs) - hbm_outs),
        scratch_shapes=list(scratch),
        cost_estimate=pl.CostEstimate(
            flops=int(flops), bytes_accessed=int(nbytes), transcendentals=0
        ),
        compiler_params=pltpu.CompilerParams(vmem_limit_bytes=mib << 20),
    )(*smem, *vmem)


class Place:
    def __init__(self, n_f, n_t, n_d):
        self.n_f, self.n_t, self.n_d, self.chips = n_f, n_t, n_d, n_d // 2

    f = property(lambda self: lax.axis_index("fsdp"))
    t = property(lambda self: lax.axis_index("tensor"))
    chip = property(lambda self: lax.axis_index("dp") // 2)
    core = property(lambda self: lax.rem(lax.axis_index("dp"), 2))

    def live(self, counts):
        return counts[self.f * self.n_t + self.t]


def first_kernel(
    place, q_blocks, counts, rows, cols, tok, left, vals, sums, part, low, acc, stage, sems
):
    rank = jnp.dot(tok[...], left[:, lanes(place.t)], preferred_element_type=F32)
    part[...] = rank
    low[...] = rank.astype(BF16)
    live = place.live(counts)
    copies = []
    for quarter in range(place.n_f):
        acc[...] = jnp.zeros_like(acc)

        def body(s, carry):
            col = cols[s] - quarter * q_blocks

            @pl.when((col >= 0) & (col < q_blocks))
            def _():
                acc[:, lanes(col)] += jnp.dot(
                    tok[:, lanes(rows[s])], vals[s], preferred_element_type=F32
                )

            return carry

        lax.fori_loop(0, live, body, 0)
        slot = quarter % 2
        if quarter >= 2:
            copies[quarter - 2].wait()
        stage[slot] = acc[...].astype(BF16)
        copies.append(pltpu.make_async_copy(stage.at[slot], sums.at[quarter], sems.at[slot]))
        copies[-1].start()
    for copy in copies[-2:]:
        copy.wait()


def back_kernel(place, cot, right, own, s1, s2, s3, full):
    quarter = right.shape[1]
    here = pl.ds(pl.multiple_of(place.f * quarter, SIDE), quarter)
    full[...] = lax.dot_general(
        cot[:, here], right[...], (((1,), (1,)), ((), ())), preferred_element_type=F32
    )
    own[...] = full[:, lanes(place.t)]
    for k, out in ((1, s1), (2, s2), (3, s3)):
        out[...] = full[:, lanes(lax.rem(place.t + k, place.n_t))].astype(BF16)


def blocks_kernel(place, counts, rows, cols, tok, cot, mine, theirs):
    mine[...] = jnp.zeros_like(mine)
    theirs[...] = jnp.zeros_like(theirs)
    per = mine.shape[1] // SIDE
    chip, core = place.chip, place.core

    def body(s, carry):
        grad = lax.dot_general(
            tok[:, lanes(rows[s])],
            cot[:, lanes(cols[s])],
            (((0,), (0,)), ((), ())),
            preferred_element_type=F32,
        )
        owner = s // per
        j = lax.rem(owner // 2 - chip + place.chips, place.chips)
        at = sublanes(lax.rem(s, per), SIDE)
        keep = lax.rem(owner, 2) == core

        @pl.when(keep)
        def _():
            mine[j, at] = grad

        @pl.when(jnp.logical_not(keep))
        def _():
            theirs[j, at] = grad.astype(BF16)

        return carry

    lax.fori_loop(0, place.live(counts), body, 0)


def factors_kernel(
    place, tok, cot, g0, g1, g2, g3, back, blocks_mine, blocks_theirs, mine, theirs, left, right
):
    quarter = right.shape[1]
    here = pl.ds(pl.multiple_of(place.f * quarter, SIDE), quarter)
    left[...] = lax.dot_general(
        back[...], tok[...], (((0,), (0,)), ((), ())), preferred_element_type=F32
    ).T
    for k, g in enumerate((g0, g1, g2, g3)):
        right[sublanes(lax.rem(place.t - k + place.n_t, place.n_t), SIDE), :] = lax.dot_general(
            g[...], cot[:, here], (((0,), (0,)), ((), ())), preferred_element_type=F32
        )
    n_l = left.shape[0] // place.n_d
    n_r = right.shape[0] // place.n_d
    n_lr = n_l + quarter // SIDE * n_r
    for j in range(place.chips):
        chip = lax.rem(place.chip + j, place.chips)
        for core, out in ((place.core, mine), (1 - place.core, theirs)):
            at = chip * 2 + core
            out[j, :n_l] = left[sublanes(at, n_l), :].astype(out.dtype)
            for p in range(quarter // SIDE):
                out[j, n_l + p * n_r : n_l + (p + 1) * n_r] = right[
                    sublanes(at, n_r), p * SIDE : (p + 1) * SIDE
                ].astype(out.dtype)
        mine[j, n_lr:] = blocks_mine[j]
        theirs[j, n_lr:] = blocks_theirs[j]


def cores_kernel(mine, got, own, *pieces):
    own[...] = mine[0] + got[0].astype(F32)
    for k, piece in enumerate(pieces):
        piece[...] = (mine[k + 1] + got[k + 1].astype(F32)).astype(BF16)


def total_kernel(n_in, *refs):
    total = refs[0][...]
    for r in refs[1:n_in]:
        total = total + r[...].astype(F32)
    row = 0
    for out in refs[n_in:]:
        out[...] = total[row : row + out.shape[0]].astype(BF16)
        row += out.shape[0]


def stack_kernel(*refs):
    out, rows = refs[-1], refs[0].shape[0]
    for k, part in enumerate(refs[:-1]):
        out[k * rows : (k + 1) * rows] = part[...]


def low_kernel(place, g0, g1, g2, g3, right, out):
    acc = jnp.zeros(out.shape, F32)
    for k, g in enumerate((g0, g1, g2, g3)):
        rows = sublanes(lax.rem(place.t - k + place.n_t, place.n_t), SIDE)
        acc += jnp.dot(g[...], right[rows, :], preferred_element_type=F32)
    out[...] = acc


def finish_kernel(low, residual, out):
    out[...] = (low[...] + residual[...].astype(F32)).astype(BF16)


def spread_kernel(place, ours_l, theirs_l, ours_r, theirs_r, left, right, blocks):
    n_l = left.shape[0] // place.n_d
    n_r = right.shape[0] // place.n_d
    n_b = blocks.shape[0] // place.n_d
    panels = right.shape[1] // SIDE
    for core, src_l, src_r in ((place.core, ours_l, ours_r), (1 - place.core, theirs_l, theirs_r)):
        for j in range(place.chips):
            at = lax.rem(place.chip - j + place.chips, place.chips) * 2 + core
            for k in range(place.n_t):
                col = lax.rem(place.t - k + place.n_t, place.n_t)
                left[sublanes(at, n_l), lanes(col)] = src_l[j, k * n_l : (k + 1) * n_l]
            for p in range(panels):
                right[sublanes(at, n_r), p * SIDE : (p + 1) * SIDE] = src_r[
                    j, p * n_r : (p + 1) * n_r
                ]
            blocks[sublanes(at, n_b)] = src_r[j, panels * n_r :]


def shift(x, axis, n, k):
    return lax.ppermute(x, axis, [(i, (i + k) % n) for i in range(n)])


def chip_shift(x, n_data, k):
    chips = n_data // 2
    perm = [(2 * a + c, 2 * ((a + k) % chips) + c) for a in range(chips) for c in range(2)]
    return lax.ppermute(x, "dp", perm)


def core_swap(x, n_data):
    return lax.ppermute(x, "dp", [(i, i ^ 1) for i in range(n_data)])


def per_device(
    tokens, cotangent, left_factor, right_factor, block_values, block_rows, block_cols, block_counts
):
    n_f = lax.axis_size("fsdp")
    n_t = lax.axis_size("tensor")
    n_d = lax.axis_size("dp")
    place = Place(n_f, n_t, n_d)
    chips = n_d // 2
    maxb = block_values.shape[0]
    tok_rows, features = tokens.shape
    right = right_factor.reshape(right_factor.shape[0], -1)
    rank_size, quarter = right.shape
    q_blocks = quarter // SIDE
    r_part = rank_size // n_t
    lists = (block_counts, block_rows, block_cols)
    block_flops = 2 * tok_rows * SIDE * SIDE * maxb

    def bind(kernel, *args):
        return lambda *refs: kernel(place, *args, *refs)

    def over(n, k_shift):
        return [k_shift(k) for k in range(1, n)]

    def total(parts, outs):
        n_in = len(parts)
        return call(lambda *refs: total_kernel(n_in, *refs), outs, (), parts)

    part = shape((tok_rows, r_part), F32)
    part_low = shape((tok_rows, r_part), BF16)

    sums, rank_part, rank_low = call(
        bind(first_kernel, q_blocks),
        (shape((n_f, tok_rows, quarter), BF16), part, part_low),
        lists,
        (tokens, left_factor, block_values),
        [
            pltpu.VMEM((tok_rows, quarter), F32),
            pltpu.VMEM((2, tok_rows, quarter), BF16),
            pltpu.SemaphoreType.DMA((2,)),
        ],
        flops=block_flops,
        mib=24,
        hbm_outs=1,
    )
    residual = lax.psum_scatter(sums, "fsdp", scatter_dimension=0, tiled=False)
    rank_in = over(n_f, lambda k: shift(rank_low, "fsdp", n_f, k))
    (rank_t,) = total((rank_part, *rank_in), (part_low,))
    ranks = [rank_t] + over(n_t, lambda k: shift(rank_t, "tensor", n_t, k))

    back_part, *back_out = call(
        bind(back_kernel),
        (part, part_low, part_low, part_low),
        (),
        (cotangent, right),
        [pltpu.VMEM((tok_rows, rank_size), F32)],
        flops=2 * tok_rows * quarter * rank_size,
        mib=16,
    )
    back_in = [shift(b, "tensor", n_t, k + 1) for k, b in enumerate(back_out)]
    back_sum = back_part
    for b in back_in:
        back_sum = back_sum + b.astype(F32)
    back_low = back_sum.astype(BF16)
    for b in over(n_f, lambda k: shift(back_low, "fsdp", n_f, k)):
        back_sum = back_sum + b.astype(F32)
    back = back_sum.astype(BF16)

    n_b = maxb // n_d * SIDE
    blocks_mine, blocks_theirs = call(
        bind(blocks_kernel),
        (shape((chips, n_b, SIDE), F32), shape((chips, n_b, SIDE), BF16)),
        lists,
        (tokens, cotangent),
        flops=block_flops,
        mib=20,
    )

    n_l = features // n_d
    n_r = rank_size // n_d
    n_rb = q_blocks * n_r + n_b
    mine, theirs = call(
        bind(factors_kernel),
        (shape((chips, n_l + n_rb, SIDE), F32), shape((chips, n_l + n_rb, SIDE), BF16)),
        (),
        (tokens, cotangent, *ranks, back, blocks_mine, blocks_theirs),
        [pltpu.VMEM((features, r_part), F32), pltpu.VMEM((rank_size, quarter), F32)],
        flops=2 * tok_rows * (quarter * rank_size + features * r_part),
        mib=28,
    )
    got = core_swap(theirs, n_d)
    own, *out = call(
        cores_kernel,
        (shape((n_l + n_rb, SIDE), F32),) + (shape((n_l + n_rb, SIDE), BF16),) * (chips - 1),
        (),
        (mine, got),
        mib=10,
    )
    pieces = [chip_shift(b, n_d, k + 1) for k, b in enumerate(out)]
    left_part, rest_part = total(
        (own, *pieces), (shape((n_l, SIDE), BF16), shape((n_rb, SIDE), BF16))
    )

    def gather_chips(x):
        return jnp.stack([x] + over(chips, lambda k: chip_shift(x, n_d, k)))

    lefts = [left_part] + over(n_t, lambda k: shift(left_part, "tensor", n_t, k))
    rest_ours = gather_chips(rest_part)
    rest_theirs = core_swap(rest_ours, n_d)
    (left_chunk,) = call(stack_kernel, (shape((n_t * n_l, SIDE), BF16),), (), lefts)
    left_ours = gather_chips(left_chunk)
    left_theirs = core_swap(left_ours, n_d)
    out_left, out_right, out_blocks = call(
        bind(spread_kernel),
        (
            shape((features, rank_size), BF16),
            shape((rank_size, quarter), BF16),
            shape((maxb * SIDE, SIDE), BF16),
        ),
        (),
        (left_ours, left_theirs, rest_ours, rest_theirs),
        mib=14,
    )
    (low,) = call(
        bind(low_kernel),
        (shape((tok_rows, quarter), F32),),
        (),
        (*ranks, right),
        flops=2 * tok_rows * quarter * rank_size,
        mib=16,
    )
    (mixed,) = call(
        finish_kernel, (shape((tok_rows, quarter), BF16),), (), (low, residual), mib=14
    )
    return (
        mixed.reshape(tok_rows, 1, quarter),
        out_left,
        out_right.reshape(right_factor.shape),
        out_blocks.reshape(maxb, SIDE, SIDE),
    )


def solution(mesh):
    return jax.shard_map(
        per_device,
        mesh=mesh,
        in_specs=(
            P("dp", "fsdp"),
            P("dp", "tensor"),
            P("fsdp", None),
            P(None, "tensor", "fsdp"),
            P(("fsdp", "tensor"), None, None),
            P(("fsdp", "tensor")),
            P(("fsdp", "tensor")),
            P(),
        ),
        out_specs=(
            P("dp", "tensor", "fsdp"),
            P("fsdp", None),
            P(None, "tensor", "fsdp"),
            P(("fsdp", "tensor"), None, None),
        ),
        check_vma=False,
    )
```

time: 230 us -> 161 us (0.70); the launches traced: 226 us -> 161 us
  starting transfers between devices: 69.9 us -> 35.3 us
  blocking collectives: 25.9 us -> 0 us
  Pallas kernels: 53.3 us -> 34.3 us
  local copies, waits for them, and re-layouts: 42.5 us -> 25 us
  waiting for transfers between devices: 33.7 us -> 51.1 us
  between operations: 1.16 us -> 14.2 us
    all_to_all x8 -> x0, starting transfers between devices: 39.1 us -> none  [the longest x5 20.6 us: chip_exchange(): return lax.all_to_all(x, 'dp', 0, 0, axis_index_groups=groups, tiled=True)]
    ppermute x0 -> x9, waiting for transfers between devices: none -> 32.8 us  [chip_shift(): return lax.ppermute(x, 'dp', perm)]
    all_to_all x2 -> x0, blocking collectives: 25.9 us -> none  [exchange(): return lax.all_to_all(x, axis, 0, 0, tiled=True)]
    pallas_call x16 -> x11, Pallas kernels: 53.3 us -> 34.3 us  [call(): pl.pallas_call(kernel, out_shape=tuple(outs), in_specs=[SMEM] * len(smem)...]
    unnamed x92 -> x36, local copies, waits for them, and re-layouts: 42.5 us -> 25 us
    ppermute x5 -> x3, starting transfers between devices: 20.7 us -> 6.89 us  [core_swap(): return lax.ppermute(x, 'dp', [(i, i ^ 1) for i in range(n_data)])]
    all_to_all x8 -> x0, waiting for transfers between devices: 12.8 us -> none  [the longest x5 11.6 us: chip_exchange(): return lax.all_to_all(x, 'dp', 0, 0, axis_index_groups=groups, tiled=True)]
    ppermute x0 -> x9, starting transfers between devices: none -> 12.3 us  [chip_shift(): return lax.ppermute(x, 'dp', perm)]
  transfers between devices with their start and end apart: 19 -> 28, of which waited for: 8 -> 15; matrix products, arithmetic and copies ran while one was open for 0% -> 0% of each run, Pallas kernels for 14% -> 12%
where the time goes in v4:
time: 161 us
  waiting for transfers between devices  51.1 us (32%)
  starting transfers between devices  35.3 us (22%)
  Pallas kernels  34.3 us (21%)
  local copies, waits for them, and re-layouts  25 us (16%)
  between operations  14.2 us (9%)
    pallas_call x11, Pallas kernels, call(): pl.pallas_call(kernel, out_shape=tuple(outs), in_specs=[SMEM] * len(smem)...  34.3 us
    ppermute x9, waiting for transfers between devices, chip_shift(): return lax.ppermute(x, 'dp', perm)  32.8 us
    unnamed x36, local copies, waits for them, and re-layouts  25 us
    ppermute x15, starting transfers between devices, shift(): return lax.ppermute(x, axis, [(i, (i + k) % n) for i in range(n)])  16.1 us
    ppermute x15, waiting for transfers between devices, shift(): return lax.ppermute(x, axis, [(i, (i + k) % n) for i in range(n)])  15.1 us
    ppermute x9, starting transfers between devices, chip_shift(): return lax.ppermute(x, 'dp', perm)  12.3 us
    ppermute x3, starting transfers between devices, core_swap(): return lax.ppermute(x, 'dp', [(i, i ^ 1) for i in range(n_data)])  6.89 us
    ppermute x3, waiting for transfers between devices, core_swap(): return lax.ppermute(x, 'dp', [(i, i ^ 1) for i in range(n_data)])  3.23 us
  transfers between devices with their start and end apart: 28, of which 15 were waited for; matrix products, arithmetic and copies ran while one was open for 0% of the time, Pallas kernels for 12%

profile of v4, /device:TPU:1, one launch (start us, length us, event | category | flops | bytes accessed | tf_op | source)
XLA Modules:
  0.0 160.6 jit_solution(11430040797239185580)
XLA Ops:
  13.7 12.7 %shard_map.111 = (bf16[4,640,1792]{2,1,0:T(8,128)(2,1)S(1)}, f32[640,128]{1,0:T(8,128)S(1)}, bf16[640,128]{1,0:T(8,128)(2,1)S(1)}) custom-call(s32[16]{0:T(128)S(1)} %copy-done.12, s32[32]{0:T(128)S(1)} %copy-done.14, s32[32]{0:T(128)S(1)} %copy-done.16, bf16[640,2048]{1,0:T(8,128)(2,1)S(1)} %copy-done.3, bf16[2048,512]{1,0:T(8,128)(2,1)S(1)} %copy-done.10, ...), custom_call_target="tpu_custom_call" | custom-call | flops 671088640 | bytes 15433728 | tf_op jit(solution)/shard_map/pallas_call | solution.py:30
  26.5 3.6 %copy-done.7 = bf16[4,640,1792]{2,1,0:T(8,128)(2,1)} copy-done((bf16[4,640,1792]{2,1,0:T(8,128)(2,1)}, bf16[4,640,1792]{2,1,0:T(8,128)(2,1)S(1)}, u32[]{:S(2)}) %copy-start.7) | copy-done | bytes 9175064
  31.6 3.6 %copy-done = bf16[640,7168]{1,0:T(8,128)(2,1)S(1)} copy-done((bf16[640,7168]{1,0:T(8,128)(2,1)S(1)}, bf16[640,7168]{1,0:T(8,128)(2,1)}, u32[]{:S(2)}) %copy-start) | copy-done | bytes 9175064
  39.5 3.2 %collective-permute-start.2 = (bf16[640,128]{1,0:T(8,128)(2,1)S(1)}, bf16[640,128]{1,0:T(8,128)(2,1)S(1)}, u32[]{:S(2)}, u32[]{:S(2)}) collective-permute-start(bf16[640,128]{1,0:T(8,128)(2,1)S(1)} %get-tuple-element.25), channel_id=1, source_target_pairs={{0,12},{4,0},{8,4},{12,8},{1,13},{5,1},{9,5},{13,9},{2,14},{6,2},{... | collective-permute-start | bytes 491528 | tf_op jit(solution)/shard_map/ppermute | solution.py:212
  46.5 3.5 %collective-permute-start.11 = (bf16[640,128]{1,0:T(8,128)(2,1)S(1)}, bf16[640,128]{1,0:T(8,128)(2,1)S(1)}, u32[]{:S(2)}, u32[]{:S(2)}) collective-permute-start(bf16[640,128]{1,0:T(8,128)(2,1)S(1)} %fusion), channel_id=1, source_target_pairs={{0,12},{4,0},{8,4},{12,8},{1,13},{5,1},{9,5},{13,9},{2,14},{6,2},{... | collective-permute-start | bytes 491528 | tf_op jit(solution)/shard_map/ppermute | solution.py:212
  51.5 3.7 %copy-done.1 = bf16[640,7168]{1,0:T(8,128)(2,1)S(1)} copy-done((bf16[640,7168]{1,0:T(8,128)(2,1)S(1)}, bf16[640,7168]{1,0:T(8,128)(2,1)}, u32[]{:S(2)}) %copy-start.1) | copy-done | bytes 9175064
  55.2 9.8 %shard_map.116 = (f32[4,512,128]{2,1,0:T(8,128)S(1)}, bf16[4,512,128]{2,1,0:T(8,128)(2,1)S(1)}) custom-call(s32[16]{0:T(128)S(1)} %copy-done.13, s32[32]{0:T(128)S(1)} %copy-done.15, s32[32]{0:T(128)S(1)} %copy-done.17, bf16[640,2048]{1,0:T(8,128)(2,1)S(1)} %copy-done.4, bf16[640,7168]{1,0:T(8,128)(2,1)S(1)} %copy-done.1), custom_call_target="tpu_custom_call" | custom-call | flops 671088640 | bytes 13369344 | tf_op jit(solution)/shard_map/pallas_call | solution.py:30
  67.4 4.4 %collective-permute-done.9 = bf16[640,128]{1,0:T(8,128)(2,1)S(1)} collective-permute-done((bf16[640,128]{1,0:T(8,128)(2,1)S(1)}, bf16[640,128]{1,0:T(8,128)(2,1)S(1)}, u32[]{:S(2)}, u32[]{:S(2)}) %collective-permute-start.9) | collective-permute-done | bytes 163872 | tf_op jit(solution)/shard_map/ppermute | solution.py:212
  73.1 2.4 %shard_map.117 = (f32[4,1664,128]{2,1,0:T(8,128)S(1)}, bf16[4,1664,128]{2,1,0:T(8,128)(2,1)S(1)}) custom-call(bf16[640,2048]{1,0:T(8,128)(2,1)S(1)} %copy-done.4, bf16[640,7168]{1,0:T(8,128)(2,1)S(1)} %copy-done.2, bf16[640,128]{1,0:T(8,128)(2,1)S(1)} %shard_map.112.refs_0_.refs_2_, bf16[640,128]{1,0:T(8,128)(2,1)S(1)} %collective-permute-done.3.refs_1_.refs_3_, ...), custom_call_target="tpu_custom_call" | custom-call | flops 1509949440 | bytes 19300352 | tf_op jit(solution)/shard_map/pallas_call | solution.py:30
  75.4 4.5 %collective-permute-start.12 = (bf16[4,1664,128]{2,1,0:T(8,128)(2,1)S(1)}, bf16[4,1664,128]{2,1,0:T(8,128)(2,1)S(1)}, u32[]{:S(2)}, u32[]{:S(2)}) collective-permute-start(bf16[4,1664,128]{2,1,0:T(8,128)(2,1)S(1)} %get-tuple-element.34), channel_id=1, source_target_pairs={{0,16},{16,0},{32,48},{48,32},{64,80},{80,64},{96,112},{112,96},{1... | collective-permute-start | bytes 5111816 | tf_op jit(solution)/shard_map/ppermute | solution.py:222
  80.0 3.2 %collective-permute-done.12.got = bf16[4,1664,128]{2,1,0:T(8,128)(2,1)S(1)} collective-permute-done((bf16[4,1664,128]{2,1,0:T(8,128)(2,1)S(1)}, bf16[4,1664,128]{2,1,0:T(8,128)(2,1)S(1)}, u32[]{:S(2)}, u32[]{:S(2)}) %collective-permute-start.12) | collective-permute-done | bytes 1703968 | tf_op jit(solution)/shard_map/ppermute | solution.py:222
  84.8 2.4 %collective-permute-start.14 = (bf16[1664,128]{1,0:T(8,128)(2,1)S(1)}, bf16[1664,128]{1,0:T(8,128)(2,1)S(1)}, u32[]{:S(2)}, u32[]{:S(2)}) collective-permute-start(bf16[1664,128]{1,0:T(8,128)(2,1)S(1)} %get-tuple-element.37), channel_id=1, source_target_pairs={{0,64},{16,80},{32,96},{48,112},{64,0},{80,16},{96,32},{112,48},{1... | collective-permute-start | bytes 1277960 | tf_op jit(solution)/shard_map/ppermute | solution.py:218
  88.4 7.5 %collective-permute-done.13.refs_1_ = bf16[1664,128]{1,0:T(8,128)(2,1)S(1)} collective-permute-done((bf16[1664,128]{1,0:T(8,128)(2,1)S(1)}, bf16[1664,128]{1,0:T(8,128)(2,1)S(1)}, u32[]{:S(2)}, u32[]{:S(2)}) %collective-permute-start.13) | collective-permute-done | bytes 426016 | tf_op jit(solution)/shard_map/ppermute | solution.py:218
  95.9 10.0 %collective-permute-done.14.refs_2_ = bf16[1664,128]{1,0:T(8,128)(2,1)S(1)} collective-permute-done((bf16[1664,128]{1,0:T(8,128)(2,1)S(1)}, bf16[1664,128]{1,0:T(8,128)(2,1)S(1)}, u32[]{:S(2)}, u32[]{:S(2)}) %collective-permute-start.14) | collective-permute-done | bytes 426016 | tf_op jit(solution)/shard_map/ppermute | solution.py:218
  106.1 2.9 %collective-permute-start.25 = (bf16[1408,128]{1,0:T(8,128)(2,1)S(1)}, bf16[1408,128]{1,0:T(8,128)(2,1)S(1)}, u32[]{:S(2)}, u32[]{:S(2)}) collective-permute-start(bf16[1408,128]{1,0:T(8,128)(2,1)S(1)} %get-tuple-element.40), channel_id=1, source_target_pairs={{0,96},{16,112},{32,0},{48,16},{64,32},{80,48},{96,64},{112,80},{1... | collective-permute-start | bytes 1081352 | tf_op jit(solution)/shard_map/ppermute | solution.py:218
  113.1 2.5 %collective-permute-done.17.refs_2_ = bf16[256,128]{1,0:T(8,128)(2,1)S(1)} collective-permute-done((bf16[256,128]{1,0:T(8,128)(2,1)S(1)}, bf16[256,128]{1,0:T(8,128)(2,1)S(1)}, u32[]{:S(2)}, u32[]{:S(2)}) %collective-permute-start.17) | collective-permute-done | bytes 65568 | tf_op jit(solution)/shard_map/ppermute | solution.py:212
  115.6 2.8 %collective-permute-done.16.refs_1_ = bf16[256,128]{1,0:T(8,128)(2,1)S(1)} collective-permute-done((bf16[256,128]{1,0:T(8,128)(2,1)S(1)}, bf16[256,128]{1,0:T(8,128)(2,1)S(1)}, u32[]{:S(2)}, u32[]{:S(2)}) %collective-permute-start.16) | collective-permute-done | bytes 65568 | tf_op jit(solution)/shard_map/ppermute | solution.py:212
  122.6 6.2 %collective-permute-done.23 = bf16[1408,128]{1,0:T(8,128)(2,1)S(1)} collective-permute-done((bf16[1408,128]{1,0:T(8,128)(2,1)S(1)}, bf16[1408,128]{1,0:T(8,128)(2,1)S(1)}, u32[]{:S(2)}, u32[]{:S(2)}) %collective-permute-start.23) | collective-permute-done | bytes 360480 | tf_op jit(solution)/shard_map/ppermute | solution.py:218
  130.5 4.7 %collective-permute-done.21 = bf16[1024,128]{1,0:T(8,128)(2,1)S(1)} collective-permute-done((bf16[1024,128]{1,0:T(8,128)(2,1)S(1)}, bf16[1024,128]{1,0:T(8,128)(2,1)S(1)}, u32[]{:S(2)}, u32[]{:S(2)}) %collective-permute-start.21) | collective-permute-done | bytes 262176 | tf_op jit(solution)/shard_map/ppermute | solution.py:218
  135.2 4.1 %collective-permute-done.19 = bf16[1024,128]{1,0:T(8,128)(2,1)S(1)} collective-permute-done((bf16[1024,128]{1,0:T(8,128)(2,1)S(1)}, bf16[1024,128]{1,0:T(8,128)(2,1)S(1)}, u32[]{:S(2)}, u32[]{:S(2)}) %collective-permute-start.19) | collective-permute-done | bytes 262176 | tf_op jit(solution)/shard_map/ppermute | solution.py:218
  140.3 2.5 %shard_map.113.low = f32[640,1792]{1,0:T(8,128)S(1)} custom-call(bf16[640,128]{1,0:T(8,128)(2,1)S(1)} %shard_map.112.refs_0_.refs_2_, bf16[640,128]{1,0:T(8,128)(2,1)S(1)} %collective-permute-done.3.refs_1_.refs_3_, bf16[640,128]{1,0:T(8,128)(2,1)S(1)} %collective-permute-done.4.refs_2_.refs_4_, bf16[640,128]{1,0:T(8,128)(2,1)S(1)} %collective-permute-done.5.refs_3_.refs_5_, ...), custom_call_target="tpu_custom_call" | custom-call | flops 1174405120 | bytes 7077888 | tf_op jit(solution)/shard_map/pallas_call | solution.py:30
  142.8 2.2 %copy-done.5 = f32[640,1792]{1,0:T(8,128)} copy-done((f32[640,1792]{1,0:T(8,128)}, f32[640,1792]{1,0:T(8,128)S(1)}, u32[]{:S(2)}) %copy-start.5) | copy-done | bytes 4587544
  145.0 3.0 %shard_map.121 = (bf16[2048,512]{1,0:T(8,128)(2,1)}, bf16[512,1792]{1,0:T(8,128)(2,1)}, bf16[4096,128]{1,0:T(8,128)(2,1)}) custom-call(bf16[4,1024,128]{2,1,0:T(8,128)(2,1)S(1)} %pad_maximum_fusion.1.refs_0_, bf16[4,1024,128]{2,1,0:T(8,128)(2,1)S(1)} %collective-permute-done.22.refs_1_, bf16[4,1408,128]{2,1,0:T(8,128)(2,1)S(1)} %pad_maximum_fusion.refs_2_, ...), custom_call_target="tpu_custom_call" | custom-call | bytes 9961472 | tf_op jit(solution)/shard_map/pallas_call | solution.py:30
  148.0 2.3 %copy-done.6 = f32[640,1792]{1,0:T(8,128)S(1)} copy-done((f32[640,1792]{1,0:T(8,128)S(1)}, f32[640,1792]{1,0:T(8,128)}, u32[]{:S(2)}) %copy-start.6) | copy-done | bytes 4587544
  (84 shorter events, 38.7 us)
Async XLA Ops:
  7.2 140.8 %reduce-scatter.2.cloned.1.call-start = ((), (), s32[]{:S(2)}) async-start(), calls=%async_computation.1 | async-start | bytes 11468800 | tf_op jit(solution)/shard_map/reduce_scatter | solution.py:269
  36.8 7.0 %collective-permute-start.6 = (bf16[640,128]{1,0:T(8,128)(2,1)S(1)}, bf16[640,128]{1,0:T(8,128)(2,1)S(1)}, u32[]{:S(2)}, u32[]{:S(2)}) collective-permute-start(bf16[640,128]{1,0:T(8,128)(2,1)S(1)} %get-tuple-element.28), channel_id=1, source_target_pairs={{0,1},{1,2},{2,3},{3,0},{4,5},{5,6},{6,7},{7,4},{8,9},{9,10},{10,1... | collective-permute-start | bytes 491528 | tf_op jit(solution)/shard_map/ppermute | solution.py:212
  36.9 8.6 %collective-permute-start.7 = (bf16[640,128]{1,0:T(8,128)(2,1)S(1)}, bf16[640,128]{1,0:T(8,128)(2,1)S(1)}, u32[]{:S(2)}, u32[]{:S(2)}) collective-permute-start(bf16[640,128]{1,0:T(8,128)(2,1)S(1)} %get-tuple-element.29), channel_id=1, source_target_pairs={{0,2},{1,3},{2,0},{3,1},{4,6},{5,7},{6,4},{7,5},{8,10},{9,11},{10,... | collective-permute-start | bytes 491528 | tf_op jit(solution)/shard_map/ppermute | solution.py:212
  38.3 8.1 %collective-permute-start.8 = (bf16[640,128]{1,0:T(8,128)(2,1)S(1)}, bf16[640,128]{1,0:T(8,128)(2,1)S(1)}, u32[]{:S(2)}, u32[]{:S(2)}) collective-permute-start(bf16[640,128]{1,0:T(8,128)(2,1)S(1)} %get-tuple-element.30), channel_id=1, source_target_pairs={{0,3},{1,0},{2,1},{3,2},{4,7},{5,4},{6,5},{7,6},{8,11},{9,8},{10,9... | collective-permute-start | bytes 491528 | tf_op jit(solution)/shard_map/ppermute | solution.py:212
  39.5 11.6 %collective-permute-start.2 = (bf16[640,128]{1,0:T(8,128)(2,1)S(1)}, bf16[640,128]{1,0:T(8,128)(2,1)S(1)}, u32[]{:S(2)}, u32[]{:S(2)}) collective-permute-start(bf16[640,128]{1,0:T(8,128)(2,1)S(1)} %get-tuple-element.25), channel_id=1, source_target_pairs={{0,12},{4,0},{8,4},{12,8},{1,13},{5,1},{9,5},{13,9},{2,14},{6,2},{... | collective-permute-start | bytes 491528 | tf_op jit(solution)/shard_map/ppermute | solution.py:212
  42.8 22.2 %collective-permute-start.1 = (bf16[640,128]{1,0:T(8,128)(2,1)S(1)}, bf16[640,128]{1,0:T(8,128)(2,1)S(1)}, u32[]{:S(2)}, u32[]{:S(2)}) collective-permute-start(bf16[640,128]{1,0:T(8,128)(2,1)S(1)} %get-tuple-element.25), channel_id=1, source_target_pairs={{0,8},{4,12},{8,0},{12,4},{1,9},{5,13},{9,1},{13,5},{2,10},{6,14},... | collective-permute-start | bytes 491528 | tf_op jit(solution)/shard_map/ppermute | solution.py:212
  43.8 21.2 %collective-permute-start = (bf16[640,128]{1,0:T(8,128)(2,1)S(1)}, bf16[640,128]{1,0:T(8,128)(2,1)S(1)}, u32[]{:S(2)}, u32[]{:S(2)}) collective-permute-start(bf16[640,128]{1,0:T(8,128)(2,1)S(1)} %get-tuple-element.25), channel_id=1, source_target_pairs={{0,4},{4,8},{8,12},{12,0},{1,5},{5,9},{9,13},{13,1},{2,6},{6,10},{... | collective-permute-start | bytes 491528 | tf_op jit(solution)/shard_map/ppermute | solution.py:212
  46.5 18.7 %collective-permute-start.11 = (bf16[640,128]{1,0:T(8,128)(2,1)S(1)}, bf16[640,128]{1,0:T(8,128)(2,1)S(1)}, u32[]{:S(2)}, u32[]{:S(2)}) collective-permute-start(bf16[640,128]{1,0:T(8,128)(2,1)S(1)} %fusion), channel_id=1, source_target_pairs={{0,12},{4,0},{8,4},{12,8},{1,13},{5,1},{9,5},{13,9},{2,14},{6,2},{... | collective-permute-start | bytes 491528 | tf_op jit(solution)/shard_map/ppermute | solution.py:212
  50.0 17.3 %collective-permute-start.10 = (bf16[640,128]{1,0:T(8,128)(2,1)S(1)}, bf16[640,128]{1,0:T(8,128)(2,1)S(1)}, u32[]{:S(2)}, u32[]{:S(2)}) collective-permute-start(bf16[640,128]{1,0:T(8,128)(2,1)S(1)} %fusion), channel_id=1, source_target_pairs={{0,8},{4,12},{8,0},{12,4},{1,9},{5,13},{9,1},{13,5},{2,10},{6,14},... | collective-permute-start | bytes 491528 | tf_op jit(solution)/shard_map/ppermute | solution.py:212
  51.1 20.6 %collective-permute-start.9 = (bf16[640,128]{1,0:T(8,128)(2,1)S(1)}, bf16[640,128]{1,0:T(8,128)(2,1)S(1)}, u32[]{:S(2)}, u32[]{:S(2)}) collective-permute-start(bf16[640,128]{1,0:T(8,128)(2,1)S(1)} %fusion), channel_id=1, source_target_pairs={{0,4},{4,8},{8,12},{12,0},{1,5},{5,9},{9,13},{13,1},{2,6},{6,10},{... | collective-permute-start | bytes 491528 | tf_op jit(solution)/shard_map/ppermute | solution.py:212
  65.1 6.8 %collective-permute-start.5 = (bf16[640,128]{1,0:T(8,128)(2,1)S(1)}, bf16[640,128]{1,0:T(8,128)(2,1)S(1)}, u32[]{:S(2)}, u32[]{:S(2)}) collective-permute-start(bf16[640,128]{1,0:T(8,128)(2,1)S(1)} %shard_map.112.refs_0_.refs_2_), channel_id=1, source_target_pairs={{0,3},{1,0},{2,1},{3,2},{4,7},{5,4},{6,5},{7,6},{8,11},{9,8},{10,9... | collective-permute-start | bytes 491528 | tf_op jit(solution)/shard_map/ppermute | solution.py:212
  65.2 6.7 %collective-permute-start.4 = (bf16[640,128]{1,0:T(8,128)(2,1)S(1)}, bf16[640,128]{1,0:T(8,128)(2,1)S(1)}, u32[]{:S(2)}, u32[]{:S(2)}) collective-permute-start(bf16[640,128]{1,0:T(8,128)(2,1)S(1)} %shard_map.112.refs_0_.refs_2_), channel_id=1, source_target_pairs={{0,2},{1,3},{2,0},{3,1},{4,6},{5,7},{6,4},{7,5},{8,10},{9,11},{10,... | collective-permute-start | bytes 491528 | tf_op jit(solution)/shard_map/ppermute | solution.py:212
  65.3 7.8 %collective-permute-start.3 = (bf16[640,128]{1,0:T(8,128)(2,1)S(1)}, bf16[640,128]{1,0:T(8,128)(2,1)S(1)}, u32[]{:S(2)}, u32[]{:S(2)}) collective-permute-start(bf16[640,128]{1,0:T(8,128)(2,1)S(1)} %shard_map.112.refs_0_.refs_2_), channel_id=1, source_target_pairs={{0,1},{1,2},{2,3},{3,0},{4,5},{5,6},{6,7},{7,4},{8,9},{9,10},{10,1... | collective-permute-start | bytes 491528 | tf_op jit(solution)/shard_map/ppermute | solution.py:212
  75.4 7.8 %collective-permute-start.12 = (bf16[4,1664,128]{2,1,0:T(8,128)(2,1)S(1)}, bf16[4,1664,128]{2,1,0:T(8,128)(2,1)S(1)}, u32[]{:S(2)}, u32[]{:S(2)}) collective-permute-start(bf16[4,1664,128]{2,1,0:T(8,128)(2,1)S(1)} %get-tuple-element.34), channel_id=1, source_target_pairs={{0,16},{16,0},{32,48},{48,32},{64,80},{80,64},{96,112},{112,96},{1... | collective-permute-start | bytes 5111816 | tf_op jit(solution)/shard_map/ppermute | solution.py:222
  83.5 12.4 %collective-permute-start.13 = (bf16[1664,128]{1,0:T(8,128)(2,1)S(1)}, bf16[1664,128]{1,0:T(8,128)(2,1)S(1)}, u32[]{:S(2)}, u32[]{:S(2)}) collective-permute-start(bf16[1664,128]{1,0:T(8,128)(2,1)S(1)} %get-tuple-element.36), channel_id=1, source_target_pairs={{0,32},{16,48},{32,64},{48,80},{64,96},{80,112},{96,0},{112,16},{1... | collective-permute-start | bytes 1277960 | tf_op jit(solution)/shard_map/ppermute | solution.py:218
  84.8 21.1 %collective-permute-start.14 = (bf16[1664,128]{1,0:T(8,128)(2,1)S(1)}, bf16[1664,128]{1,0:T(8,128)(2,1)S(1)}, u32[]{:S(2)}, u32[]{:S(2)}) collective-permute-start(bf16[1664,128]{1,0:T(8,128)(2,1)S(1)} %get-tuple-element.37), channel_id=1, source_target_pairs={{0,64},{16,80},{32,96},{48,112},{64,0},{80,16},{96,32},{112,48},{1... | collective-permute-start | bytes 1277960 | tf_op jit(solution)/shard_map/ppermute | solution.py:218
  87.2 18.7 %collective-permute-start.15 = (bf16[1664,128]{1,0:T(8,128)(2,1)S(1)}, bf16[1664,128]{1,0:T(8,128)(2,1)S(1)}, u32[]{:S(2)}, u32[]{:S(2)}) collective-permute-start(bf16[1664,128]{1,0:T(8,128)(2,1)S(1)} %get-tuple-element.38), channel_id=1, source_target_pairs={{0,96},{16,112},{32,0},{48,16},{64,32},{80,48},{96,64},{112,80},{1... | collective-permute-start | bytes 1277960 | tf_op jit(solution)/shard_map/ppermute | solution.py:218
  106.1 16.5 %collective-permute-start.25 = (bf16[1408,128]{1,0:T(8,128)(2,1)S(1)}, bf16[1408,128]{1,0:T(8,128)(2,1)S(1)}, u32[]{:S(2)}, u32[]{:S(2)}) collective-permute-start(bf16[1408,128]{1,0:T(8,128)(2,1)S(1)} %get-tuple-element.40), channel_id=1, source_target_pairs={{0,96},{16,112},{32,0},{48,16},{64,32},{80,48},{96,64},{112,80},{1... | collective-permute-start | bytes 1081352 | tf_op jit(solution)/shard_map/ppermute | solution.py:218
  108.9 13.7 %collective-permute-start.24 = (bf16[1408,128]{1,0:T(8,128)(2,1)S(1)}, bf16[1408,128]{1,0:T(8,128)(2,1)S(1)}, u32[]{:S(2)}, u32[]{:S(2)}) collective-permute-start(bf16[1408,128]{1,0:T(8,128)(2,1)S(1)} %get-tuple-element.40), channel_id=1, source_target_pairs={{0,64},{16,80},{32,96},{48,112},{64,0},{80,16},{96,32},{112,48},{1... | collective-permute-start | bytes 1081352 | tf_op jit(solution)/shard_map/ppermute | solution.py:218
  109.1 19.8 %collective-permute-start.23 = (bf16[1408,128]{1,0:T(8,128)(2,1)S(1)}, bf16[1408,128]{1,0:T(8,128)(2,1)S(1)}, u32[]{:S(2)}, u32[]{:S(2)}) collective-permute-start(bf16[1408,128]{1,0:T(8,128)(2,1)S(1)} %get-tuple-element.40), channel_id=1, source_target_pairs={{0,32},{16,48},{32,64},{48,80},{64,96},{80,112},{96,0},{112,16},{1... | collective-permute-start | bytes 1081352 | tf_op jit(solution)/shard_map/ppermute | solution.py:218
  118.4 16.8 %collective-permute-start.21 = (bf16[1024,128]{1,0:T(8,128)(2,1)S(1)}, bf16[1024,128]{1,0:T(8,128)(2,1)S(1)}, u32[]{:S(2)}, u32[]{:S(2)}) collective-permute-start(bf16[1024,128]{1,0:T(8,128)(2,1)S(1)} %shard_map.120), channel_id=1, source_target_pairs={{0,96},{16,112},{32,0},{48,16},{64,32},{80,48},{96,64},{112,80},{1... | collective-permute-start | bytes 786440 | tf_op jit(solution)/shard_map/ppermute | solution.py:218
  120.4 14.8 %collective-permute-start.20 = (bf16[1024,128]{1,0:T(8,128)(2,1)S(1)}, bf16[1024,128]{1,0:T(8,128)(2,1)S(1)}, u32[]{:S(2)}, u32[]{:S(2)}) collective-permute-start(bf16[1024,128]{1,0:T(8,128)(2,1)S(1)} %shard_map.120), channel_id=1, source_target_pairs={{0,64},{16,80},{32,96},{48,112},{64,0},{80,16},{96,32},{112,48},{1... | collective-permute-start | bytes 786440 | tf_op jit(solution)/shard_map/ppermute | solution.py:218
  122.6 16.7 %collective-permute-start.19 = (bf16[1024,128]{1,0:T(8,128)(2,1)S(1)}, bf16[1024,128]{1,0:T(8,128)(2,1)S(1)}, u32[]{:S(2)}, u32[]{:S(2)}) collective-permute-start(bf16[1024,128]{1,0:T(8,128)(2,1)S(1)} %shard_map.120), channel_id=1, source_target_pairs={{0,32},{16,48},{32,64},{48,80},{64,96},{80,112},{96,0},{112,16},{1... | collective-permute-start | bytes 786440 | tf_op jit(solution)/shard_map/ppermute | solution.py:218
  129.0 16.0 %collective-permute-start.26 = (bf16[4,1408,128]{2,1,0:T(8,128)(2,1)S(1)}, bf16[4,1408,128]{2,1,0:T(8,128)(2,1)S(1)}, u32[]{:S(2)}, u32[]{:S(2)}) collective-permute-start(bf16[4,1408,128]{2,1,0:T(8,128)(2,1)S(1)} %pad_maximum_fusion.refs_2_), channel_id=1, source_target_pairs={{0,16},{16,0},{32,48},{48,32},{64,80},{80,64},{96,112},{112,96},{1... | collective-permute-start | bytes 4325384 | tf_op jit(solution)/shard_map/ppermute | solution.py:222
  (22 other events, 127.3 us)
Sparse Core Ops, SparseCore 0:
  30.2 101.3 reduce-scatter.1

commit v5 on v4

v5 whole, which is shorter than its diff:
```python
import jax
import jax.numpy as jnp
from jax import lax
from jax.experimental import pallas as pl
from jax.experimental.pallas import tpu as pltpu
from jax.sharding import PartitionSpec as P

F32 = jnp.float32
BF16 = jnp.bfloat16
SIDE = 128
SMEM = pl.BlockSpec(memory_space=pltpu.SMEM)
VMEM = pl.BlockSpec(memory_space=pltpu.VMEM)
HBM = pl.BlockSpec(memory_space=pl.ANY)
ROWS = (((0,), (0,)), ((), ()))
COLS = (((1,), (1,)), ((), ()))


def lanes(block):
    return pl.ds(pl.multiple_of(block * SIDE, SIDE), SIDE)


def span(block, size):
    return pl.ds(pl.multiple_of(block * size, size), size)


def shape(dims, dtype):
    return jax.ShapeDtypeStruct(dims, dtype)


def call(kernel, outs, smem=(), hbm=(), vmem=(), scratch=(), after=(), mib=8):
    n_in, n_out = len(smem) + len(hbm) + len(vmem), len(outs)

    def body(*refs):
        rest = refs[n_in + len(after) :]
        rest[n_out][0] = 0
        kernel(*refs[:n_in], *rest[:n_out], *rest[n_out + 1 :])

    return pl.pallas_call(
        body,
        out_shape=(*outs, shape((1,), jnp.int32)),
        in_specs=[SMEM] * len(smem) + [HBM] * len(hbm) + [VMEM] * len(vmem) + [SMEM] * len(after),
        out_specs=(VMEM,) * n_out + (SMEM,),
        scratch_shapes=list(scratch),
        cost_estimate=pl.CostEstimate(flops=0, bytes_accessed=0, transcendentals=0),
        compiler_params=pltpu.CompilerParams(vmem_limit_bytes=mib << 20),
    )(*smem, *hbm, *vmem, *after)


class Place:
    def __init__(self, n_f, n_t, n_d):
        self.n_f, self.n_t, self.n_d, self.chips = n_f, n_t, n_d, n_d // 2

    f = property(lambda self: lax.axis_index("fsdp"))
    t = property(lambda self: lax.axis_index("tensor"))
    chip = property(lambda self: lax.axis_index("dp") // 2)
    core = property(lambda self: lax.rem(lax.axis_index("dp"), 2))

    def live(self, counts):
        return counts[self.f * self.n_t + self.t]


def fetch(*pairs_and_sems):
    copies = [pltpu.make_async_copy(src, dst, sem) for src, dst, sem in pairs_and_sems]
    for copy in copies:
        copy.start()
    return copies


def front_kernel(place, tok, left, cot, right, own, s1, s2, s3, tokv, leftv, cotv, rightv, both, sems):
    quarter, r = cotv.shape[1], rightv.shape[0]
    here = pl.ds(pl.multiple_of(place.f * quarter, SIDE), quarter)
    c_tok, c_left, c_cot, c_right = fetch(
        (tok, tokv, sems.at[0]),
        (left.at[:, lanes(place.t)], leftv, sems.at[1]),
        (cot.at[:, here], cotv, sems.at[2]),
        (right, rightv, sems.at[3]),
    )
    c_tok.wait()
    c_left.wait()
    both[:, r:] = jnp.dot(tokv[...], leftv[...], preferred_element_type=F32)
    c_cot.wait()
    c_right.wait()
    both[:, :r] = lax.dot_general(cotv[...], rightv[...], COLS, preferred_element_type=F32)
    rows = own.shape[0]
    own[...] = both[span(place.f, rows), :]
    for k, out in ((1, s1), (2, s2), (3, s3)):
        out[...] = both[span(lax.rem(place.f + k, place.n_f), rows), :].astype(BF16)


def columns_kernel(place, own, g1, g2, g3, back, rank, s1, s2, s3, total):
    r = place.n_t * SIDE
    total[...] = own[...] + g1[...].astype(F32) + g2[...].astype(F32) + g3[...].astype(F32)
    back[...] = total[:, lanes(place.t)]
    low = total[:, r:].astype(BF16)
    rank[...] = low
    for k, out in ((1, s1), (2, s2), (3, s3)):
        out[:, :SIDE] = total[:, lanes(lax.rem(place.t + k, place.n_t))].astype(BF16)
        out[:, SIDE:] = low


def rows_kernel(place, back, rank, g1, g2, g3, out):
    total = back[...]
    out[:, lanes(place.t + 1)] = rank[...]
    for k, g in ((1, g1), (2, g2), (3, g3)):
        total = total + g[:, :SIDE].astype(F32)
        out[:, lanes(lax.rem(place.t - k + place.n_t, place.n_t) + 1)] = g[:, SIDE:]
    out[:, :SIDE] = total.astype(BF16)


def residual_kernel(place, q_blocks, steps, counts, rows, cols, tok, vals, *refs):
    outs, (tokv, valv, acc, sems) = refs[:-4], refs[-4:]
    n_out = len(outs) // len(steps)
    c_tok, c_val = fetch((tok, tokv, sems.at[0]), (vals, valv, sems.at[1]))
    live = place.live(counts)
    c_tok.wait()
    c_val.wait()
    for step in steps:
        acc[...] = jnp.zeros_like(acc)
        first = lax.rem(place.f + step, place.n_f) * q_blocks

        def body(s, carry):
            col = cols[s] - first

            @pl.when((col >= 0) & (col < q_blocks))
            def _():
                acc[:, lanes(col)] += jnp.dot(
                    tokv[:, lanes(rows[s])], valv[s], preferred_element_type=F32
                )

            return carry

        lax.fori_loop(0, live, body, 0)
        row = 0
        for out in outs[:n_out]:
            out[...] = acc[row : row + out.shape[0]].astype(BF16)
            row += out.shape[0]
        outs = outs[n_out:]


PANELS = 8


def blocks_kernel(place, counts, rows, cols, tok, cot, mine, theirs, tokv, panels, sems, tok_sem):
    live = place.live(counts)

    def panel(s):
        slot = lax.rem(s, PANELS)
        return pltpu.make_async_copy(cot.at[:, lanes(cols[s])], panels.at[slot], sems.at[slot])

    def start(s):
        @pl.when(s < live)
        def _():
            panel(s).start()

    (c_tok,) = fetch((tok, tokv, tok_sem))
    for s in range(PANELS - 1):
        start(jnp.int32(s))
    mine[...] = jnp.zeros_like(mine)
    theirs[...] = jnp.zeros_like(theirs)
    per = mine.shape[1] // SIDE
    c_tok.wait()

    def body(s, carry):
        start(s + PANELS - 1)
        panel(s).wait()
        grad = lax.dot_general(
            tokv[:, lanes(rows[s])], panels[lax.rem(s, PANELS)], ROWS, preferred_element_type=F32
        )
        owner = s // per
        j = lax.rem(owner // 2 - place.chip + place.chips, place.chips)
        at = span(lax.rem(s, per), SIDE)
        keep = lax.rem(owner, 2) == place.core

        @pl.when(keep)
        def _():
            mine[j, at] = grad

        @pl.when(jnp.logical_not(keep))
        def _():
            theirs[j, at] = grad.astype(BF16)

        return carry

    lax.fori_loop(0, live, body, 0)


def factors_kernel(
    place, tok, cot, g0, g1, g2, g3, blocks_mine, blocks_theirs, mine, theirs0, theirs1, theirs2, theirs3,
    tokv, cotv, both, left, right, sems,
):
    quarter, n_rows = cotv.shape[1], g0.shape[0]
    here = pl.ds(pl.multiple_of(place.f * quarter, SIDE), quarter)
    c_tok, c_cot = fetch((tok, tokv, sems.at[0]), (cot.at[:, here], cotv, sems.at[1]))
    for k, g in enumerate((g0, g1, g2, g3)):
        both[span(lax.rem(place.f - k + place.n_f, place.n_f), n_rows), :] = g[...]
    n_l = left.shape[0] // place.n_d
    n_r = right.shape[0] // place.n_d
    n_lr = n_l + quarter // SIDE * n_r
    theirs = (theirs0, theirs1, theirs2, theirs3)
    for j in range(place.chips):
        mine[j, n_lr:] = blocks_mine[j]
        theirs[j][n_lr:] = blocks_theirs[j]
    c_tok.wait()
    left[...] = lax.dot_general(both[:, :SIDE], tokv[...], ROWS, preferred_element_type=F32).T
    c_cot.wait()
    right[...] = lax.dot_general(both[:, SIDE:], cotv[...], ROWS, preferred_element_type=F32)
    for j in range(place.chips):
        chip = lax.rem(place.chip + j, place.chips)
        for core, out in ((place.core, mine.at[j]), (1 - place.core, theirs[j])):
            at = chip * 2 + core
            out[:n_l] = left[span(at, n_l), :].astype(out.dtype)
            for p in range(quarter // SIDE):
                out[n_l + p * n_r : n_l + (p + 1) * n_r] = right[
                    span(at, n_r), p * SIDE : (p + 1) * SIDE
                ].astype(out.dtype)


def cores_kernel(mine, got0, got1, got2, got3, own, ahead, behind, near):
    half = own.shape[0] // 2
    got = (got0, got1, got2, got3)
    own[...] = mine[0] + got[0][...].astype(F32)
    far = (mine[2] + got[2][...].astype(F32)).astype(BF16)
    ahead[:half] = far[:half]
    behind[:half] = far[half:]
    ahead[half:] = (mine[1, half:] + got[1][half:].astype(F32)).astype(BF16)
    behind[half:] = (mine[3, :half] + got[3][:half].astype(F32)).astype(BF16)
    near[:half] = mine[1, :half] + got[1][:half].astype(F32)
    near[half:] = mine[3, half:] + got[3][half:].astype(F32)


def relay_kernel(near, from_behind, from_ahead, ahead, behind):
    half = ahead.shape[0]
    ahead[...] = (near[:half].astype(F32) + from_behind[:half].astype(F32)).astype(BF16)
    behind[...] = (near[half:].astype(F32) + from_ahead[:half].astype(F32)).astype(BF16)


def pass_kernel(p1, p3, from_behind, from_ahead, ahead, behind):
    half = from_behind.shape[0]
    ahead[:half] = (p1[:half].astype(F32) + from_behind[...].astype(F32)).astype(BF16)
    ahead[half:] = p1[half:]
    behind[:half] = p3[:half]
    behind[half:] = (p3[half:].astype(F32) + from_ahead[...].astype(F32)).astype(BF16)


def chunk_kernel(own, from_behind, from_ahead, last_behind, last_ahead, left, rest, total):
    half = last_behind.shape[0]
    n_l = left.shape[0]
    total[:half] = own[:half] + from_ahead[half:].astype(F32) + last_behind[...].astype(F32)
    total[half:] = own[half:] + from_behind[half:].astype(F32) + last_ahead[...].astype(F32)
    left[...] = total[:n_l].astype(BF16)
    rest[...] = total[n_l:].astype(BF16)


def stack_kernel(*refs):
    out, row = refs[-1], 0
    for part in refs[:-1]:
        out[row : row + part.shape[0]] = part[...]
        row += part.shape[0]


def second_kernel(left_pair, left_far, rest_behind, rest_ahead, ahead, behind):
    n = left_pair.shape[0]
    half = rest_behind.shape[0] // 2
    for out, piece in ((ahead, rest_behind[:half]), (behind, rest_ahead[half:])):
        out[:n] = left_pair[...]
        out[n : 2 * n] = left_far[...]
        out[2 * n :] = piece


def low_kernel(place, g0, g1, g2, g3, right, p0, out):
    n_rows = g0.shape[0]
    for k, g in enumerate((g0, g1, g2, g3)):
        at = span(lax.rem(place.f - k + place.n_f, place.n_f), n_rows)
        prod = jnp.dot(g[:, SIDE:], right[...], preferred_element_type=F32)
        out[at, :] = prod + p0[at, :].astype(F32)


def finish_kernel(low, from_behind, from_ahead, out):
    out[...] = (low[...] + from_behind[...].astype(F32) + from_ahead[...].astype(F32)).astype(BF16)


def spread_kernel(place, *refs):
    refs, (left, right, blocks) = refs[:-3], refs[-3:]
    n_l = left.shape[0] // place.n_d
    n_r = right.shape[0] // place.n_d
    n_b = blocks.shape[0] // place.n_d
    panels = right.shape[1] // SIDE
    n_rest = panels * n_r + n_b
    n_left = place.n_t * n_l
    t = place.t
    near_t = t + 1 - 2 * lax.rem(t, 2)
    far_t = place.n_t - 1 - t
    order = (t, near_t, far_t, place.n_t - 1 - near_t)
    n = len(refs) // 2
    for core, mine in ((place.core, refs[:n]), (1 - place.core, refs[n:])):
        rest, rest_behind, rest_ahead, pair, far, behind, ahead, left_behind, left_ahead = mine
        for j, whole, lefts in (
            (0, rest, (pair, far)),
            (-1, rest_behind, (behind.at[: n_left // 2], behind.at[n_left // 2 : n_left])),
            (1, rest_ahead, (ahead.at[: n_left // 2], ahead.at[n_left // 2 : n_left])),
            (2, None, (left_behind, left_ahead)),
        ):
            at = lax.rem(place.chip + j + place.chips, place.chips) * 2 + core
            for k in range(place.n_t):
                row = k % 2 * n_l
                left[span(at, n_l), lanes(order[k])] = lefts[k // 2][row : row + n_l]

            def piece(lo, hi):
                if whole is not None:
                    return whole[lo:hi]
                if lo < n_rest // 2:
                    return behind[n_left + lo : n_left + hi]
                base = n_left - n_rest // 2
                return ahead[base + lo : base + hi]

            for p in range(panels):
                right[span(at, n_r), p * SIDE : (p + 1) * SIDE] = piece(p * n_r, (p + 1) * n_r)
            blocks[span(at, n_b)] = piece(panels * n_r, n_rest)


def shift(x, axis, n, k):
    return lax.ppermute(x, axis, [(i, (i + k) % n) for i in range(n)])


def chip_shift(x, n_data, k):
    chips = n_data // 2
    perm = [(2 * a + c, 2 * ((a + k) % chips) + c) for a in range(chips) for c in range(2)]
    return lax.ppermute(x, "dp", perm)


def core_swap(x, n_data):
    return lax.ppermute(x, "dp", [(i, i ^ 1) for i in range(n_data)])


def per_device(
    tokens, cotangent, left_factor, right_factor, block_values, block_rows, block_cols, block_counts
):
    n_f = lax.axis_size("fsdp")
    n_t = lax.axis_size("tensor")
    n_d = lax.axis_size("dp")
    place = Place(n_f, n_t, n_d)
    chips = n_d // 2
    maxb = block_values.shape[0]
    tok_rows, features = tokens.shape
    right = right_factor.reshape(right_factor.shape[0], -1)
    rank_size, quarter = right.shape
    q_blocks = quarter // SIDE
    n_rows = tok_rows // n_f
    width = rank_size + SIDE
    half = tok_rows // 2
    lists = (block_counts, block_rows, block_cols)
    vm, dma = pltpu.VMEM, pltpu.SemaphoreType.DMA

    def bind(kernel, *args):
        return lambda *refs: kernel(place, *args, *refs)

    def over(n, k_shift):
        return [k_shift(k) for k in range(1, n)]

    def residual(steps, outs, after, mib):
        return call(
            bind(residual_kernel, q_blocks, steps),
            outs,
            smem=lists,
            hbm=(tokens, block_values),
            scratch=[
                vm((tok_rows, features), BF16),
                vm((maxb, SIDE, SIDE), BF16),
                vm((tok_rows, quarter), F32),
                dma((2,)),
            ],
            after=after,
            mib=mib,
        )

    part, whole = shape((half, quarter), BF16), shape((tok_rows, quarter), BF16)
    ahead, behind, step = residual((2,), (part, part), (), 56)
    from_behind = shift(ahead, "fsdp", n_f, 1)
    from_ahead = shift(behind, "fsdp", n_f, -1)

    message = shape((n_rows, width), BF16)
    own, *out, step = call(
        bind(front_kernel),
        (shape((n_rows, width), F32),) + (message,) * 3,
        hbm=(tokens, left_factor, cotangent, right),
        scratch=[
            vm((tok_rows, features), BF16),
            vm((features, SIDE), BF16),
            vm((tok_rows, quarter), BF16),
            vm((rank_size, quarter), BF16),
            vm((tok_rows, width), F32),
            dma((4,)),
        ],
        after=(step,),
        mib=52,
    )
    shares = [shift(x, "fsdp", n_f, k + 1) for k, x in enumerate(out)]
    p1, p3, p0, step = residual((1, 3, 0), (whole,) * 3, (step,), 24)

    back, rank, *out, step = call(
        bind(columns_kernel),
        (shape((n_rows, SIDE), F32), shape((n_rows, SIDE), BF16))
        + (shape((n_rows, 2 * SIDE), BF16),) * 3,
        vmem=(own, *shares),
        scratch=[vm((n_rows, width), F32)],
        after=(step,),
    )
    shares = [shift(x, "tensor", n_t, k + 1) for k, x in enumerate(out)]

    n_b = maxb // n_d * SIDE
    blocks_mine, blocks_theirs, step = call(
        bind(blocks_kernel),
        (shape((chips, n_b, SIDE), F32), shape((chips, n_b, SIDE), BF16)),
        smem=lists,
        hbm=(tokens, cotangent),
        scratch=[
            vm((tok_rows, features), BF16),
            vm((PANELS, tok_rows, SIDE), BF16),
            dma((PANELS,)),
            dma,
        ],
        after=(step,),
        mib=48,
    )

    rows, step = call(bind(rows_kernel), (message,), vmem=(back, rank, *shares), after=(step,))
    gathered = [rows] + over(n_f, lambda k: shift(rows, "fsdp", n_f, k))

    ahead, behind, step = call(
        pass_kernel, (whole, whole), vmem=(p1, p3, from_behind, from_ahead), after=(step,), mib=16
    )
    last_behind = shift(ahead, "fsdp", n_f, 1)
    last_ahead = shift(behind, "fsdp", n_f, -1)

    n_l = features // n_d
    n_r = rank_size // n_d
    n_rest = q_blocks * n_r + n_b
    n_all = n_l + n_rest
    chunk = shape((n_all, SIDE), BF16)
    mine, *theirs, step = call(
        bind(factors_kernel),
        (shape((chips, n_all, SIDE), F32),) + (chunk,) * chips,
        hbm=(tokens, cotangent),
        vmem=(*gathered, blocks_mine, blocks_theirs),
        scratch=[
            vm((tok_rows, features), BF16),
            vm((tok_rows, quarter), BF16),
            vm((tok_rows, width), BF16),
            vm((features, SIDE), F32),
            vm((rank_size, quarter), F32),
            dma((2,)),
        ],
        after=(step,),
        mib=36,
    )
    got = [core_swap(x, n_d) for x in theirs]
    own, c_ahead, c_behind, c_near, step = call(
        cores_kernel,
        (shape((n_all, SIDE), F32), chunk, chunk, shape((n_all, SIDE), F32)),
        vmem=(mine, *got),
        mib=16,
    )
    c_from_behind = chip_shift(c_ahead, n_d, 1)
    c_from_ahead = chip_shift(c_behind, n_d, -1)
    low, step = call(
        bind(low_kernel),
        (shape((tok_rows, quarter), F32),),
        vmem=(*gathered, right, p0),
        after=(step,),
        mib=20,
    )
    c_ahead, c_behind, step = call(
        relay_kernel,
        (shape((n_all // 2, SIDE), BF16),) * 2,
        vmem=(c_near, c_from_behind, c_from_ahead),
        after=(step,),
    )
    c_last_behind = chip_shift(c_ahead, n_d, 1)
    c_last_ahead = chip_shift(c_behind, n_d, -1)
    left, rest, step = call(
        chunk_kernel,
        (shape((n_l, SIDE), BF16), shape((n_rest, SIDE), BF16)),
        vmem=(own, c_from_behind, c_from_ahead, c_last_behind, c_last_ahead),
        scratch=[vm((n_all, SIDE), F32)],
    )

    rest_behind = chip_shift(rest, n_d, 1)
    rest_ahead = chip_shift(rest, n_d, -1)
    left_near = lax.ppermute(left, "tensor", [(i, i ^ 1) for i in range(n_t)])
    left_pair, step = call(
        stack_kernel, (shape((2 * n_l, SIDE), BF16),), vmem=(left, left_near)
    )
    left_far = lax.ppermute(left_pair, "tensor", [(i, n_t - 1 - i) for i in range(n_t)])

    n_msg = n_t * n_l + n_rest // 2
    c_ahead, c_behind, step = call(
        second_kernel,
        (shape((n_msg, SIDE), BF16),) * 2,
        vmem=(left_pair, left_far, rest_behind, rest_ahead),
    )
    c_from_behind = chip_shift(c_ahead, n_d, 1)
    c_from_ahead = chip_shift(c_behind, n_d, -1)
    n_left = n_t * n_l
    left_behind = chip_shift(c_from_behind[: n_left // 2], n_d, 1)
    left_ahead = chip_shift(c_from_ahead[n_left // 2 : n_left], n_d, -1)
    ours = (
        rest, rest_behind, rest_ahead, left_pair, left_far,
        c_from_behind, c_from_ahead, left_behind, left_ahead,
    )
    partner = [core_swap(x, n_d) for x in ours]

    out_left, out_right, out_blocks, step = call(
        bind(spread_kernel),
        (
            shape((features, rank_size), BF16),
            shape((rank_size, quarter), BF16),
            shape((maxb * SIDE, SIDE), BF16),
        ),
        vmem=(*ours, *partner),
        mib=14,
    )
    mixed, _ = call(
        finish_kernel, (whole,), vmem=(low, last_behind, last_ahead), mib=12
    )
    return (
        mixed.reshape(tok_rows, 1, quarter),
        out_left,
        out_right.reshape(right_factor.shape),
        out_blocks.reshape(maxb, SIDE, SIDE),
    )


def solution(mesh):
    return jax.shard_map(
        per_device,
        mesh=mesh,
        in_specs=(
            P("dp", "fsdp"),
            P("dp", "tensor"),
            P("fsdp", None),
            P(None, "tensor", "fsdp"),
            P(("fsdp", "tensor"), None, None),
            P(("fsdp", "tensor")),
            P(("fsdp", "tensor")),
            P(),
        ),
        out_specs=(
            P("dp", "tensor", "fsdp"),
            P("fsdp", None),
            P(None, "tensor", "fsdp"),
            P(("fsdp", "tensor"), None, None),
        ),
        check_vma=False,
    )
```

time: 161 us -> 149 us (0.925)
  local copies, waits for them, and re-layouts: 25 us -> 0.05 us
  starting transfers between devices: 35.3 us -> 57.3 us
  between operations: 14.2 us -> 1.1 us
  Pallas kernels: 34.3 us -> 43 us
  waiting for transfers between devices: 51.1 us -> 47.1 us
    unnamed x36 -> x12, local copies, waits for them, and re-layouts: 25 us -> 0.03 us
    ppermute x9 -> x10, waiting for transfers between devices: 32.8 us -> 14.4 us  [chip_shift(): return lax.ppermute(x, 'dp', perm)]
    ppermute x15 -> x13, waiting for transfers between devices: 15.1 us -> 25.6 us  [shift(): return lax.ppermute(x, axis, [(i, (i + k) % n) for i in range(n)])]
    ppermute x3 -> x13, starting transfers between devices: 6.89 us -> 16.9 us  [core_swap(): return lax.ppermute(x, 'dp', [(i, i ^ 1) for i in range(n_data)])]
    pallas_call x11 -> x16, Pallas kernels: 34.3 us -> 43 us  [call(): pl.pallas_call(body, out_shape=(*outs, shape((1,), jnp.int32)), in_specs=...]
    ppermute x0 -> x2, waiting for transfers between devices: none -> 6.06 us  [the longest x1 3.41 us: per_device(): left_near = lax.ppermute(left, 'tensor', [(i, i ^ 1) for i in range(n_t)])]
    ppermute x15 -> x13, starting transfers between devices: 16.1 us -> 21.4 us  [shift(): return lax.ppermute(x, axis, [(i, (i + k) % n) for i in range(n)])]
    ppermute x0 -> x2, starting transfers between devices: none -> 4.24 us  [the longest x1 4.23 us: per_device(): lax.ppermute(left_pair, 'tensor', [(i, n_t - 1 - i) for i in range(n_t)])]
  transfers between devices with their start and end apart: 28 -> 38, of which waited for: 15 -> 12; matrix products, arithmetic and copies ran while one was open for 0% -> 0% of each run, Pallas kernels for 12% -> 20%
where the time goes in v5:
time: 149 us
  starting transfers between devices  57.3 us (38%)
  waiting for transfers between devices  47.1 us (32%)
  Pallas kernels  43 us (29%)
    pallas_call x16, Pallas kernels, call(): pl.pallas_call(body, out_shape=(*outs, shape((1,), jnp.int32)), in_specs=...  43 us
    ppermute x13, waiting for transfers between devices, shift(): return lax.ppermute(x, axis, [(i, (i + k) % n) for i in range(n)])  25.6 us
    ppermute x13, starting transfers between devices, shift(): return lax.ppermute(x, axis, [(i, (i + k) % n) for i in range(n)])  21.4 us
    ppermute x13, starting transfers between devices, core_swap(): return lax.ppermute(x, 'dp', [(i, i ^ 1) for i in range(n_data)])  16.9 us
    ppermute x10, starting transfers between devices, chip_shift(): return lax.ppermute(x, 'dp', perm)  14.8 us
    ppermute x10, waiting for transfers between devices, chip_shift(): return lax.ppermute(x, 'dp', perm)  14.4 us
    ppermute x1, starting transfers between devices, per_device(): lax.ppermute(left_pair, 'tensor', [(i, n_t - 1 - i) for i in range(n_t)])  4.23 us
    ppermute x1, waiting for transfers between devices, per_device(): left_near = lax.ppermute(left, 'tensor', [(i, i ^ 1) for i in range(n_t)])  3.41 us
  transfers between devices with their start and end apart: 38, of which 12 were waited for; matrix products, arithmetic and copies ran while one was open for 0% of the time, Pallas kernels for 20%

profile of v5, /device:TPU:1, one launch (start us, length us, event | category | flops | bytes accessed | tf_op | source)
XLA Modules:
  0.0 148.5 jit_solution(12757911946651607666)
XLA Ops:
  0.6 5.0 %shard_map.111 = (bf16[320,1792]{1,0:T(8,128)(2,1)}, bf16[320,1792]{1,0:T(8,128)(2,1)}, s32[1]{0:T(128)}) custom-call(s32[16]{0:T(128)} %refs_0_.8, s32[32]{0:T(128)} %refs_1_.8, s32[32]{0:T(128)} %refs_2_.7, bf16[640,2048]{1,0:T(8,128)(2,1)} %refs_0_.9, bf16[32,128,128]{2,1,0:T(8,128)(2,1)} %refs_4_.4), custom_call_target="tpu_custom_call" | custom-call | tf_op jit(solution)/shard_map/pallas_call | solution.py:38
  5.7 3.1 %collective-permute-start.9 = (bf16[320,1792]{1,0:T(8,128)(2,1)}, bf16[320,1792]{1,0:T(8,128)(2,1)S(1)}, u32[]{:S(2)}, u32[]{:S(2)}) collective-permute-start(bf16[320,1792]{1,0:T(8,128)(2,1)} %get-tuple-element.73), channel_id=1, source_target_pairs={{0,4},{4,8},{8,12},{12,0},{1,5},{5,9},{9,13},{13,1},{2,6},{6,10},{... | collective-permute-start | bytes 3440648 | tf_op jit(solution)/shard_map/ppermute | solution.py:322
  8.9 6.7 %shard_map.112 = (f32[160,640]{1,0:T(8,128)S(1)}, bf16[160,640]{1,0:T(8,128)(2,1)S(1)}, bf16[160,640]{1,0:T(8,128)(2,1)S(1)}, bf16[160,640]{1,0:T(8,128)(2,1)S(1)}, s32[1]{0:T(128)}) custom-call(bf16[640,2048]{1,0:T(8,128)(2,1)} %refs_0_.9, bf16[2048,512]{1,0:T(8,128)(2,1)} %refs_1_.6, bf16[640,7168]{1,0:T(8,128)(2,1)} %refs_1_.9, ...), custom_call_target="tpu_custom_call" | custom-call | tf_op jit(solution)/shard_map/pallas_call | solution.py:38
  20.2 5.3 %shard_map.113 = (bf16[640,1792]{1,0:T(8,128)(2,1)S(1)}, bf16[640,1792]{1,0:T(8,128)(2,1)S(1)}, bf16[640,1792]{1,0:T(8,128)(2,1)S(1)}, s32[1]{0:T(128)}) custom-call(s32[16]{0:T(128)S(1)} %copy-done.3, s32[32]{0:T(128)S(1)} %copy-done.4, s32[32]{0:T(128)S(1)} %copy-done.5, bf16[640,2048]{1,0:T(8,128)(2,1)S(1)} %copy-done, ...), custom_call_target="tpu_custom_call" | custom-call | tf_op jit(solution)/shard_map/pallas_call | solution.py:38
  25.4 12.3 %collective-permute-done.refs_1_ = bf16[160,640]{1,0:T(8,128)(2,1)S(1)} collective-permute-done((bf16[160,640]{1,0:T(8,128)(2,1)S(1)}, bf16[160,640]{1,0:T(8,128)(2,1)S(1)}, u32[]{:S(2)}, u32[]{:S(2)}) %collective-permute-start) | collective-permute-done | bytes 204832 | tf_op jit(solution)/shard_map/ppermute | solution.py:322
  37.7 5.9 %collective-permute-done.1.refs_2_ = bf16[160,640]{1,0:T(8,128)(2,1)S(1)} collective-permute-done((bf16[160,640]{1,0:T(8,128)(2,1)S(1)}, bf16[160,640]{1,0:T(8,128)(2,1)S(1)}, u32[]{:S(2)}, u32[]{:S(2)}) %collective-permute-start.1) | collective-permute-done | bytes 204832 | tf_op jit(solution)/shard_map/ppermute | solution.py:322
  47.0 3.8 %collective-permute-start.4 = (bf16[160,256]{1,0:T(8,128)(2,1)S(1)}, bf16[160,256]{1,0:T(8,128)(2,1)S(1)}, u32[]{:S(2)}, u32[]{:S(2)}) collective-permute-start(bf16[160,256]{1,0:T(8,128)(2,1)S(1)} %get-tuple-element.63), channel_id=1, source_target_pairs={{0,2},{1,3},{2,0},{3,1},{4,6},{5,7},{6,4},{7,5},{8,10},{9,11},{10,... | collective-permute-start | bytes 245768 | tf_op jit(solution)/shard_map/ppermute | solution.py:322
  51.6 6.0 %shard_map.115 = (f32[4,512,128]{2,1,0:T(8,128)S(1)}, bf16[4,512,128]{2,1,0:T(8,128)(2,1)S(1)}, s32[1]{0:T(128)}) custom-call(s32[16]{0:T(128)S(1)} %copy-done.3, s32[32]{0:T(128)S(1)} %copy-done.4, s32[32]{0:T(128)S(1)} %copy-done.5, bf16[640,2048]{1,0:T(8,128)(2,1)S(1)} %copy-done, bf16[640,7168]{1,0:T(8,128)(2,1)} %refs_1_.9, s32[1]{0:T(128)} %get-tuple-element.65.refs_5_), custom_call_target="tpu_custom_call" | custom-call | tf_op jit(solution)/shard_map/pallas_call | solution.py:38
  59.0 4.1 %collective-permute-start.7 = (bf16[160,640]{1,0:T(8,128)(2,1)S(1)}, bf16[160,640]{1,0:T(8,128)(2,1)S(1)}, u32[]{:S(2)}, u32[]{:S(2)}) collective-permute-start(bf16[160,640]{1,0:T(8,128)(2,1)S(1)} %get-tuple-element.67.refs_2_.refs_0_), channel_id=1, source_target_pairs={{0,8},{4,12},{8,0},{12,4},{1,9},{5,13},{9,1},{13,5},{2,10},{6,14},... | collective-permute-start | bytes 614408 | tf_op jit(solution)/shard_map/ppermute | solution.py:322
  66.2 5.5 %collective-permute-done.6.refs_3_.refs_1_ = bf16[160,640]{1,0:T(8,128)(2,1)S(1)} collective-permute-done((bf16[160,640]{1,0:T(8,128)(2,1)S(1)}, bf16[160,640]{1,0:T(8,128)(2,1)S(1)}, u32[]{:S(2)}, u32[]{:S(2)}) %collective-permute-start.6) | collective-permute-done | bytes 204832 | tf_op jit(solution)/shard_map/ppermute | solution.py:322
  71.6 4.8 %shard_map.118 = (f32[4,1664,128]{2,1,0:T(8,128)S(1)}, bf16[1664,128]{1,0:T(8,128)(2,1)S(1)}, bf16[1664,128]{1,0:T(8,128)(2,1)S(1)}, bf16[1664,128]{1,0:T(8,128)...) custom-call(bf16[640,2048]{1,0:T(8,128)(2,1)S(1)} %copy-done, bf16[640,7168]{1,0:T(8,128)(2,1)} %refs_1_.9, ...), custom_call_target="tpu_custom_call" | custom-call | tf_op jit(solution)/shard_map/pallas_call | solution.py:38
  76.5 2.4 %collective-permute-start.11 = (bf16[1664,128]{1,0:T(8,128)(2,1)S(1)}, bf16[1664,128]{1,0:T(8,128)(2,1)S(1)}, u32[]{:S(2)}, u32[]{:S(2)}) collective-permute-start(bf16[1664,128]{1,0:T(8,128)(2,1)S(1)} %get-tuple-element.78), channel_id=1, source_target_pairs={{0,16},{16,0},{32,48},{48,32},{64,80},{80,64},{96,112},{112,96},{1... | collective-permute-start | bytes 1277960 | tf_op jit(solution)/shard_map/ppermute | solution.py:332
  85.7 2.5 %shard_map.120 = (f32[640,1792]{1,0:T(8,128)S(1)}, s32[1]{0:T(128)}) custom-call(bf16[160,640]{1,0:T(8,128)(2,1)S(1)} %get-tuple-element.67.refs_2_.refs_0_, bf16[160,640]{1,0:T(8,128)(2,1)S(1)} %collective-permute-done.6.refs_3_.refs_1_, bf16[160,640]{1,0:T(8,128)(2,1)S(1)} %collective-permute-done.7.refs_4_.refs_2_, ...), custom_call_target="tpu_custom_call" | custom-call | tf_op jit(solution)/shard_map/pallas_call | solution.py:38
  88.3 6.3 %collective-permute-done.17.refs_1_ = bf16[1664,128]{1,0:T(8,128)(2,1)S(1)} collective-permute-done((bf16[1664,128]{1,0:T(8,128)(2,1)S(1)}, bf16[1664,128]{1,0:T(8,128)(2,1)S(1)}, u32[]{:S(2)}, u32[]{:S(2)}) %collective-permute-start.17) | collective-permute-done | bytes 426016 | tf_op jit(solution)/shard_map/ppermute | solution.py:328
  98.6 3.5 %collective-permute-done.19.refs_3_ = bf16[832,128]{1,0:T(8,128)(2,1)S(1)} collective-permute-done((bf16[832,128]{1,0:T(8,128)(2,1)S(1)}, bf16[832,128]{1,0:T(8,128)(2,1)S(1)}, u32[]{:S(2)}, u32[]{:S(2)}) %collective-permute-start.19) | collective-permute-done | bytes 213024 | tf_op jit(solution)/shard_map/ppermute | solution.py:328
  102.7 2.7 %collective-permute-start.22 = (bf16[1408,128]{1,0:T(8,128)(2,1)S(1)}, bf16[1408,128]{1,0:T(8,128)(2,1)S(1)}, u32[]{:S(2)}, u32[]{:S(2)}) collective-permute-start(bf16[1408,128]{1,0:T(8,128)(2,1)S(1)} %get-tuple-element.94.refs_0_), channel_id=1, source_target_pairs={{0,96},{16,112},{32,0},{48,16},{64,32},{80,48},{96,64},{112,80},{1... | collective-permute-start | bytes 1081352 | tf_op jit(solution)/shard_map/ppermute | solution.py:328
  105.4 3.4 %collective-permute-done.23.refs_1_ = bf16[256,128]{1,0:T(8,128)(2,1)S(1)} collective-permute-done((bf16[256,128]{1,0:T(8,128)(2,1)S(1)}, bf16[256,128]{1,0:T(8,128)(2,1)S(1)}, u32[]{:S(2)}, u32[]{:S(2)}) %collective-permute-start.23) | collective-permute-done | bytes 65568 | tf_op jit(solution)/shard_map/ppermute | solution.py:489
  109.4 4.2 %collective-permute-start.24 = (bf16[512,128]{1,0:T(8,128)(2,1)S(1)}, bf16[512,128]{1,0:T(8,128)(2,1)S(1)}, u32[]{:S(2)}, u32[]{:S(2)}) collective-permute-start(bf16[512,128]{1,0:T(8,128)(2,1)S(1)} %get-tuple-element.96.refs_0_.refs_3_), channel_id=1, source_target_pairs={{0,3},{1,2},{2,1},{3,0},{4,7},{5,6},{6,5},{7,4},{8,11},{9,10},{10,... | collective-permute-start | bytes 393224 | tf_op jit(solution)/shard_map/ppermute | solution.py:493
  113.6 2.7 %collective-permute-done.24.refs_1_.refs_4_ = bf16[512,128]{1,0:T(8,128)(2,1)S(1)} collective-permute-done((bf16[512,128]{1,0:T(8,128)(2,1)S(1)}, bf16[512,128]{1,0:T(8,128)(2,1)S(1)}, u32[]{:S(2)}, u32[]{:S(2)}) %collective-permute-start.24) | collective-permute-done | bytes 131104 | tf_op jit(solution)/shard_map/ppermute | solution.py:493
  117.0 5.0 %collective-permute-start.32 = (bf16[512,128]{1,0:T(8,128)(2,1)S(1)}, bf16[512,128]{1,0:T(8,128)(2,1)S(1)}, u32[]{:S(2)}, u32[]{:S(2)}) collective-permute-start(bf16[512,128]{1,0:T(8,128)(2,1)S(1)} %get-tuple-element.96.refs_0_.refs_3_), channel_id=1, source_target_pairs={{0,16},{16,0},{32,48},{48,32},{64,80},{80,64},{96,112},{112,96},{1... | collective-permute-start | bytes 393224 | tf_op jit(solution)/shard_map/ppermute | solution.py:332
  121.9 2.8 %collective-permute-start.26 = (bf16[1728,128]{1,0:T(8,128)(2,1)S(1)}, bf16[1728,128]{1,0:T(8,128)(2,1)S(1)}, u32[]{:S(2)}, u32[]{:S(2)}) collective-permute-start(bf16[1728,128]{1,0:T(8,128)(2,1)S(1)} %get-tuple-element.98), channel_id=1, source_target_pairs={{0,96},{16,112},{32,0},{48,16},{64,32},{80,48},{96,64},{112,80},{1... | collective-permute-start | bytes 1327112 | tf_op jit(solution)/shard_map/ppermute | solution.py:328
  126.5 4.8 %collective-permute-start.31 = (bf16[1408,128]{1,0:T(8,128)(2,1)S(1)}, bf16[1408,128]{1,0:T(8,128)(2,1)S(1)}, u32[]{:S(2)}, u32[]{:S(2)}) collective-permute-start(bf16[1408,128]{1,0:T(8,128)(2,1)S(1)} %collective-permute-done.22.refs_3_.refs_2_), channel_id=1, source_target_pairs={{0,16},{16,0},{32,48},{48,32},{64,80},{80,64},{96,112},{112,96},{1... | collective-permute-start | bytes 1081352 | tf_op jit(solution)/shard_map/ppermute | solution.py:332
  131.2 3.1 %collective-permute-done.26.refs_6_ = bf16[1728,128]{1,0:T(8,128)(2,1)S(1)} collective-permute-done((bf16[1728,128]{1,0:T(8,128)(2,1)S(1)}, bf16[1728,128]{1,0:T(8,128)(2,1)S(1)}, u32[]{:S(2)}, u32[]{:S(2)}) %collective-permute-start.26) | collective-permute-done | bytes 442400 | tf_op jit(solution)/shard_map/ppermute | solution.py:328
  145.3 3.1 %shard_map.126 = (bf16[2048,512]{1,0:T(8,128)(2,1)}, bf16[512,1792]{1,0:T(8,128)(2,1)}, bf16[4096,128]{1,0:T(8,128)(2,1)}, s32[1]{0:T(128)}) custom-call(bf16[1408,128]{1,0:T(8,128)(2,1)S(1)} %get-tuple-element.94.refs_0_, bf16[1408,128]{1,0:T(8,128)(2,1)S(1)} %collective-permute-done.21.refs_2_.refs_1_, ...), custom_call_target="tpu_custom_call" | custom-call | tf_op jit(solution)/shard_map/pallas_call | solution.py:38
  (82 shorter events, 38.5 us)
Async XLA Ops:
  5.7 57.4 %collective-permute-start.9 = (bf16[320,1792]{1,0:T(8,128)(2,1)}, bf16[320,1792]{1,0:T(8,128)(2,1)S(1)}, u32[]{:S(2)}, u32[]{:S(2)}) collective-permute-start(bf16[320,1792]{1,0:T(8,128)(2,1)} %get-tuple-element.73), channel_id=1, source_target_pairs={{0,4},{4,8},{8,12},{12,0},{1,5},{5,9},{9,13},{13,1},{2,6},{6,10},{... | collective-permute-start | bytes 3440648 | tf_op jit(solution)/shard_map/ppermute | solution.py:322
  8.7 54.3 %collective-permute-start.10 = (bf16[320,1792]{1,0:T(8,128)(2,1)}, bf16[320,1792]{1,0:T(8,128)(2,1)S(1)}, u32[]{:S(2)}, u32[]{:S(2)}) collective-permute-start(bf16[320,1792]{1,0:T(8,128)(2,1)} %get-tuple-element.74), channel_id=1, source_target_pairs={{0,12},{4,0},{8,4},{12,8},{1,13},{5,1},{9,5},{13,9},{2,14},{6,2},{... | collective-permute-start | bytes 3440648 | tf_op jit(solution)/shard_map/ppermute | solution.py:322
  15.7 22.1 %collective-permute-start = (bf16[160,640]{1,0:T(8,128)(2,1)S(1)}, bf16[160,640]{1,0:T(8,128)(2,1)S(1)}, u32[]{:S(2)}, u32[]{:S(2)}) collective-permute-start(bf16[160,640]{1,0:T(8,128)(2,1)S(1)} %get-tuple-element.55), channel_id=1, source_target_pairs={{0,4},{4,8},{8,12},{12,0},{1,5},{5,9},{9,13},{13,1},{2,6},{6,10},{... | collective-permute-start | bytes 614408 | tf_op jit(solution)/shard_map/ppermute | solution.py:322
  17.0 26.7 %collective-permute-start.1 = (bf16[160,640]{1,0:T(8,128)(2,1)S(1)}, bf16[160,640]{1,0:T(8,128)(2,1)S(1)}, u32[]{:S(2)}, u32[]{:S(2)}) collective-permute-start(bf16[160,640]{1,0:T(8,128)(2,1)S(1)} %get-tuple-element.56), channel_id=1, source_target_pairs={{0,8},{4,12},{8,0},{12,4},{1,9},{5,13},{9,1},{13,5},{2,10},{6,14},... | collective-permute-start | bytes 614408 | tf_op jit(solution)/shard_map/ppermute | solution.py:322
  18.3 25.4 %collective-permute-start.2 = (bf16[160,640]{1,0:T(8,128)(2,1)S(1)}, bf16[160,640]{1,0:T(8,128)(2,1)S(1)}, u32[]{:S(2)}, u32[]{:S(2)}) collective-permute-start(bf16[160,640]{1,0:T(8,128)(2,1)S(1)} %get-tuple-element.57), channel_id=1, source_target_pairs={{0,12},{4,0},{8,4},{12,8},{1,13},{5,1},{9,5},{13,9},{2,14},{6,2},{... | collective-permute-start | bytes 614408 | tf_op jit(solution)/shard_map/ppermute | solution.py:322
  44.8 12.8 %collective-permute-start.3 = (bf16[160,256]{1,0:T(8,128)(2,1)S(1)}, bf16[160,256]{1,0:T(8,128)(2,1)S(1)}, u32[]{:S(2)}, u32[]{:S(2)}) collective-permute-start(bf16[160,256]{1,0:T(8,128)(2,1)S(1)} %get-tuple-element.62), channel_id=1, source_target_pairs={{0,1},{1,2},{2,3},{3,0},{4,5},{5,6},{6,7},{7,4},{8,9},{9,10},{10,1... | collective-permute-start | bytes 245768 | tf_op jit(solution)/shard_map/ppermute | solution.py:322
  47.0 10.7 %collective-permute-start.4 = (bf16[160,256]{1,0:T(8,128)(2,1)S(1)}, bf16[160,256]{1,0:T(8,128)(2,1)S(1)}, u32[]{:S(2)}, u32[]{:S(2)}) collective-permute-start(bf16[160,256]{1,0:T(8,128)(2,1)S(1)} %get-tuple-element.63), channel_id=1, source_target_pairs={{0,2},{1,3},{2,0},{3,1},{4,6},{5,7},{6,4},{7,5},{8,10},{9,11},{10,... | collective-permute-start | bytes 245768 | tf_op jit(solution)/shard_map/ppermute | solution.py:322
  50.8 6.9 %collective-permute-start.5 = (bf16[160,256]{1,0:T(8,128)(2,1)S(1)}, bf16[160,256]{1,0:T(8,128)(2,1)S(1)}, u32[]{:S(2)}, u32[]{:S(2)}) collective-permute-start(bf16[160,256]{1,0:T(8,128)(2,1)S(1)} %get-tuple-element.64), channel_id=1, source_target_pairs={{0,3},{1,0},{2,1},{3,2},{4,7},{5,4},{6,5},{7,6},{8,11},{9,8},{10,9... | collective-permute-start | bytes 245768 | tf_op jit(solution)/shard_map/ppermute | solution.py:322
  59.0 7.2 %collective-permute-start.7 = (bf16[160,640]{1,0:T(8,128)(2,1)S(1)}, bf16[160,640]{1,0:T(8,128)(2,1)S(1)}, u32[]{:S(2)}, u32[]{:S(2)}) collective-permute-start(bf16[160,640]{1,0:T(8,128)(2,1)S(1)} %get-tuple-element.67.refs_2_.refs_0_), channel_id=1, source_target_pairs={{0,8},{4,12},{8,0},{12,4},{1,9},{5,13},{9,1},{13,5},{2,10},{6,14},... | collective-permute-start | bytes 614408 | tf_op jit(solution)/shard_map/ppermute | solution.py:322
  63.0 8.6 %collective-permute-start.6 = (bf16[160,640]{1,0:T(8,128)(2,1)S(1)}, bf16[160,640]{1,0:T(8,128)(2,1)S(1)}, u32[]{:S(2)}, u32[]{:S(2)}) collective-permute-start(bf16[160,640]{1,0:T(8,128)(2,1)S(1)} %get-tuple-element.67.refs_2_.refs_0_), channel_id=1, source_target_pairs={{0,4},{4,8},{8,12},{12,0},{1,5},{5,9},{9,13},{13,1},{2,6},{6,10},{... | collective-permute-start | bytes 614408 | tf_op jit(solution)/shard_map/ppermute | solution.py:322
  79.4 63.1 %collective-permute-start.15 = (bf16[640,1792]{1,0:T(8,128)(2,1)S(1)}, bf16[640,1792]{1,0:T(8,128)(2,1)S(1)}, u32[]{:S(2)}, u32[]{:S(2)}) collective-permute-start(bf16[640,1792]{1,0:T(8,128)(2,1)S(1)} %get-tuple-element.84), channel_id=1, source_target_pairs={{0,4},{4,8},{8,12},{12,0},{1,5},{5,9},{9,13},{13,1},{2,6},{6,10},{... | collective-permute-start | bytes 6881288 | tf_op jit(solution)/shard_map/ppermute | solution.py:322
  80.5 62.2 %collective-permute-start.16 = (bf16[640,1792]{1,0:T(8,128)(2,1)S(1)}, bf16[640,1792]{1,0:T(8,128)(2,1)S(1)}, u32[]{:S(2)}, u32[]{:S(2)}) collective-permute-start(bf16[640,1792]{1,0:T(8,128)(2,1)S(1)} %get-tuple-element.85), channel_id=1, source_target_pairs={{0,12},{4,0},{8,4},{12,8},{1,13},{5,1},{9,5},{13,9},{2,14},{6,2},{... | collective-permute-start | bytes 6881288 | tf_op jit(solution)/shard_map/ppermute | solution.py:322
  83.0 11.6 %collective-permute-start.17 = (bf16[1664,128]{1,0:T(8,128)(2,1)S(1)}, bf16[1664,128]{1,0:T(8,128)(2,1)S(1)}, u32[]{:S(2)}, u32[]{:S(2)}) collective-permute-start(bf16[1664,128]{1,0:T(8,128)(2,1)S(1)} %get-tuple-element.88), channel_id=1, source_target_pairs={{0,32},{16,48},{32,64},{48,80},{64,96},{80,112},{96,0},{112,16},{1... | collective-permute-start | bytes 1277960 | tf_op jit(solution)/shard_map/ppermute | solution.py:328
  84.2 10.3 %collective-permute-start.18 = (bf16[1664,128]{1,0:T(8,128)(2,1)S(1)}, bf16[1664,128]{1,0:T(8,128)(2,1)S(1)}, u32[]{:S(2)}, u32[]{:S(2)}) collective-permute-start(bf16[1664,128]{1,0:T(8,128)(2,1)S(1)} %get-tuple-element.89), channel_id=1, source_target_pairs={{0,96},{16,112},{32,0},{48,16},{64,32},{80,48},{96,64},{112,80},{1... | collective-permute-start | bytes 1277960 | tf_op jit(solution)/shard_map/ppermute | solution.py:328
  102.7 13.6 %collective-permute-start.22 = (bf16[1408,128]{1,0:T(8,128)(2,1)S(1)}, bf16[1408,128]{1,0:T(8,128)(2,1)S(1)}, u32[]{:S(2)}, u32[]{:S(2)}) collective-permute-start(bf16[1408,128]{1,0:T(8,128)(2,1)S(1)} %get-tuple-element.94.refs_0_), channel_id=1, source_target_pairs={{0,96},{16,112},{32,0},{48,16},{64,32},{80,48},{96,64},{112,80},{1... | collective-permute-start | bytes 1081352 | tf_op jit(solution)/shard_map/ppermute | solution.py:328
  105.4 10.8 %collective-permute-start.21 = (bf16[1408,128]{1,0:T(8,128)(2,1)S(1)}, bf16[1408,128]{1,0:T(8,128)(2,1)S(1)}, u32[]{:S(2)}, u32[]{:S(2)}) collective-permute-start(bf16[1408,128]{1,0:T(8,128)(2,1)S(1)} %get-tuple-element.94.refs_0_), channel_id=1, source_target_pairs={{0,32},{16,48},{32,64},{48,80},{64,96},{80,112},{96,0},{112,16},{1... | collective-permute-start | bytes 1081352 | tf_op jit(solution)/shard_map/ppermute | solution.py:328
  109.4 6.9 %collective-permute-start.24 = (bf16[512,128]{1,0:T(8,128)(2,1)S(1)}, bf16[512,128]{1,0:T(8,128)(2,1)S(1)}, u32[]{:S(2)}, u32[]{:S(2)}) collective-permute-start(bf16[512,128]{1,0:T(8,128)(2,1)S(1)} %get-tuple-element.96.refs_0_.refs_3_), channel_id=1, source_target_pairs={{0,3},{1,2},{2,1},{3,0},{4,7},{5,6},{6,5},{7,4},{8,11},{9,10},{10,... | collective-permute-start | bytes 393224 | tf_op jit(solution)/shard_map/ppermute | solution.py:493
  116.9 9.6 %collective-permute-start.25 = (bf16[1728,128]{1,0:T(8,128)(2,1)S(1)}, bf16[1728,128]{1,0:T(8,128)(2,1)S(1)}, u32[]{:S(2)}, u32[]{:S(2)}) collective-permute-start(bf16[1728,128]{1,0:T(8,128)(2,1)S(1)} %get-tuple-element.97), channel_id=1, source_target_pairs={{0,32},{16,48},{32,64},{48,80},{64,96},{80,112},{96,0},{112,16},{1... | collective-permute-start | bytes 1327112 | tf_op jit(solution)/shard_map/ppermute | solution.py:328
  117.0 7.8 %collective-permute-start.32 = (bf16[512,128]{1,0:T(8,128)(2,1)S(1)}, bf16[512,128]{1,0:T(8,128)(2,1)S(1)}, u32[]{:S(2)}, u32[]{:S(2)}) collective-permute-start(bf16[512,128]{1,0:T(8,128)(2,1)S(1)} %get-tuple-element.96.refs_0_.refs_3_), channel_id=1, source_target_pairs={{0,16},{16,0},{32,48},{48,32},{64,80},{80,64},{96,112},{112,96},{1... | collective-permute-start | bytes 393224 | tf_op jit(solution)/shard_map/ppermute | solution.py:332
  121.9 12.3 %collective-permute-start.26 = (bf16[1728,128]{1,0:T(8,128)(2,1)S(1)}, bf16[1728,128]{1,0:T(8,128)(2,1)S(1)}, u32[]{:S(2)}, u32[]{:S(2)}) collective-permute-start(bf16[1728,128]{1,0:T(8,128)(2,1)S(1)} %get-tuple-element.98), channel_id=1, source_target_pairs={{0,96},{16,112},{32,0},{48,16},{64,32},{80,48},{96,64},{112,80},{1... | collective-permute-start | bytes 1327112 | tf_op jit(solution)/shard_map/ppermute | solution.py:328
  126.1 10.2 %collective-permute-start.29 = (bf16[1408,128]{1,0:T(8,128)(2,1)S(1)}, bf16[1408,128]{1,0:T(8,128)(2,1)S(1)}, u32[]{:S(2)}, u32[]{:S(2)}) collective-permute-start(bf16[1408,128]{1,0:T(8,128)(2,1)S(1)} %get-tuple-element.94.refs_0_), channel_id=1, source_target_pairs={{0,16},{16,0},{32,48},{48,32},{64,80},{80,64},{96,112},{112,96},{1... | collective-permute-start | bytes 1081352 | tf_op jit(solution)/shard_map/ppermute | solution.py:332
  126.5 11.5 %collective-permute-start.31 = (bf16[1408,128]{1,0:T(8,128)(2,1)S(1)}, bf16[1408,128]{1,0:T(8,128)(2,1)S(1)}, u32[]{:S(2)}, u32[]{:S(2)}) collective-permute-start(bf16[1408,128]{1,0:T(8,128)(2,1)S(1)} %collective-permute-done.22.refs_3_.refs_2_), channel_id=1, source_target_pairs={{0,16},{16,0},{32,48},{48,32},{64,80},{80,64},{96,112},{112,96},{1... | collective-permute-start | bytes 1081352 | tf_op jit(solution)/shard_map/ppermute | solution.py:332
  134.3 6.4 %collective-permute-start.27 = (bf16[512,128]{1,0:T(8,128)(2,1)S(1)}, bf16[512,128]{1,0:T(8,128)(2,1)S(1)}, u32[]{:S(2)}, u32[]{:S(2)}) collective-permute-start(bf16[512,128]{1,0:T(8,128)(2,1)S(1)} %slice.8), channel_id=1, source_target_pairs={{0,32},{16,48},{32,64},{48,80},{64,96},{80,112},{96,0},{112,16},{1... | collective-permute-start | bytes 393224 | tf_op jit(solution)/shard_map/ppermute | solution.py:328
  138.0 7.2 %collective-permute-start.34 = (bf16[1728,128]{1,0:T(8,128)(2,1)S(1)}, bf16[1728,128]{1,0:T(8,128)(2,1)S(1)}, u32[]{:S(2)}, u32[]{:S(2)}) collective-permute-start(bf16[1728,128]{1,0:T(8,128)(2,1)S(1)} %collective-permute-done.25.refs_5_), channel_id=1, source_target_pairs={{0,16},{16,0},{32,48},{48,32},{64,80},{80,64},{96,112},{112,96},{1... | collective-permute-start | bytes 1327112 | tf_op jit(solution)/shard_map/ppermute | solution.py:332
  (20 other events, 113.6 us)

commit v6 on v5

--- a/solution.py
+++ b/solution.py
@@ -66,8 +66,10 @@
     return copies
 
 
-def front_kernel(place, tok, left, cot, right, own, s1, s2, s3, tokv, leftv, cotv, rightv, both, sems):
-    quarter, r = cotv.shape[1], rightv.shape[0]
+def front_kernel(
+    place, tok, left, cot, right, rank, low, back, s1, s2, s3, tokv, leftv, cotv, rightv, full, sems
+):
+    quarter = cotv.shape[1]
     here = pl.ds(pl.multiple_of(place.f * quarter, SIDE), quarter)
     c_tok, c_left, c_cot, c_right = fetch(
         (tok, tokv, sems.at[0]),
@@ -77,44 +79,31 @@
     )
     c_tok.wait()
     c_left.wait()
-    both[:, r:] = jnp.dot(tokv[...], leftv[...], preferred_element_type=F32)
+    rank[...] = jnp.dot(tokv[...], leftv[...], preferred_element_type=F32)
+    low[...] = rank[...].astype(BF16)
     c_cot.wait()
     c_right.wait()
-    both[:, :r] = lax.dot_general(cotv[...], rightv[...], COLS, preferred_element_type=F32)
-    rows = own.shape[0]
-    own[...] = both[span(place.f, rows), :]
+    full[...] = lax.dot_general(cotv[...], rightv[...], COLS, preferred_element_type=F32)
+    back[...] = full[:, lanes(place.t)]
     for k, out in ((1, s1), (2, s2), (3, s3)):
-        out[...] = both[span(lax.rem(place.f + k, place.n_f), rows), :].astype(BF16)
-
-
-def columns_kernel(place, own, g1, g2, g3, back, rank, s1, s2, s3, total):
-    r = place.n_t * SIDE
-    total[...] = own[...] + g1[...].astype(F32) + g2[...].astype(F32) + g3[...].astype(F32)
-    back[...] = total[:, lanes(place.t)]
-    low = total[:, r:].astype(BF16)
-    rank[...] = low
-    for k, out in ((1, s1), (2, s2), (3, s3)):
-        out[:, :SIDE] = total[:, lanes(lax.rem(place.t + k, place.n_t))].astype(BF16)
-        out[:, SIDE:] = low
-
-
-def rows_kernel(place, back, rank, g1, g2, g3, out):
-    total = back[...]
-    out[:, lanes(place.t + 1)] = rank[...]
-    for k, g in ((1, g1), (2, g2), (3, g3)):
-        total = total + g[:, :SIDE].astype(F32)
-        out[:, lanes(lax.rem(place.t - k + place.n_t, place.n_t) + 1)] = g[:, SIDE:]
-    out[:, :SIDE] = total.astype(BF16)
-
-
-def residual_kernel(place, q_blocks, steps, counts, rows, cols, tok, vals, *refs):
-    outs, (tokv, valv, acc, sems) = refs[:-4], refs[-4:]
-    n_out = len(outs) // len(steps)
+        out[...] = full[:, lanes(lax.rem(place.t + k, place.n_t))].astype(BF16)
+
+
+def total_kernel(own, g1, g2, g3, *outs):
+    total = own[...] + g1[...].astype(F32) + g2[...].astype(F32) + g3[...].astype(F32)
+    for out in outs:
+        out[...] = total.astype(out.dtype)
+
+
+def residual_kernel(
+    place, q_blocks, counts, rows, cols, tok, vals, ahead, behind, p1, p3, p0, tokv, valv, acc, sems
+):
     c_tok, c_val = fetch((tok, tokv, sems.at[0]), (vals, valv, sems.at[1]))
     live = place.live(counts)
+    half = ahead.shape[0]
     c_tok.wait()
     c_val.wait()
-    for step in steps:
+    for step in (2, 1, 3, 0):
         acc[...] = jnp.zeros_like(acc)
         first = lax.rem(place.f + step, place.n_f) * q_blocks
 
@@ -130,11 +119,11 @@
             return carry
 
         lax.fori_loop(0, live, body, 0)
-        row = 0
-        for out in outs[:n_out]:
-            out[...] = acc[row : row + out.shape[0]].astype(BF16)
-            row += out.shape[0]
-        outs = outs[n_out:]
+        if step == 2:
+            ahead[...] = acc[:half].astype(BF16)
+            behind[...] = acc[half:].astype(BF16)
+        else:
+            {1: p1, 3: p3, 0: p0}[step][...] = acc[...].astype(BF16)
 
 
 PANELS = 8
@@ -185,14 +174,12 @@
 
 
 def factors_kernel(
-    place, tok, cot, g0, g1, g2, g3, blocks_mine, blocks_theirs, mine, theirs0, theirs1, theirs2, theirs3,
-    tokv, cotv, both, left, right, sems,
+    place, tok, cot, g0, g1, g2, g3, b0, b1, b2, b3, blocks_mine, blocks_theirs,
+    mine, theirs0, theirs1, theirs2, theirs3, tokv, cotv, left, right, sems,
 ):
-    quarter, n_rows = cotv.shape[1], g0.shape[0]
+    quarter = cotv.shape[1]
     here = pl.ds(pl.multiple_of(place.f * quarter, SIDE), quarter)
     c_tok, c_cot = fetch((tok, tokv, sems.at[0]), (cot.at[:, here], cotv, sems.at[1]))
-    for k, g in enumerate((g0, g1, g2, g3)):
-        both[span(lax.rem(place.f - k + place.n_f, place.n_f), n_rows), :] = g[...]
     n_l = left.shape[0] // place.n_d
     n_r = right.shape[0] // place.n_d
     n_lr = n_l + quarter // SIDE * n_r
@@ -201,9 +188,14 @@
         mine[j, n_lr:] = blocks_mine[j]
         theirs[j][n_lr:] = blocks_theirs[j]
     c_tok.wait()
-    left[...] = lax.dot_general(both[:, :SIDE], tokv[...], ROWS, preferred_element_type=F32).T
+    back = b0[...] + b1[...].astype(F32) + b2[...].astype(F32) + b3[...].astype(F32)
+    left[...] = lax.dot_general(
+        back.astype(BF16), tokv[...], ROWS, preferred_element_type=F32
+    ).T
     c_cot.wait()
-    right[...] = lax.dot_general(both[:, SIDE:], cotv[...], ROWS, preferred_element_type=F32)
+    for k, g in enumerate((g0, g1, g2, g3)):
+        at = span(lax.rem(place.t - k + place.n_t, place.n_t), SIDE)
+        right[at, :] = lax.dot_general(g[...], cotv[...], ROWS, preferred_element_type=F32)
     for j in range(place.chips):
         chip = lax.rem(place.chip + j, place.chips)
         for core, out in ((place.core, mine.at[j]), (1 - place.core, theirs[j])):
@@ -268,11 +260,11 @@
 
 
 def low_kernel(place, g0, g1, g2, g3, right, p0, out):
-    n_rows = g0.shape[0]
+    acc = p0[...].astype(F32)
     for k, g in enumerate((g0, g1, g2, g3)):
-        at = span(lax.rem(place.f - k + place.n_f, place.n_f), n_rows)
-        prod = jnp.dot(g[:, SIDE:], right[...], preferred_element_type=F32)
-        out[at, :] = prod + p0[at, :].astype(F32)
+        at = span(lax.rem(place.t - k + place.n_t, place.n_t), SIDE)
+        acc += jnp.dot(g[...], right[at, :], preferred_element_type=F32)
+    out[...] = acc
 
 
 def finish_kernel(low, from_behind, from_ahead, out):
@@ -345,8 +337,6 @@
     right = right_factor.reshape(right_factor.shape[0], -1)
     rank_size, quarter = right.shape
     q_blocks = quarter // SIDE
-    n_rows = tok_rows // n_f
-    width = rank_size + SIDE
     half = tok_rows // 2
     lists = (block_counts, block_rows, block_cols)
     vm, dma = pltpu.VMEM, pltpu.SemaphoreType.DMA
@@ -357,55 +347,46 @@
     def over(n, k_shift):
         return [k_shift(k) for k in range(1, n)]
 
-    def residual(steps, outs, after, mib):
-        return call(
-            bind(residual_kernel, q_blocks, steps),
-            outs,
-            smem=lists,
-            hbm=(tokens, block_values),
-            scratch=[
-                vm((tok_rows, features), BF16),
-                vm((maxb, SIDE, SIDE), BF16),
-                vm((tok_rows, quarter), F32),
-                dma((2,)),
-            ],
-            after=after,
-            mib=mib,
-        )
-
-    part, whole = shape((half, quarter), BF16), shape((tok_rows, quarter), BF16)
-    ahead, behind, step = residual((2,), (part, part), (), 56)
-    from_behind = shift(ahead, "fsdp", n_f, 1)
-    from_ahead = shift(behind, "fsdp", n_f, -1)
-
-    message = shape((n_rows, width), BF16)
-    own, *out, step = call(
+    wide, narrow = shape((tok_rows, SIDE), F32), shape((tok_rows, SIDE), BF16)
+    rank, rank_low, back, *back_out, step = call(
         bind(front_kernel),
-        (shape((n_rows, width), F32),) + (message,) * 3,
+        (wide, narrow, wide, narrow, narrow, narrow),
         hbm=(tokens, left_factor, cotangent, right),
         scratch=[
             vm((tok_rows, features), BF16),
             vm((features, SIDE), BF16),
             vm((tok_rows, quarter), BF16),
             vm((rank_size, quarter), BF16),
-            vm((tok_rows, width), F32),
+            vm((tok_rows, rank_size), F32),
             dma((4,)),
         ],
+        mib=56,
+    )
+    rank_in = over(n_f, lambda k: shift(rank_low, "fsdp", n_f, k))
+    back_in = [shift(x, "tensor", n_t, k + 1) for k, x in enumerate(back_out)]
+
+    part, whole = shape((half, quarter), BF16), shape((tok_rows, quarter), BF16)
+    ahead, behind, p1, p3, p0, step = call(
+        bind(residual_kernel, q_blocks),
+        (part, part, whole, whole, whole),
+        smem=lists,
+        hbm=(tokens, block_values),
+        scratch=[
+            vm((tok_rows, features), BF16),
+            vm((maxb, SIDE, SIDE), BF16),
+            vm((tok_rows, quarter), F32),
+            dma((2,)),
+        ],
         after=(step,),
-        mib=52,
-    )
-    shares = [shift(x, "fsdp", n_f, k + 1) for k, x in enumerate(out)]
-    p1, p3, p0, step = residual((1, 3, 0), (whole,) * 3, (step,), 24)
-
-    back, rank, *out, step = call(
-        bind(columns_kernel),
-        (shape((n_rows, SIDE), F32), shape((n_rows, SIDE), BF16))
-        + (shape((n_rows, 2 * SIDE), BF16),) * 3,
-        vmem=(own, *shares),
-        scratch=[vm((n_rows, width), F32)],
-        after=(step,),
-    )
-    shares = [shift(x, "tensor", n_t, k + 1) for k, x in enumerate(out)]
+        mib=56,
+    )
+
+    rank, step = call(total_kernel, (narrow,), vmem=(rank, *rank_in), after=(step,))
+    ranks = [rank] + over(n_t, lambda k: shift(rank, "tensor", n_t, k))
+    back, back_low, step = call(
+        total_kernel, (wide, narrow), vmem=(back, *back_in), after=(step,)
+    )
+    backs = [back] + over(n_f, lambda k: shift(back_low, "fsdp", n_f, k))
 
     n_b = maxb // n_d * SIDE
     blocks_mine, blocks_theirs, step = call(
@@ -423,14 +404,15 @@
         mib=48,
     )
 
-    rows, step = call(bind(rows_kernel), (message,), vmem=(back, rank, *shares), after=(step,))
-    gathered = [rows] + over(n_f, lambda k: shift(rows, "fsdp", n_f, k))
-
-    ahead, behind, step = call(
-        pass_kernel, (whole, whole), vmem=(p1, p3, from_behind, from_ahead), after=(step,), mib=16
-    )
-    last_behind = shift(ahead, "fsdp", n_f, 1)
-    last_ahead = shift(behind, "fsdp", n_f, -1)
+    ahead, behind = pl.pallas_call(
+        lambda *refs: None,
+        out_shape=(part, part),
+        in_specs=[HBM] * 2 + [VMEM] * 6,
+        out_specs=(HBM,) * 2,
+        input_output_aliases={0: 0, 1: 1},
+    )(ahead, behind, *ranks[1:], *backs[1:])
+    from_behind = shift(ahead, "fsdp", n_f, 1)
+    from_ahead = shift(behind, "fsdp", n_f, -1)
 
     n_l = features // n_d
     n_r = rank_size // n_d
@@ -441,11 +423,10 @@
         bind(factors_kernel),
         (shape((chips, n_all, SIDE), F32),) + (chunk,) * chips,
         hbm=(tokens, cotangent),
-        vmem=(*gathered, blocks_mine, blocks_theirs),
+        vmem=(*ranks, *backs, blocks_mine, blocks_theirs),
         scratch=[
             vm((tok_rows, features), BF16),
             vm((tok_rows, quarter), BF16),
-            vm((tok_rows, width), BF16),
             vm((features, SIDE), F32),
             vm((rank_size, quarter), F32),
             dma((2,)),
@@ -465,7 +446,7 @@
     low, step = call(
         bind(low_kernel),
         (shape((tok_rows, quarter), F32),),
-        vmem=(*gathered, right, p0),
+        vmem=(*ranks, right, p0),
         after=(step,),
         mib=20,
     )
@@ -477,11 +458,17 @@
     )
     c_last_behind = chip_shift(c_ahead, n_d, 1)
     c_last_ahead = chip_shift(c_behind, n_d, -1)
+    ahead, behind, step = call(
+        pass_kernel, (whole, whole), vmem=(p1, p3, from_behind, from_ahead), after=(step,), mib=16
+    )
+    last_behind = shift(ahead, "fsdp", n_f, 1)
+    last_ahead = shift(behind, "fsdp", n_f, -1)
     left, rest, step = call(
         chunk_kernel,
         (shape((n_l, SIDE), BF16), shape((n_rest, SIDE), BF16)),
         vmem=(own, c_from_behind, c_from_ahead, c_last_behind, c_last_ahead),
         scratch=[vm((n_all, SIDE), F32)],
+        after=(step,),
     )
 
     rest_behind = chip_shift(rest, n_d, 1)

time: 149 us -> 154 us (1.034)
  Pallas kernels: 43 us -> 54.3 us
  waiting for transfers between devices: 47.1 us -> 40 us
  local copies, waits for them, and re-layouts: 0.05 us -> 2.37 us
  starting transfers between devices: 57.3 us -> 55.3 us
    ppermute x13 -> x16, waiting for transfers between devices: 25.6 us -> 7.13 us  [shift(): return lax.ppermute(x, axis, [(i, (i + k) % n) for i in range(n)])]
    pallas_call x16 -> x15, Pallas kernels: 43 us -> 53 us  [call(): pl.pallas_call(body, out_shape=(*outs, shape((1,), jnp.int32)), in_specs=...]
    ppermute x13, waiting for transfers between devices: 1.03 us -> 7.97 us  [core_swap(): return lax.ppermute(x, 'dp', [(i, i ^ 1) for i in range(n_data)])]
    ppermute x10, waiting for transfers between devices: 14.4 us -> 17.4 us  [chip_shift(): return lax.ppermute(x, 'dp', perm)]
    ppermute x1, starting transfers between devices: 4.23 us -> 1.29 us  [per_device(): lax.ppermute(left_pair, 'tensor', [(i, n_t - 1 - i) for i in range(n_t)])]
    unnamed x12 -> x50, local copies, waits for them, and re-layouts: 0.03 us -> 2.35 us
    ppermute x13 -> x16, starting transfers between devices: 21.4 us -> 23.2 us  [shift(): return lax.ppermute(x, axis, [(i, (i + k) % n) for i in range(n)])]
  transfers between devices with their start and end apart: 38 -> 41, of which waited for: 12 -> 15; matrix products, arithmetic and copies ran while one was open for 0% -> 0% of each run, Pallas kernels for 20% -> 26%
where the time goes in v6:
time: 154 us; the launch traced here: 153 us
  starting transfers between devices  55.3 us (36%)
  Pallas kernels  54.3 us (35%)
  waiting for transfers between devices  40 us (26%)
  local copies, waits for them, and re-layouts  2.37 us (2%)
    pallas_call x15, Pallas kernels, call(): pl.pallas_call(body, out_shape=(*outs, shape((1,), jnp.int32)), in_specs=...  53 us
    ppermute x16, starting transfers between devices, shift(): return lax.ppermute(x, axis, [(i, (i + k) % n) for i in range(n)])  23.2 us
    ppermute x10, waiting for transfers between devices, chip_shift(): return lax.ppermute(x, 'dp', perm)  17.4 us
    ppermute x13, starting transfers between devices, core_swap(): return lax.ppermute(x, 'dp', [(i, i ^ 1) for i in range(n_data)])  16.4 us
    ppermute x10, starting transfers between devices, chip_shift(): return lax.ppermute(x, 'dp', perm)  14.5 us
    ppermute x13, waiting for transfers between devices, core_swap(): return lax.ppermute(x, 'dp', [(i, i ^ 1) for i in range(n_data)])  7.97 us
    ppermute x16, waiting for transfers between devices, shift(): return lax.ppermute(x, axis, [(i, (i + k) % n) for i in range(n)])  7.13 us
    ppermute x1, waiting for transfers between devices, per_device(): lax.ppermute(left_pair, 'tensor', [(i, n_t - 1 - i) for i in range(n_t)])  4.11 us
  transfers between devices with their start and end apart: 41, of which 15 were waited for; matrix products, arithmetic and copies ran while one was open for 0% of the time, Pallas kernels for 26%

profile of v6, /device:TPU:1, one launch (start us, length us, event | category | flops | bytes accessed | tf_op | source)
XLA Modules:
  0.0 153.3 jit_solution(16610777683251528173)
XLA Ops:
  0.6 6.5 %shard_map.111 = (f32[640,128]{1,0:T(8,128)}, bf16[640,128]{1,0:T(8,128)(2,1)}, f32[640,128]{1,0:T(8,128)}, bf16[640,128]{1,0:T(8,128)(2,1)}, bf16[640,128]{1,0:...) custom-call(bf16[640,2048]{1,0:T(8,128)(2,1)} %refs_0_.7, bf16[2048,512]{1,0:T(8,128)(2,1)} %refs_1_.4, ...), custom_call_target="tpu_custom_call" | custom-call | tf_op jit(solution)/shard_map/pallas_call | solution.py:38
  9.4 2.6 %collective-permute-start.1 = (bf16[640,128]{1,0:T(8,128)(2,1)}, bf16[640,128]{1,0:T(8,128)(2,1)S(1)}, u32[]{:S(2)}, u32[]{:S(2)}) collective-permute-start(bf16[640,128]{1,0:T(8,128)(2,1)} %get-tuple-element.55), channel_id=1, source_target_pairs={{0,8},{4,12},{8,0},{12,4},{1,9},{5,13},{9,1},{13,5},{2,10},{6,14},... | collective-permute-start | bytes 491528 | tf_op jit(solution)/shard_map/ppermute | solution.py:314
  14.7 3.3 %collective-permute-start.7 = (bf16[640,128]{1,0:T(8,128)(2,1)}, bf16[640,128]{1,0:T(8,128)(2,1)S(1)}, u32[]{:S(2)}, u32[]{:S(2)}) collective-permute-start(bf16[640,128]{1,0:T(8,128)(2,1)} %get-tuple-element.62), channel_id=1, source_target_pairs={{0,2},{1,3},{2,0},{3,1},{4,6},{5,7},{6,4},{7,5},{8,10},{9,11},{10,... | collective-permute-start | bytes 491528 | tf_op jit(solution)/shard_map/ppermute | solution.py:314
  18.1 14.6 %shard_map.112 = (bf16[320,1792]{1,0:T(8,128)(2,1)}, bf16[320,1792]{1,0:T(8,128)(2,1)}, bf16[640,1792]{1,0:T(8,128)(2,1)}, bf16[640,1792]{1,0:T(8,128)(2,1)}, bf16[640,1792]{1,0:T(8,128)(2,1)}, /*index=5*/s32[1]{0:T(128)}) custom-call(s32[16]{0:T(128)} %refs_0_.6, s32[32]{0:T(128)} %refs_1_.6, s32[32]{0:T(128)} %refs_2_.5, bf16[640,2048]{1,0:T(8,128)(2,1)} %refs_0_.7, ...), custom_call_target="tpu_custom_call" | custom-call | tf_op jit(solution)/shard_map/pallas_call | solution.py:38
  35.5 2.5 %collective-permute-start.5 = (bf16[640,128]{1,0:T(8,128)(2,1)S(1)}, bf16[640,128]{1,0:T(8,128)(2,1)S(1)}, u32[]{:S(2)}, u32[]{:S(2)}) collective-permute-start(bf16[640,128]{1,0:T(8,128)(2,1)S(1)} %get-tuple-element.58.refs_2_.refs_0_), channel_id=1, source_target_pairs={{0,3},{1,0},{2,1},{3,2},{4,7},{5,4},{6,5},{7,6},{8,11},{9,8},{10,9... | collective-permute-start | bytes 491528 | tf_op jit(solution)/shard_map/ppermute | solution.py:314
  39.8 2.3 %collective-permute-start.11 = (bf16[640,128]{1,0:T(8,128)(2,1)S(1)}, bf16[640,128]{1,0:T(8,128)(2,1)S(1)}, u32[]{:S(2)}, u32[]{:S(2)}) collective-permute-start(bf16[640,128]{1,0:T(8,128)(2,1)S(1)} %get-tuple-element.66), channel_id=1, source_target_pairs={{0,12},{4,0},{8,4},{12,8},{1,13},{5,1},{9,5},{13,9},{2,14},{6,2},{... | collective-permute-start | bytes 491528 | tf_op jit(solution)/shard_map/ppermute | solution.py:314
  42.1 9.5 %shard_map.115 = (f32[4,512,128]{2,1,0:T(8,128)S(1)}, bf16[4,512,128]{2,1,0:T(8,128)(2,1)S(1)}, s32[1]{0:T(128)}) custom-call(s32[16]{0:T(128)S(1)} %copy-done.18, s32[32]{0:T(128)S(1)} %copy-done.19, s32[32]{0:T(128)S(1)} %copy-done.20, bf16[640,2048]{1,0:T(8,128)(2,1)S(1)} %copy-done, bf16[640,7168]{1,0:T(8,128)(2,1)} %refs_1_.7, s32[1]{0:T(128)} %get-tuple-element.67.refs_5_), custom_call_target="tpu_custom_call" | custom-call | tf_op jit(solution)/shard_map/pallas_call | solution.py:38
  51.6 5.1 %shard_map.116 = (f32[4,1664,128]{2,1,0:T(8,128)S(1)}, bf16[1664,128]{1,0:T(8,128)(2,1)}, bf16[1664,128]{1,0:T(8,128)(2,1)S(1)}, bf16[1664,128]{1,0:T(8,128)(2,1...) custom-call(bf16[640,2048]{1,0:T(8,128)(2,1)S(1)} %copy-done, bf16[640,7168]{1,0:T(8,128)(2,1)} %refs_1_.7, ...), custom_call_target="tpu_custom_call" | custom-call | tf_op jit(solution)/shard_map/pallas_call | solution.py:38
  59.0 3.9 %collective-permute-start.12 = (bf16[1664,128]{1,0:T(8,128)(2,1)}, bf16[1664,128]{1,0:T(8,128)(2,1)}, u32[]{:S(2)}, u32[]{:S(2)}) collective-permute-start(bf16[1664,128]{1,0:T(8,128)(2,1)} %get-tuple-element.72), channel_id=1, source_target_pairs={{0,16},{16,0},{32,48},{48,32},{64,80},{80,64},{96,112},{112,96},{1... | collective-permute-start | bytes 1277960 | tf_op jit(solution)/shard_map/ppermute | solution.py:324
  64.3 2.7 %collective-permute-start.17 = (bf16[320,1792]{1,0:T(8,128)(2,1)}, bf16[320,1792]{1,0:T(8,128)(2,1)S(1)}, u32[]{:S(2)}, u32[]{:S(2)}) collective-permute-start(bf16[320,1792]{1,0:T(8,128)(2,1)} %get-tuple-element.83), channel_id=1, source_target_pairs={{0,12},{4,0},{8,4},{12,8},{1,13},{5,1},{9,5},{13,9},{2,14},{6,2},{... | collective-permute-start | bytes 3440648 | tf_op jit(solution)/shard_map/ppermute | solution.py:314
  74.9 3.4 %shard_map.118 = (f32[640,1792]{1,0:T(8,128)S(1)}, s32[1]{0:T(128)}) custom-call(bf16[640,128]{1,0:T(8,128)(2,1)S(1)} %copy-done.12, bf16[640,128]{1,0:T(8,128)(2,1)S(1)} %copy-done.6, bf16[640,128]{1,0:T(8,128)(2,1)S(1)} %copy-done.8, bf16[640,128]{1,0:T(8,128)(2,1)S(1)} %copy-done.10, bf16[512,1792]{1,0:T(8,128)(2,1)S(1)} %bitcast.5, ...), custom_call_target="tpu_custom_call" | custom-call | tf_op jit(solution)/shard_map/pallas_call | solution.py:38
  78.2 6.1 %collective-permute-done.18.refs_1_ = bf16[1664,128]{1,0:T(8,128)(2,1)S(1)} collective-permute-done((bf16[1664,128]{1,0:T(8,128)(2,1)S(1)}, bf16[1664,128]{1,0:T(8,128)(2,1)S(1)}, u32[]{:S(2)}, u32[]{:S(2)}) %collective-permute-start.18) | collective-permute-done | bytes 426016 | tf_op jit(solution)/shard_map/ppermute | solution.py:320
  85.5 7.1 %collective-permute-done.16.refs_2_ = bf16[320,1792]{1,0:T(8,128)(2,1)S(1)} collective-permute-done((bf16[320,1792]{1,0:T(8,128)(2,1)}, bf16[320,1792]{1,0:T(8,128)(2,1)S(1)}, u32[]{:S(2)}, u32[]{:S(2)}) %collective-permute-start.16) | collective-permute-done | bytes 1146912 | tf_op jit(solution)/shard_map/ppermute | solution.py:314
  94.0 2.7 %collective-permute-start.21 = (bf16[640,1792]{1,0:T(8,128)(2,1)S(1)}, bf16[640,1792]{1,0:T(8,128)(2,1)S(1)}, u32[]{:S(2)}, u32[]{:S(2)}) collective-permute-start(bf16[640,1792]{1,0:T(8,128)(2,1)S(1)} %get-tuple-element.90), channel_id=1, source_target_pairs={{0,12},{4,0},{8,4},{12,8},{1,13},{5,1},{9,5},{13,9},{2,14},{6,2},{... | collective-permute-start | bytes 6881288 | tf_op jit(solution)/shard_map/ppermute | solution.py:314
  99.3 3.9 %collective-permute-done.22.refs_3_ = bf16[832,128]{1,0:T(8,128)(2,1)S(1)} collective-permute-done((bf16[832,128]{1,0:T(8,128)(2,1)S(1)}, bf16[832,128]{1,0:T(8,128)(2,1)S(1)}, u32[]{:S(2)}, u32[]{:S(2)}) %collective-permute-start.22) | collective-permute-done | bytes 213024 | tf_op jit(solution)/shard_map/ppermute | solution.py:320
  107.3 3.4 %collective-permute-done.26.refs_1_ = bf16[256,128]{1,0:T(8,128)(2,1)S(1)} collective-permute-done((bf16[256,128]{1,0:T(8,128)(2,1)S(1)}, bf16[256,128]{1,0:T(8,128)(2,1)S(1)}, u32[]{:S(2)}, u32[]{:S(2)}) %collective-permute-start.26) | collective-permute-done | bytes 65568 | tf_op jit(solution)/shard_map/ppermute | solution.py:476
  112.5 4.1 %collective-permute-done.27.refs_1_.refs_4_ = bf16[512,128]{1,0:T(8,128)(2,1)S(1)} collective-permute-done((bf16[512,128]{1,0:T(8,128)(2,1)S(1)}, bf16[512,128]{1,0:T(8,128)(2,1)S(1)}, u32[]{:S(2)}, u32[]{:S(2)}) %collective-permute-start.27) | collective-permute-done | bytes 131104 | tf_op jit(solution)/shard_map/ppermute | solution.py:480
  117.3 4.8 %collective-permute-start.32 = (bf16[1408,128]{1,0:T(8,128)(2,1)S(1)}, bf16[1408,128]{1,0:T(8,128)(2,1)S(1)}, u32[]{:S(2)}, u32[]{:S(2)}) collective-permute-start(bf16[1408,128]{1,0:T(8,128)(2,1)S(1)} %get-tuple-element.96.refs_0_), channel_id=1, source_target_pairs={{0,16},{16,0},{32,48},{48,32},{64,80},{80,64},{96,112},{112,96},{1... | collective-permute-start | bytes 1081352 | tf_op jit(solution)/shard_map/ppermute | solution.py:324
  125.3 2.7 %collective-permute-start.29 = (bf16[1728,128]{1,0:T(8,128)(2,1)S(1)}, bf16[1728,128]{1,0:T(8,128)(2,1)S(1)}, u32[]{:S(2)}, u32[]{:S(2)}) collective-permute-start(bf16[1728,128]{1,0:T(8,128)(2,1)S(1)} %get-tuple-element.100), channel_id=1, source_target_pairs={{0,96},{16,112},{32,0},{48,16},{64,32},{80,48},{96,64},{112,80},{1... | collective-permute-start | bytes 1327112 | tf_op jit(solution)/shard_map/ppermute | solution.py:320
  128.0 3.3 %collective-permute-start.34 = (bf16[1408,128]{1,0:T(8,128)(2,1)S(1)}, bf16[1408,128]{1,0:T(8,128)(2,1)S(1)}, u32[]{:S(2)}, u32[]{:S(2)}) collective-permute-start(bf16[1408,128]{1,0:T(8,128)(2,1)S(1)} %collective-permute-done.25.refs_3_.refs_2_), channel_id=1, source_target_pairs={{0,16},{16,0},{32,48},{48,32},{64,80},{80,64},{96,112},{112,96},{1... | collective-permute-start | bytes 1081352 | tf_op jit(solution)/shard_map/ppermute | solution.py:324
  133.0 4.4 %collective-permute-done.29.refs_6_ = bf16[1728,128]{1,0:T(8,128)(2,1)S(1)} collective-permute-done((bf16[1728,128]{1,0:T(8,128)(2,1)S(1)}, bf16[1728,128]{1,0:T(8,128)(2,1)S(1)}, u32[]{:S(2)}, u32[]{:S(2)}) %collective-permute-start.29) | collective-permute-done | bytes 442400 | tf_op jit(solution)/shard_map/ppermute | solution.py:320
  138.4 3.5 %collective-permute-start.31 = (bf16[512,128]{1,0:T(8,128)(2,1)S(1)}, bf16[512,128]{1,0:T(8,128)(2,1)S(1)}, u32[]{:S(2)}, u32[]{:S(2)}) collective-permute-start(bf16[512,128]{1,0:T(8,128)(2,1)S(1)} %slice.9), channel_id=1, source_target_pairs={{0,96},{16,112},{32,0},{48,16},{64,32},{80,48},{96,64},{112,80},{1... | collective-permute-start | bytes 393224 | tf_op jit(solution)/shard_map/ppermute | solution.py:320
  141.9 2.9 %collective-permute-done.31.refs_8_ = bf16[512,128]{1,0:T(8,128)(2,1)S(1)} collective-permute-done((bf16[512,128]{1,0:T(8,128)(2,1)S(1)}, bf16[512,128]{1,0:T(8,128)(2,1)S(1)}, u32[]{:S(2)}, u32[]{:S(2)}) %collective-permute-start.31) | collective-permute-done | bytes 131104 | tf_op jit(solution)/shard_map/ppermute | solution.py:320
  147.9 3.1 %shard_map.126 = (bf16[2048,512]{1,0:T(8,128)(2,1)}, bf16[512,1792]{1,0:T(8,128)(2,1)}, bf16[4096,128]{1,0:T(8,128)(2,1)}, s32[1]{0:T(128)}) custom-call(bf16[1408,128]{1,0:T(8,128)(2,1)S(1)} %get-tuple-element.96.refs_0_, bf16[1408,128]{1,0:T(8,128)(2,1)S(1)} %collective-permute-done.24.refs_2_.refs_1_, ...), custom_call_target="tpu_custom_call" | custom-call | tf_op jit(solution)/shard_map/pallas_call | solution.py:38
  (126 shorter events, 43.6 us)
Async XLA Ops:
  7.2 25.5 %collective-permute-start = (bf16[640,128]{1,0:T(8,128)(2,1)}, bf16[640,128]{1,0:T(8,128)(2,1)S(1)}, u32[]{:S(2)}, u32[]{:S(2)}) collective-permute-start(bf16[640,128]{1,0:T(8,128)(2,1)} %get-tuple-element.55), channel_id=1, source_target_pairs={{0,4},{4,8},{8,12},{12,0},{1,5},{5,9},{9,13},{13,1},{2,6},{6,10},{... | collective-permute-start | bytes 491528 | tf_op jit(solution)/shard_map/ppermute | solution.py:314
  9.4 23.4 %collective-permute-start.1 = (bf16[640,128]{1,0:T(8,128)(2,1)}, bf16[640,128]{1,0:T(8,128)(2,1)S(1)}, u32[]{:S(2)}, u32[]{:S(2)}) collective-permute-start(bf16[640,128]{1,0:T(8,128)(2,1)} %get-tuple-element.55), channel_id=1, source_target_pairs={{0,8},{4,12},{8,0},{12,4},{1,9},{5,13},{9,1},{13,5},{2,10},{6,14},... | collective-permute-start | bytes 491528 | tf_op jit(solution)/shard_map/ppermute | solution.py:314
  12.0 20.8 %collective-permute-start.2 = (bf16[640,128]{1,0:T(8,128)(2,1)}, bf16[640,128]{1,0:T(8,128)(2,1)S(1)}, u32[]{:S(2)}, u32[]{:S(2)}) collective-permute-start(bf16[640,128]{1,0:T(8,128)(2,1)} %get-tuple-element.55), channel_id=1, source_target_pairs={{0,12},{4,0},{8,4},{12,8},{1,13},{5,1},{9,5},{13,9},{2,14},{6,2},{... | collective-permute-start | bytes 491528 | tf_op jit(solution)/shard_map/ppermute | solution.py:314
  13.1 22.4 %collective-permute-start.6 = (bf16[640,128]{1,0:T(8,128)(2,1)}, bf16[640,128]{1,0:T(8,128)(2,1)S(1)}, u32[]{:S(2)}, u32[]{:S(2)}) collective-permute-start(bf16[640,128]{1,0:T(8,128)(2,1)} %get-tuple-element.61), channel_id=1, source_target_pairs={{0,1},{1,2},{2,3},{3,0},{4,5},{5,6},{6,7},{7,4},{8,9},{9,10},{10,1... | collective-permute-start | bytes 491528 | tf_op jit(solution)/shard_map/ppermute | solution.py:314
  14.7 23.3 %collective-permute-start.7 = (bf16[640,128]{1,0:T(8,128)(2,1)}, bf16[640,128]{1,0:T(8,128)(2,1)S(1)}, u32[]{:S(2)}, u32[]{:S(2)}) collective-permute-start(bf16[640,128]{1,0:T(8,128)(2,1)} %get-tuple-element.62), channel_id=1, source_target_pairs={{0,2},{1,3},{2,0},{3,1},{4,6},{5,7},{6,4},{7,5},{8,10},{9,11},{10,... | collective-permute-start | bytes 491528 | tf_op jit(solution)/shard_map/ppermute | solution.py:314
  35.5 16.0 %collective-permute-start.4 = (bf16[640,128]{1,0:T(8,128)(2,1)S(1)}, bf16[640,128]{1,0:T(8,128)(2,1)S(1)}, u32[]{:S(2)}, u32[]{:S(2)}) collective-permute-start(bf16[640,128]{1,0:T(8,128)(2,1)S(1)} %get-tuple-element.58.refs_2_.refs_0_), channel_id=1, source_target_pairs={{0,2},{1,3},{2,0},{3,1},{4,6},{5,7},{6,4},{7,5},{8,10},{9,11},{10,... | collective-permute-start | bytes 491528 | tf_op jit(solution)/shard_map/ppermute | solution.py:314
  35.5 16.0 %collective-permute-start.5 = (bf16[640,128]{1,0:T(8,128)(2,1)S(1)}, bf16[640,128]{1,0:T(8,128)(2,1)S(1)}, u32[]{:S(2)}, u32[]{:S(2)}) collective-permute-start(bf16[640,128]{1,0:T(8,128)(2,1)S(1)} %get-tuple-element.58.refs_2_.refs_0_), channel_id=1, source_target_pairs={{0,3},{1,0},{2,1},{3,2},{4,7},{5,4},{6,5},{7,6},{8,11},{9,8},{10,9... | collective-permute-start | bytes 491528 | tf_op jit(solution)/shard_map/ppermute | solution.py:314
  39.2 12.3 %collective-permute-start.9 = (bf16[640,128]{1,0:T(8,128)(2,1)S(1)}, bf16[640,128]{1,0:T(8,128)(2,1)S(1)}, u32[]{:S(2)}, u32[]{:S(2)}) collective-permute-start(bf16[640,128]{1,0:T(8,128)(2,1)S(1)} %get-tuple-element.66), channel_id=1, source_target_pairs={{0,4},{4,8},{8,12},{12,0},{1,5},{5,9},{9,13},{13,1},{2,6},{6,10},{... | collective-permute-start | bytes 491528 | tf_op jit(solution)/shard_map/ppermute | solution.py:314
  39.3 12.3 %collective-permute-start.10 = (bf16[640,128]{1,0:T(8,128)(2,1)S(1)}, bf16[640,128]{1,0:T(8,128)(2,1)S(1)}, u32[]{:S(2)}, u32[]{:S(2)}) collective-permute-start(bf16[640,128]{1,0:T(8,128)(2,1)S(1)} %get-tuple-element.66), channel_id=1, source_target_pairs={{0,8},{4,12},{8,0},{12,4},{1,9},{5,13},{9,1},{13,5},{2,10},{6,14},... | collective-permute-start | bytes 491528 | tf_op jit(solution)/shard_map/ppermute | solution.py:314
  39.8 11.8 %collective-permute-start.11 = (bf16[640,128]{1,0:T(8,128)(2,1)S(1)}, bf16[640,128]{1,0:T(8,128)(2,1)S(1)}, u32[]{:S(2)}, u32[]{:S(2)}) collective-permute-start(bf16[640,128]{1,0:T(8,128)(2,1)S(1)} %get-tuple-element.66), channel_id=1, source_target_pairs={{0,12},{4,0},{8,4},{12,8},{1,13},{5,1},{9,5},{13,9},{2,14},{6,2},{... | collective-permute-start | bytes 491528 | tf_op jit(solution)/shard_map/ppermute | solution.py:314
  59.0 8.5 %collective-permute-start.12 = (bf16[1664,128]{1,0:T(8,128)(2,1)}, bf16[1664,128]{1,0:T(8,128)(2,1)}, u32[]{:S(2)}, u32[]{:S(2)}) collective-permute-start(bf16[1664,128]{1,0:T(8,128)(2,1)} %get-tuple-element.72), channel_id=1, source_target_pairs={{0,16},{16,0},{32,48},{48,32},{64,80},{80,64},{96,112},{112,96},{1... | collective-permute-start | bytes 1277960 | tf_op jit(solution)/shard_map/ppermute | solution.py:324
  64.3 28.3 %collective-permute-start.16 = (bf16[320,1792]{1,0:T(8,128)(2,1)}, bf16[320,1792]{1,0:T(8,128)(2,1)S(1)}, u32[]{:S(2)}, u32[]{:S(2)}) collective-permute-start(bf16[320,1792]{1,0:T(8,128)(2,1)} %get-tuple-element.82), channel_id=1, source_target_pairs={{0,4},{4,8},{8,12},{12,0},{1,5},{5,9},{9,13},{13,1},{2,6},{6,10},{... | collective-permute-start | bytes 3440648 | tf_op jit(solution)/shard_map/ppermute | solution.py:314
  64.3 28.3 %collective-permute-start.17 = (bf16[320,1792]{1,0:T(8,128)(2,1)}, bf16[320,1792]{1,0:T(8,128)(2,1)S(1)}, u32[]{:S(2)}, u32[]{:S(2)}) collective-permute-start(bf16[320,1792]{1,0:T(8,128)(2,1)} %get-tuple-element.83), channel_id=1, source_target_pairs={{0,12},{4,0},{8,4},{12,8},{1,13},{5,1},{9,5},{13,9},{2,14},{6,2},{... | collective-permute-start | bytes 3440648 | tf_op jit(solution)/shard_map/ppermute | solution.py:314
  72.1 12.3 %collective-permute-start.18 = (bf16[1664,128]{1,0:T(8,128)(2,1)S(1)}, bf16[1664,128]{1,0:T(8,128)(2,1)S(1)}, u32[]{:S(2)}, u32[]{:S(2)}) collective-permute-start(bf16[1664,128]{1,0:T(8,128)(2,1)S(1)} %get-tuple-element.85), channel_id=1, source_target_pairs={{0,32},{16,48},{32,64},{48,80},{64,96},{80,112},{96,0},{112,16},{1... | collective-permute-start | bytes 1277960 | tf_op jit(solution)/shard_map/ppermute | solution.py:320
  73.3 11.0 %collective-permute-start.19 = (bf16[1664,128]{1,0:T(8,128)(2,1)S(1)}, bf16[1664,128]{1,0:T(8,128)(2,1)S(1)}, u32[]{:S(2)}, u32[]{:S(2)}) collective-permute-start(bf16[1664,128]{1,0:T(8,128)(2,1)S(1)} %get-tuple-element.86), channel_id=1, source_target_pairs={{0,96},{16,112},{32,0},{48,16},{64,32},{80,48},{96,64},{112,80},{1... | collective-permute-start | bytes 1277960 | tf_op jit(solution)/shard_map/ppermute | solution.py:320
  93.9 57.1 %collective-permute-start.20 = (bf16[640,1792]{1,0:T(8,128)(2,1)S(1)}, bf16[640,1792]{1,0:T(8,128)(2,1)S(1)}, u32[]{:S(2)}, u32[]{:S(2)}) collective-permute-start(bf16[640,1792]{1,0:T(8,128)(2,1)S(1)} %get-tuple-element.89), channel_id=1, source_target_pairs={{0,4},{4,8},{8,12},{12,0},{1,5},{5,9},{9,13},{13,1},{2,6},{6,10},{... | collective-permute-start | bytes 6881288 | tf_op jit(solution)/shard_map/ppermute | solution.py:314
  94.0 57.0 %collective-permute-start.21 = (bf16[640,1792]{1,0:T(8,128)(2,1)S(1)}, bf16[640,1792]{1,0:T(8,128)(2,1)S(1)}, u32[]{:S(2)}, u32[]{:S(2)}) collective-permute-start(bf16[640,1792]{1,0:T(8,128)(2,1)S(1)} %get-tuple-element.90), channel_id=1, source_target_pairs={{0,12},{4,0},{8,4},{12,8},{1,13},{5,1},{9,5},{13,9},{2,14},{6,2},{... | collective-permute-start | bytes 6881288 | tf_op jit(solution)/shard_map/ppermute | solution.py:314
  104.5 12.1 %collective-permute-start.24 = (bf16[1408,128]{1,0:T(8,128)(2,1)S(1)}, bf16[1408,128]{1,0:T(8,128)(2,1)S(1)}, u32[]{:S(2)}, u32[]{:S(2)}) collective-permute-start(bf16[1408,128]{1,0:T(8,128)(2,1)S(1)} %get-tuple-element.96.refs_0_), channel_id=1, source_target_pairs={{0,32},{16,48},{32,64},{48,80},{64,96},{80,112},{96,0},{112,16},{1... | collective-permute-start | bytes 1081352 | tf_op jit(solution)/shard_map/ppermute | solution.py:320
  105.5 11.1 %collective-permute-start.25 = (bf16[1408,128]{1,0:T(8,128)(2,1)S(1)}, bf16[1408,128]{1,0:T(8,128)(2,1)S(1)}, u32[]{:S(2)}, u32[]{:S(2)}) collective-permute-start(bf16[1408,128]{1,0:T(8,128)(2,1)S(1)} %get-tuple-element.96.refs_0_), channel_id=1, source_target_pairs={{0,96},{16,112},{32,0},{48,16},{64,32},{80,48},{96,64},{112,80},{1... | collective-permute-start | bytes 1081352 | tf_op jit(solution)/shard_map/ppermute | solution.py:320
  117.2 10.8 %collective-permute-start.28 = (bf16[1728,128]{1,0:T(8,128)(2,1)S(1)}, bf16[1728,128]{1,0:T(8,128)(2,1)S(1)}, u32[]{:S(2)}, u32[]{:S(2)}) collective-permute-start(bf16[1728,128]{1,0:T(8,128)(2,1)S(1)} %get-tuple-element.99), channel_id=1, source_target_pairs={{0,32},{16,48},{32,64},{48,80},{64,96},{80,112},{96,0},{112,16},{1... | collective-permute-start | bytes 1327112 | tf_op jit(solution)/shard_map/ppermute | solution.py:320
  117.3 8.0 %collective-permute-start.32 = (bf16[1408,128]{1,0:T(8,128)(2,1)S(1)}, bf16[1408,128]{1,0:T(8,128)(2,1)S(1)}, u32[]{:S(2)}, u32[]{:S(2)}) collective-permute-start(bf16[1408,128]{1,0:T(8,128)(2,1)S(1)} %get-tuple-element.96.refs_0_), channel_id=1, source_target_pairs={{0,16},{16,0},{32,48},{48,32},{64,80},{80,64},{96,112},{112,96},{1... | collective-permute-start | bytes 1081352 | tf_op jit(solution)/shard_map/ppermute | solution.py:324
  125.3 12.1 %collective-permute-start.29 = (bf16[1728,128]{1,0:T(8,128)(2,1)S(1)}, bf16[1728,128]{1,0:T(8,128)(2,1)S(1)}, u32[]{:S(2)}, u32[]{:S(2)}) collective-permute-start(bf16[1728,128]{1,0:T(8,128)(2,1)S(1)} %get-tuple-element.100), channel_id=1, source_target_pairs={{0,96},{16,112},{32,0},{48,16},{64,32},{80,48},{96,64},{112,80},{1... | collective-permute-start | bytes 1327112 | tf_op jit(solution)/shard_map/ppermute | solution.py:320
  132.6 15.3 %collective-permute-start.37 = (bf16[1728,128]{1,0:T(8,128)(2,1)S(1)}, bf16[1728,128]{1,0:T(8,128)(2,1)S(1)}, u32[]{:S(2)}, u32[]{:S(2)}) collective-permute-start(bf16[1728,128]{1,0:T(8,128)(2,1)S(1)} %collective-permute-done.28.refs_5_), channel_id=1, source_target_pairs={{0,16},{16,0},{32,48},{48,32},{64,80},{80,64},{96,112},{112,96},{1... | collective-permute-start | bytes 1327112 | tf_op jit(solution)/shard_map/ppermute | solution.py:324
  137.4 10.5 %collective-permute-start.38 = (bf16[1728,128]{1,0:T(8,128)(2,1)S(1)}, bf16[1728,128]{1,0:T(8,128)(2,1)S(1)}, u32[]{:S(2)}, u32[]{:S(2)}) collective-permute-start(bf16[1728,128]{1,0:T(8,128)(2,1)S(1)} %collective-permute-done.29.refs_6_), channel_id=1, source_target_pairs={{0,16},{16,0},{32,48},{48,32},{64,80},{80,64},{96,112},{112,96},{1... | collective-permute-start | bytes 1327112 | tf_op jit(solution)/shard_map/ppermute | solution.py:324
  (42 other events, 367.4 us)
